TPU v7x, 512 devices: a whole 4x8x8 slice. The times are simulated.
512 devices in a mesh: chan: 32 (over y, x), row: 2 (over core), col: 8 (over z).
Axes of the slice: x: 4, y: 8, z: 8, core: 2. Of those that a mesh axis runs over, the one named last changes fastest.
Arguments:
- voltages: bfloat16 [2, 2048, 16384], P(None, 'chan', ('row', 'col')), may hold values from -6 to 6
- fir_taps: float32 [4, 64], replicated, may hold values from -3 to 3
Outputs:
- visibilities: bfloat16 [2, 64, 2048, 2048], P(None, 'chan', 'row', 'col')
All inputs are finite; a program needn't handle non-finite values.
Results may differ from a plain program's by a relative error of at most 0.0057.
Values may be sent and summed in bfloat16 or wider, within the bound.
No kernel may reach another device: no remote copies, remote signals or barrier semaphores. Data moves between devices by JAX's collectives and lax.ppermute only.
A program may use at most 64 MiB of HBM per device.

v0:
```python
import math

import jax
import jax.numpy as jnp
from jax import lax
from jax.sharding import PartitionSpec as P


def from_behind(array, axis, by):
    length = lax.axis_size(axis)
    pairs = [(i, i + by) for i in range(length) if 0 <= i + by < length]
    return lax.ppermute(array, axis, pairs)


def dft_tables(count):
    index = jnp.arange(count, dtype=jnp.int32)
    phase = index[:, None] * index[None, :] % count
    angle = phase.astype(jnp.float32) * (2.0 * math.pi / count)
    cosine = jnp.cos(angle)
    sine_table = jnp.sin(angle)
    top = jnp.concatenate([cosine, -sine_table], 1)
    bottom = jnp.concatenate([sine_table, cosine], 1)
    return jnp.concatenate([top, bottom], 0)


def block_product(row_piece, col_piece):
    left_side = jnp.concatenate([row_piece[0], row_piece[1]], -1)
    swapped = jnp.concatenate([row_piece[1], -row_piece[0]], -1)
    operand = jnp.stack([left_side, swapped])
    right_side = jnp.concatenate([col_piece[0], col_piece[1]], -1)
    return jnp.einsum("sczk,cyk->sczy", operand, right_side, preferred_element_type=jnp.float32)


def shards(voltages, fir_taps):
    inputs_loc = voltages.shape[1]
    tap_count, channel_count = fir_taps.shape
    frames = voltages.shape[2] // channel_count
    framed = voltages.reshape(2, inputs_loc, frames, channel_count)
    history = from_behind(framed[:, :, frames - (tap_count - 1) :, :], ("row", "col"), 1)
    extended = jnp.concatenate([history, framed], 2).astype(jnp.float32)
    filtered = jnp.zeros((2, inputs_loc, frames, channel_count), jnp.float32)
    for step in range(tap_count):
        filtered = (
            filtered
            + fir_taps[step]
            * extended[:, :, tap_count - 1 - step : tap_count - 1 - step + frames, :]
        )
    table = dft_tables(channel_count)
    joined = jnp.concatenate([filtered[0], filtered[1]], -1)
    result = jnp.einsum("ifn,nk->kif", joined, table, precision=lax.Precision.HIGHEST) * (
        1.0 / math.sqrt(channel_count)
    )
    spectra = result.reshape(2, channel_count, inputs_loc, frames).astype(jnp.bfloat16)
    turned = lax.all_to_all(spectra, "chan", split_axis=1, concat_axis=2, tiled=True)
    all_inputs = turned.shape[2]
    row_size = lax.axis_size("row")
    col_size = lax.axis_size("col")
    row_count = all_inputs // row_size
    col_count = all_inputs // col_size
    row_start = lax.axis_index("row") * row_count
    col_start = lax.axis_index("col") * col_count
    paired = lax.all_gather(turned, "row", axis=3, tiled=True)
    piece = lax.all_gather(paired, "col", axis=3, tiled=True)
    row_piece = lax.dynamic_slice_in_dim(piece, row_start, row_count, 2)
    col_piece = lax.dynamic_slice_in_dim(piece, col_start, col_count, 2)
    total = block_product(row_piece, col_piece)
    frame_total = frames * row_size * col_size
    row_ids = row_start + jnp.arange(row_count, dtype=jnp.int32)
    col_ids = col_start + jnp.arange(col_count, dtype=jnp.int32)
    upper = row_ids[:, None] < col_ids[None, :]
    scaled = total * (1.0 / math.sqrt(frame_total))
    return jnp.where(upper[None, None], scaled, 0.0).astype(jnp.bfloat16)


def solution(mesh):
    placed = (P(None, "chan", ("row", "col")), P())
    return jax.shard_map(
        shards, mesh=mesh, in_specs=placed, out_specs=P(None, "chan", "row", "col"), check_vma=False
    )
```

profile of v0, /device:TPU:1, one launch (start us, length us, event | category | flops | bytes accessed | tf_op | source)
XLA Modules:
  0.0 121.5 jit_solution(5468356979396395242)
XLA Ops:
  6.5 1.3 %reshape.44 = bf16[2,64,16,64]{3,2,1,0:T(8,128)(2,1)S(1)} reshape(bf16[2,64,1024]{2,1,0:T(8,128)(2,1)} %param.2) | data formatting | bytes 524288 | tf_op jit(solution)/shard_map/reshape | solution.py:38
  8.0 4.8 %collective-permute-start = (bf16[2,64,3,64]{3,1,2,0:T(8,128)(2,1)S(1)}, bf16[2,64,3,64]{3,1,2,0:T(8,128)(2,1)S(1)}, u32[]{:S(2)}, u32[]{:S(2)}) collective-permute-start(bf16[2,64,3,64]{3,1,2,0:T(8,128)(2,1)S(1)} %slice.62), channel_id=1, source_target_pairs={{0,1},{1,2},{2,3},{3,4},{4,5},{5,6},{6,7},{7,8},{8,9},{9,10},{10,1... | collective-permute-start | bytes 147464 | tf_op jit(solution)/shard_map/ppermute | solution.py:12
  13.0 0.8 slice_bitcast_fusion.5
  14.0 8.4 %collective-permute-done = bf16[2,64,3,64]{3,1,2,0:T(8,128)(2,1)S(1)} collective-permute-done((bf16[2,64,3,64]{3,1,2,0:T(8,128)(2,1)S(1)}, bf16[2,64,3,64]{3,1,2,0:T(8,128)(2,1)S(1)}, u32[]{:S(2)}, u32[]{:S(2)}) %collective-permute-start) | collective-permute-done | bytes 49184 | tf_op jit(solution)/shard_map/ppermute | solution.py:12
  22.6 0.2 fusion.8
  22.9 0.7 fusion.7
  23.8 0.7 copy.22
  24.5 0.4 reshape.48
  24.9 19.9 %all_to_all.18 = bf16[32,2,2048]{2,1,0:T(2,128)(2,1)S(1)} all-to-all(bf16[32,2,2048]{2,1,0:T(2,128)(2,1)S(1)} %reshape.48), channel_id=1, replica_groups=mesh['chan'=32,'row'=2,'col'=8] {'chan'}, dimensions={0} | all-to-all | bytes 524288 | tf_op jit(solution)/shard_map/all_to_all | solution.py:54
  44.7 0.4 reshape.49
  45.1 0.3 copy.32
  45.5 0.4 reshape.47
  45.9 2.3 %all_gather.6 = bf16[2,2,2048,32]{2,1,0,3:T(2,128)(2,1)} all-gather(bf16[2,2,2048,16]{2,1,0,3:T(2,128)(2,1)S(1)} %reshape.47), channel_id=1, replica_groups=mesh['chan'=32,'row'=2,'col'=8] {'row'}, dimensions={3}, use_global_device_ids=true | all-gather | bytes 786432 | tf_op jit(solution)/shard_map/all_gather | solution.py:62
  48.4 52.5 %all-gather.2.cloned.1.call-done = bf16[2,2,2048,256]{2,1,0,3:T(2,128)(2,1)} async-done(((bf16[2,2,2048,32]{2,1,0,3:T(2,128)(2,1)}), bf16[2,2,2048,256]{2,1,0,3:T(2,128)(2,1)}) %all-gather.2.cloned.1.call-update) | async-done | bytes 4194320 | tf_op jit(solution)/shard_map/all_gather | solution.py:63
  101.0 3.0 %constant_dynamic-slice_fusion.2 = (bf16[1,2,1024,256]{2,1,0,3:T(2,128)(2,1)S(1)}, bf16[1,2,1024,256]{2,1,0,3:T(2,128)(2,1)S(1)}) fusion(bf16[2,2,2048,256]{2,1,0,3:T(2,128)(2,1)} %all-gather.2.cloned.1.call-done, s32[]{:T(128)S(6)} %add.57, s32[]{:T(128)S(6)} %select_n.25), kind=kLoop, calls=%fused_computation.49 | loop fusion | bytes 4194312 | tf_op jit(solution)/shard_map/slice | solution.py:27
  104.0 1.1 copy.39
  105.0 1.4 %constant_dynamic-slice_fusion.1 = (bf16[1,2,256,256]{2,1,0,3:T(2,128)(2,1)S(1)}, bf16[1,2,256,256]{2,1,0,3:T(2,128)(2,1)S(1)}) fusion(bf16[2,2,2048,256]{2,1,0,3:T(2,128)(2,1)} %all-gather.2.cloned.1.call-done, s32[]{:T(128)S(6)} %select_n.24, s32[]{:T(128)S(6)} %add.57), kind=kLoop, calls=%fused_computation.48 | loop fusion | bytes 1048584 | tf_op jit(solution)/shard_map/slice | solution.py:30
  106.5 0.9 copy.35
  107.3 0.9 copy.36
  108.2 1.0 copy.38
  109.4 0.4 maximum_bitcast_fusion
  109.7 0.6 copy-done
  110.4 1.6 %fusion.4 = bf16[2,2,1024,256]{2,3,0,1:T(8,128)(2,1)S(1)} fusion(pred[1024,256]{0,1:T(8,128)(4,1)S(1)} %broadcast_compare_fusion, bf16[1,2,1024,512]{3,2,0,1:T(8,128)(2,1)S(1)} %get-tuple-element.10, bf16[1,2,1024,512]{3,2,0,1:T(8,128)(2,1)S(1)} %get-tuple-element.9, bf16[2,256,256]{2,1,0:T(8,128)(2,1)S(1)} %bitcast.51, bf16[2,256,256]{2,1,0:T(8,128)(2,1)S(1)} %bitcast.50), kind=kOutput, calls=%fused_computation.5 | convolution fusion | flops 1086324736 | bytes 7077888 | tf_op jit(solution)/shard_map/sczk,cyk->sczy/dot_general | solution.py:31
  112.0 2.6 %copy.29 = bf16[2,2,1024,256]{3,2,1,0:T(8,128)(2,1)} copy(bf16[2,2,1024,256]{2,3,0,1:T(8,128)(2,1)S(1)} %fusion.4) | data formatting | bytes 4194304 | tf_op jit(solution)/shard_map/convert_element_type | solution.py:72
  (16 shorter events, 1.3 us)
Async XLA Ops:
  6.5 94.4 %all-gather.2.cloned.1.call-start = ((), (), s32[]{:S(2)}) async-start(), calls=%async_computation.1 | async-start | bytes 4718592 | tf_op jit(solution)/shard_map/all_gather | solution.py:63
  8.0 14.4 %collective-permute-start = (bf16[2,64,3,64]{3,1,2,0:T(8,128)(2,1)S(1)}, bf16[2,64,3,64]{3,1,2,0:T(8,128)(2,1)S(1)}, u32[]{:S(2)}, u32[]{:S(2)}) collective-permute-start(bf16[2,64,3,64]{3,1,2,0:T(8,128)(2,1)S(1)} %slice.62), channel_id=1, source_target_pairs={{0,1},{1,2},{2,3},{3,4},{4,5},{5,6},{6,7},{7,8},{8,9},{9,10},{10,1... | collective-permute-start | bytes 147464 | tf_op jit(solution)/shard_map/ppermute | solution.py:12
  109.4 1.0 copy-start
  109.4 1.0 copy-start.1
Sparse Core Ops, SparseCore 0:
  48.3 52.6 all-gather.1
where the time goes:
time: 122 us; the launch traced here: 121 us
  waiting for transfers between devices  60.9 us (50%)
  blocking collectives  22.2 us (18%)
  local copies, waits for them, and re-layouts  16.2 us (13%)
  between operations  13.6 us (11%)
  starting transfers between devices  4.83 us (4%)
  matrix products  2.3 us (2%)
  other arithmetic  1.35 us (1%)
    all_gather x1, waiting for transfers between devices, shards(): piece = lax.all_gather(paired, 'col', axis=3, tiled=True)  52.5 us
    all_to_all x1, blocking collectives, shards(): lax.all_to_all(spectra, 'chan', split_axis=1, concat_axis=2, tiled=True)  19.9 us
    ppermute x1, waiting for transfers between devices, from_behind(): return lax.ppermute(array, axis, pairs)  8.38 us
    unnamed x10, local copies, waits for them, and re-layouts  5.24 us
    ppermute x1, starting transfers between devices, from_behind(): return lax.ppermute(array, axis, pairs)  4.83 us
    slice x1, local copies, waits for them, and re-layouts, block_product(): left_side = jnp.concatenate([row_piece[0], row_piece[1]], -1)  3 us
    convert_element_type x1, local copies, waits for them, and re-layouts, shards(): return jnp.where(upper[None, None], scaled, 0.0).astype(jnp.bfloat16)  2.56 us
  transfers between devices with their start and end apart: 2, of which 2 were waited for; matrix products, arithmetic and copies ran while one was open for 1% of the time, Pallas kernels for 0%

commit v1 on v0

v1 whole, which is shorter than its diff:
```python
import functools
import math

import jax
import jax.numpy as jnp
import numpy as np
from jax import lax
from jax.experimental import pallas as pl
from jax.experimental.pallas import tpu as pltpu
from jax.sharding import PartitionSpec as P

VMEM_LIMIT = 40 * 1024 * 1024
LANES = 128


def interleaved_table(channels, group):
    index = np.arange(channels)
    angle = (index[:, None] * index[None, :] % channels) * (2.0 * math.pi / channels)
    cosine, sine = np.cos(angle), np.sin(angle)
    dft = np.stack([np.stack([cosine, sine], 1), np.stack([-sine, cosine], 1)], 1)
    dft = dft / math.sqrt(channels)
    table = np.einsum("kopn,tu->kotpun", dft, np.eye(group))
    return table.reshape(channels * 2 * group, 2 * group * channels).astype(np.float32)


def channelize_kernel(volt_ref, halo_ref, taps_ref, table_ref, out_ref):
    inputs, samples = volt_ref.shape[1:]
    channels = taps_ref.shape[1]
    wide = jnp.concatenate([taps_ref[...]] * (LANES // channels), 1)
    taps = jnp.concatenate([wide] * (samples // LANES), 1)
    head = halo_ref.shape[2]
    parts = []
    for part in range(2):
        extended = jnp.concatenate([halo_ref[part], volt_ref[part]], 1).astype(jnp.float32)
        rolled = pltpu.roll(extended, channels, 1)
        parts.append(
            taps[0:1] * extended[:, head:]
            + taps[1:2] * rolled[:, head:]
            + taps[2:3] * extended[:, head - LANES : head - LANES + samples]
            + taps[3:4] * rolled[:, head - LANES : head - LANES + samples]
        )
    width = table_ref.shape[1] // 2
    rows = []
    for start in range(0, samples, width):
        rows.append(
            jnp.concatenate([parts[0][:, start : start + width], parts[1][:, start : start + width]], 1)
        )
    frames = jnp.concatenate(rows, 0)
    spectra = lax.dot_general(
        table_ref[...],
        frames,
        (((1,), (1,)), ((), ())),
        precision=lax.Precision.HIGHEST,
        preferred_element_type=jnp.float32,
    )
    out_ref[...] = spectra.astype(jnp.bfloat16)


def turn_kernel(place_ref, in_ref, keep_ref, give_ref):
    row = place_ref[0]
    pairs = in_ref.shape[1] // 4
    lane = lax.broadcasted_iota(jnp.int32, (8, LANES), 1)
    low = lane < LANES // 2
    for mine, out_ref in ((True, keep_ref), (False, give_ref)):
        half = row if mine else 1 - row
        for pair in range(pairs):
            first = [in_ref[r, half * 2 * pairs + 2 * pair].astype(jnp.float32) for r in range(2)]
            second = [in_ref[r, half * 2 * pairs + 2 * pair + 1].astype(jnp.float32) for r in range(2)]
            pieces = []
            for ch in range(2):
                for g in range(4):
                    for r in range(2):
                        tile = (slice(ch * 8, ch * 8 + 8), slice((g // 2) * LANES, (g // 2 + 1) * LANES))
                        a, b = first[r][tile], second[r][tile]
                        if g % 2 == 0:
                            pieces.append(jnp.where(low, a, pltpu.roll(b, LANES // 2, 1)))
                        else:
                            pieces.append(jnp.where(low, pltpu.roll(a, LANES // 2, 1), b))
            block = jnp.concatenate(pieces, 0)
            out_ref[pl.ds(pair * LANES, LANES), :] = block.T.astype(jnp.bfloat16)


def by_channel(even, odd):
    low = lax.broadcasted_iota(jnp.int32, even.shape, 1) < LANES // 2
    a, b = even.astype(jnp.float32), odd.astype(jnp.float32)
    first = jnp.where(low, a, pltpu.roll(b, LANES // 2, 1))
    second = jnp.where(low, pltpu.roll(a, LANES // 2, 1), b)
    return first.astype(jnp.bfloat16), second.astype(jnp.bfloat16)


def correlate_kernel(scale, place_ref, *refs):
    left_refs, col_refs = refs[:8], refs[8:16]
    out_ref, right_ref = refs[16], refs[17]
    row, col = place_ref[0], place_ref[1]
    tile = pl.program_id(0)
    tile_rows = left_refs[0].shape[0]
    cols = col_refs[0].shape[0]

    @pl.when(tile == 0)
    def _():
        lane = lax.broadcasted_iota(jnp.int32, (cols, LANES), 1)
        real_lane = lane % 8 < 4
        for pair in range(4):
            blocks = by_channel(col_refs[2 * pair][...], col_refs[2 * pair + 1][...])
            for ch in range(2):
                block = blocks[ch]
                wide = block.astype(jnp.float32)
                turned = jnp.where(real_lane, -pltpu.roll(wide, LANES - 4, 1), pltpu.roll(wide, 4, 1))
                right_ref[ch, 0:cols, pair * LANES : (pair + 1) * LANES] = block
                right_ref[ch, cols : 2 * cols, pair * LANES : (pair + 1) * LANES] = turned.astype(jnp.bfloat16)

    lefts = ([], [])
    for pair in range(4):
        blocks = by_channel(left_refs[2 * pair][...], left_refs[2 * pair + 1][...])
        for ch in range(2):
            lefts[ch].append(blocks[ch])
    row_ids = row * (tile_rows * pl.num_programs(0)) + tile * tile_rows + lax.broadcasted_iota(
        jnp.int32, (tile_rows, cols), 0
    )
    col_ids = col * cols + lax.broadcasted_iota(jnp.int32, (tile_rows, cols), 1)
    upper = row_ids < col_ids
    for ch in range(2):
        left = jnp.concatenate(lefts[ch], 1)
        total = lax.dot_general(
            left, right_ref[ch], (((1,), (1,)), ((), ())), preferred_element_type=jnp.float32
        )
        total = total * scale
        out_ref[0, ch] = jnp.where(upper, total[:, :cols], 0.0).astype(jnp.bfloat16)
        out_ref[1, ch] = jnp.where(upper, total[:, cols:], 0.0).astype(jnp.bfloat16)


def shards(voltages, fir_taps):
    inputs_loc, samples = voltages.shape[1:]
    tap_count, channels = fir_taps.shape
    group = 4
    chan_size, row_size, col_size = (lax.axis_size(a) for a in ("chan", "row", "col"))
    row, col = lax.axis_index("row"), lax.axis_index("col")
    place = jnp.stack([row, col]).astype(jnp.int32)
    devices = row_size * col_size
    params = pltpu.CompilerParams(vmem_limit_bytes=VMEM_LIMIT)
    whole = pl.BlockSpec(memory_space=pltpu.VMEM)
    scalar = pl.BlockSpec(memory_space=pltpu.SMEM)

    halo = lax.ppermute(
        voltages[:, :, samples - group * channels :],
        ("row", "col"),
        [(i, i + 1) for i in range(devices - 1)],
    )
    table = jnp.asarray(interleaved_table(channels, group))
    frames_loc = samples // channels
    spectra = pl.pallas_call(
        channelize_kernel,
        out_shape=jax.ShapeDtypeStruct((channels * 2 * group, frames_loc // group * inputs_loc), jnp.bfloat16),
        in_specs=[whole] * 4,
        out_specs=whole,
        compiler_params=params,
        name="channelize",
    )(voltages, halo, fir_taps, table)
    spectra = spectra.reshape(chan_size, -1, spectra.shape[1])
    turned = lax.all_to_all(spectra, "chan", split_axis=0, concat_axis=0, tiled=True)
    both = lax.all_gather(turned, "row", axis=0)

    half = chan_size * inputs_loc // row_size
    keep, give = pl.pallas_call(
        turn_kernel,
        out_shape=[jax.ShapeDtypeStruct((half, LANES), jnp.bfloat16)] * 2,
        in_specs=[scalar, whole],
        out_specs=[whole] * 2,
        compiler_params=params,
        name="turn",
    )(place, both)

    ahead = [(c, (c + 1) % col_size) for c in range(col_size)]
    behind = [(col_size + c, col_size + (c - 1) % col_size) for c in range(col_size)]
    on_ring = lambda array: lax.ppermute(array, ("row", "col"), ahead + behind)
    swap = lambda array: lax.ppermute(array, "row", [(0, 1), (1, 0)])

    cols = chan_size * inputs_loc // col_size
    col_offset = lax.rem(col, col_size // row_size) * cols
    next_offset = lax.rem(col + 1, col_size // row_size) * cols
    keeps, gives, others = [keep], [give], []
    for step in range(col_size // 2 - 1):
        keeps.append(on_ring(keeps[-1]))
        gives.append(on_ring(gives[-1]))
        others.append(swap(gives[-1]))
    last = on_ring(keeps[-1])
    last_col = on_ring(lax.dynamic_slice_in_dim(gives[-1], next_offset, cols, 0))
    col_part = lambda array: lax.dynamic_slice_in_dim(array, col_offset, cols, 0)
    far_cols = swap(jnp.stack([col_part(k) for k in keeps[1:]]))

    lefts = keeps + [last] + others
    elsewhere = (row == 0) & (col >= col_size // row_size)
    own_cols = [col_part(a) for a in lefts]
    other_cols = [col_part(a) for a in gives] + [last_col] + [far_cols[i] for i in range(len(others))]
    col_blocks = [jnp.where(elsewhere, o, m) for m, o in zip(own_cols, other_cols)]

    tile = 256
    out = pl.pallas_call(
        functools.partial(correlate_kernel, 1.0 / math.sqrt(frames_loc * devices)),
        grid=(half // tile,),
        out_shape=jax.ShapeDtypeStruct((2, 2, half, cols), jnp.bfloat16),
        in_specs=[scalar]
        + [pl.BlockSpec((tile, LANES), lambda i: (i, 0))] * 8
        + [pl.BlockSpec((cols, LANES), lambda i: (0, 0))] * 8,
        out_specs=pl.BlockSpec((2, 2, tile, cols), lambda i: (0, 0, i, 0)),
        scratch_shapes=[pltpu.VMEM((2, 2 * cols, 4 * LANES), jnp.bfloat16)],
        compiler_params=params,
        name="correlate",
    )(place, *lefts, *col_blocks)
    return out


def solution(mesh):
    placed = (P(None, "chan", ("row", "col")), P())
    return jax.shard_map(
        shards, mesh=mesh, in_specs=placed, out_specs=P(None, "chan", "row", "col"), check_vma=False
    )
```

time: 122 us -> 92.1 us (0.75)
  starting transfers between devices: 4.83 us -> 55.1 us
  waiting for transfers between devices: 60.9 us -> 22.4 us
  blocking collectives: 22.2 us -> 2.17 us
  between operations: 13.6 us -> 0.27 us
  local copies, waits for them, and re-layouts: 16.2 us -> 3.7 us
  Pallas kernels: 0 us -> 7.52 us
  matrix products: 2.3 us -> 0 us
    all_gather x1 -> x0, waiting for transfers between devices: 52.5 us -> none  [shards(): piece = lax.all_gather(paired, 'col', axis=3, tiled=True)]
    ppermute x1 -> x13, starting transfers between devices: 4.83 us -> 45.4 us  [the longest x8 30.5 us: shards(): on_ring = lambda array: lax.ppermute(array, ('row', 'col'), ahead + behind)]
    all_to_all x1 -> x0, blocking collectives: 19.9 us -> none  [shards(): lax.all_to_all(spectra, 'chan', split_axis=1, concat_axis=2, tiled=True)]
    all_to_all x0 -> x1, waiting for transfers between devices: none -> 10.3 us  [shards(): lax.all_to_all(spectra, 'chan', split_axis=0, concat_axis=0, tiled=True)]
    all_to_all x0 -> x1, starting transfers between devices: none -> 9.67 us  [shards(): lax.all_to_all(spectra, 'chan', split_axis=0, concat_axis=0, tiled=True)]
    pallas_call x0 -> x3, Pallas kernels: none -> 7.52 us  [the longest x1 4.42 us: shards(): pl.pallas_call(functools.partial(correlate_kernel, 1.0 / math.sqrt(frames...]
    ppermute x1 -> x13, waiting for transfers between devices: 8.38 us -> 12.1 us  [the longest x1 9.16 us: shards(): lax.ppermute(voltages[:, :, samples - group * channels:], ('row', 'col'),...]
    slice x3 -> x1, local copies, waits for them, and re-layouts: 4.42 us -> 0.84 us  [shards(): voltages[:, :, samples - group * channels:]]
  transfers between devices with their start and end apart: 2 -> 14, of which waited for: 2 -> 5; matrix products, arithmetic and copies ran while one was open for 1% -> 0% of each run, Pallas kernels for 0% -> 0%
where the time goes in v1:
time: 92.1 us; the launch traced here: 91.5 us
  starting transfers between devices  55.1 us (60%)
  waiting for transfers between devices  22.4 us (24%)
  Pallas kernels  7.52 us (8%)
  local copies, waits for them, and re-layouts  3.7 us (4%)
  blocking collectives  2.17 us (2%)
    ppermute x8, starting transfers between devices, shards(): on_ring = lambda array: lax.ppermute(array, ('row', 'col'), ahead + behind)  30.5 us
    all_to_all x1, waiting for transfers between devices, shards(): lax.all_to_all(spectra, 'chan', split_axis=0, concat_axis=0, tiled=True)  10.3 us
    ppermute x4, starting transfers between devices, shards(): swap = lambda array: lax.ppermute(array, 'row', [(0, 1), (1, 0)])  10 us
    all_to_all x1, starting transfers between devices, shards(): lax.all_to_all(spectra, 'chan', split_axis=0, concat_axis=0, tiled=True)  9.67 us
    ppermute x1, waiting for transfers between devices, shards(): lax.ppermute(voltages[:, :, samples - group * channels:], ('row', 'col'),...  9.16 us
    ppermute x1, starting transfers between devices, shards(): lax.ppermute(voltages[:, :, samples - group * channels:], ('row', 'col'),...  4.82 us
    pallas_call x1, Pallas kernels, shards(): pl.pallas_call(functools.partial(correlate_kernel, 1.0 / math.sqrt(frames...  4.42 us
    unnamed x6, local copies, waits for them, and re-layouts  2.86 us
  transfers between devices with their start and end apart: 14, of which 5 were waited for; matrix products, arithmetic and copies ran while one was open for 0% of the time, Pallas kernels for 0%

profile of v1, /device:TPU:1, one launch (start us, length us, event | category | flops | bytes accessed | tf_op | source)
XLA Modules:
  0.0 91.5 jit_solution(4801538421924840180)
XLA Ops:
  0.8 4.8 %collective-permute-start = (bf16[2,64,256]{2,1,0:T(8,128)(2,1)S(1)}, bf16[2,64,256]{2,1,0:T(8,128)(2,1)S(1)}, u32[]{:S(2)}, u32[]{:S(2)}) collective-permute-start(bf16[2,64,256]{2,1,0:T(8,128)(2,1)S(1)} %slice.12), channel_id=1, source_target_pairs={{0,1},{1,2},{2,3},{3,4},{4,5},{5,6},{6,7},{7,8},{8,9},{9,10},{10,1... | collective-permute-start | bytes 196616 | tf_op jit(solution)/shard_map/ppermute | solution.py:144
  5.7 9.2 %collective-permute-done.halo_ref = bf16[2,64,256]{2,1,0:T(8,128)(2,1)S(1)} collective-permute-done((bf16[2,64,256]{2,1,0:T(8,128)(2,1)S(1)}, bf16[2,64,256]{2,1,0:T(8,128)(2,1)S(1)}, u32[]{:S(2)}, u32[]{:S(2)}) %collective-permute-start) | collective-permute-done | bytes 65568 | tf_op jit(solution)/shard_map/ppermute | solution.py:144
  14.8 1.2 %copy-done = f32[512,512]{1,0:T(8,128)S(1)} copy-done((f32[512,512]{1,0:T(8,128)S(1)}, f32[512,512]{1,0:T(8,128)}, u32[]{:S(2)}) %copy-start) | copy-done | bytes 1048600
  16.1 0.9 %copy-done.1 = bf16[2,64,1024]{2,1,0:T(8,128)(2,1)S(1)} copy-done((bf16[2,64,1024]{2,1,0:T(8,128)(2,1)S(1)}, bf16[2,64,1024]{2,1,0:T(8,128)(2,1)}, u32[]{:S(2)}) %copy-start.1) | copy-done | bytes 262168
  17.7 2.0 %channelize.1 = bf16[512,256]{1,0:T(8,128)(2,1)} custom-call(bf16[2,64,1024]{2,1,0:T(8,128)(2,1)S(1)} %copy-done.1, bf16[2,64,256]{2,1,0:T(8,128)(2,1)S(1)} %collective-permute-done.halo_ref, f32[4,64]{1,0:T(4,128)S(1)} %copy-done.2, f32[512,512]{1,0:T(8,128)S(1)} %copy-done), custom_call_target="tpu_custom_call" | custom-call | tf_op jit(solution)/shard_map/channelize/pallas_call | solution.py:151
  19.7 9.7 %all-to-all-start = ((bf16[32,16,256]{2,1,0:T(8,128)(2,1)}), bf16[32,16,256]{2,1,0:T(8,128)(2,1)S(1)}, u32[]{:S(2)}, u32[]{:S(2)}) async-start(bf16[32,16,256]{2,1,0:T(8,128)(2,1)} %bitcast.2), calls=%async_computation | async-start | bytes 524288 | tf_op jit(solution)/shard_map/all_to_all | solution.py:160
  29.5 10.3 %all-to-all-done = bf16[32,16,256]{2,1,0:T(8,128)(2,1)S(1)} async-done(((bf16[32,16,256]{2,1,0:T(8,128)(2,1)}), bf16[32,16,256]{2,1,0:T(8,128)(2,1)S(1)}, u32[]{:S(2)}, u32[]{:S(2)}) %all-to-all-start) | async-done | bytes 262176 | tf_op jit(solution)/shard_map/all_to_all | solution.py:160
  39.8 2.2 %all-gather = bf16[64,16,256]{2,1,0:T(8,128)(2,1)S(1)} all-gather(bf16[32,16,256]{2,1,0:T(8,128)(2,1)S(1)} %all-to-all-done), channel_id=2, replica_groups=mesh['chan'=32,'row'=2,'col'=8] {'row'}, dimensions={0}, use_global_device_ids=true | all-gather | bytes 786432 | tf_op jit(solution)/shard_map/all_gather | solution.py:161
  42.0 1.1 %turn.1 = (bf16[1024,128]{1,0:T(8,128)(2,1)S(1)}, bf16[1024,128]{1,0:T(8,128)(2,1)S(1)}) custom-call(s32[2]{0:T(128)S(1)} %pad_add_fusion.place_ref, bf16[2,32,16,256]{3,2,1,0:T(8,128)(2,1)S(1)} %bitcast.22), custom_call_target="tpu_custom_call" | custom-call | tf_op jit(solution)/shard_map/turn/pallas_call | solution.py:164
  43.0 5.9 %collective-permute-start.1 = (bf16[1024,128]{1,0:T(8,128)(2,1)S(1)}, bf16[1024,128]{1,0:T(8,128)(2,1)S(1)}, u32[]{:S(2)}, u32[]{:S(2)}) collective-permute-start(bf16[1024,128]{1,0:T(8,128)(2,1)S(1)} %get-tuple-element.7.refs_0_), channel_id=1, source_target_pairs={{0,1},{1,2},{2,3},{3,4},{4,5},{5,6},{6,7},{7,0},{8,15},{9,8},{10,9... | collective-permute-start | bytes 786440 | tf_op jit(solution)/shard_map/ppermute | solution.py:175
  48.9 2.2 %collective-permute-start.5 = (bf16[1024,128]{1,0:T(8,128)(2,1)S(1)}, bf16[1024,128]{1,0:T(8,128)(2,1)S(1)}, u32[]{:S(2)}, u32[]{:S(2)}) collective-permute-start(bf16[1024,128]{1,0:T(8,128)(2,1)S(1)} %get-tuple-element.8), channel_id=1, source_target_pairs={{0,1},{1,2},{2,3},{3,4},{4,5},{5,6},{6,7},{7,0},{8,15},{9,8},{10,9... | collective-permute-start | bytes 786440 | tf_op jit(solution)/shard_map/ppermute | solution.py:175
  51.1 1.1 %collective-permute-done.1.refs_1_ = bf16[1024,128]{1,0:T(8,128)(2,1)S(1)} collective-permute-done((bf16[1024,128]{1,0:T(8,128)(2,1)S(1)}, bf16[1024,128]{1,0:T(8,128)(2,1)S(1)}, u32[]{:S(2)}, u32[]{:S(2)}) %collective-permute-start.1) | collective-permute-done | bytes 262176 | tf_op jit(solution)/shard_map/ppermute | solution.py:175
  52.2 5.0 %collective-permute-start.2 = (bf16[1024,128]{1,0:T(8,128)(2,1)S(1)}, bf16[1024,128]{1,0:T(8,128)(2,1)S(1)}, u32[]{:S(2)}, u32[]{:S(2)}) collective-permute-start(bf16[1024,128]{1,0:T(8,128)(2,1)S(1)} %collective-permute-done.1.refs_1_), channel_id=1, source_target_pairs={{0,1},{1,2},{2,3},{3,4},{4,5},{5,6},{6,7},{7,0},{8,15},{9,8},{10,9... | collective-permute-start | bytes 786440 | tf_op jit(solution)/shard_map/ppermute | solution.py:175
  57.3 2.8 %collective-permute-start.7 = (bf16[1024,128]{1,0:T(8,128)(2,1)S(1)}, bf16[1024,128]{1,0:T(8,128)(2,1)S(1)}, u32[]{:S(2)}, u32[]{:S(2)}) collective-permute-start(bf16[1024,128]{1,0:T(8,128)(2,1)S(1)} %collective-permute-done.5), channel_id=1, source_target_pairs={{0,1},{1,2},{2,3},{3,4},{4,5},{5,6},{6,7},{7,0},{8,15},{9,8},{10,9... | collective-permute-start | bytes 786440 | tf_op jit(solution)/shard_map/ppermute | solution.py:175
  60.6 5.0 %collective-permute-start.3 = (bf16[1024,128]{1,0:T(8,128)(2,1)S(1)}, bf16[1024,128]{1,0:T(8,128)(2,1)S(1)}, u32[]{:S(2)}, u32[]{:S(2)}) collective-permute-start(bf16[1024,128]{1,0:T(8,128)(2,1)S(1)} %collective-permute-done.2.refs_2_), channel_id=1, source_target_pairs={{0,1},{1,2},{2,3},{3,4},{4,5},{5,6},{6,7},{7,0},{8,15},{9,8},{10,9... | collective-permute-start | bytes 786440 | tf_op jit(solution)/shard_map/ppermute | solution.py:175
  65.6 2.8 %collective-permute-start.9 = (bf16[1024,128]{1,0:T(8,128)(2,1)S(1)}, bf16[1024,128]{1,0:T(8,128)(2,1)S(1)}, u32[]{:S(2)}, u32[]{:S(2)}) collective-permute-start(bf16[1024,128]{1,0:T(8,128)(2,1)S(1)} %collective-permute-done.7), channel_id=1, source_target_pairs={{0,1},{1,2},{2,3},{3,4},{4,5},{5,6},{6,7},{7,0},{8,15},{9,8},{10,9... | collective-permute-start | bytes 786440 | tf_op jit(solution)/shard_map/ppermute | solution.py:175
  68.4 1.9 %collective-permute-start.6 = (bf16[1024,128]{1,0:T(8,128)(2,1)S(1)}, bf16[1024,128]{1,0:T(8,128)(2,1)S(1)}, u32[]{:S(2)}, u32[]{:S(2)}) collective-permute-start(bf16[1024,128]{1,0:T(8,128)(2,1)S(1)} %collective-permute-done.5), channel_id=1, source_target_pairs={{0,8},{8,0},{1,9},{9,1},{2,10},{10,2},{3,11},{11,3},{4,12},{12,4},... | collective-permute-start | bytes 786440 | tf_op jit(solution)/shard_map/ppermute | solution.py:176
  70.4 2.4 %collective-permute-start.8 = (bf16[1024,128]{1,0:T(8,128)(2,1)S(1)}, bf16[1024,128]{1,0:T(8,128)(2,1)S(1)}, u32[]{:S(2)}, u32[]{:S(2)}) collective-permute-start(bf16[1024,128]{1,0:T(8,128)(2,1)S(1)} %collective-permute-done.7), channel_id=1, source_target_pairs={{0,8},{8,0},{1,9},{9,1},{2,10},{10,2},{3,11},{11,3},{4,12},{12,4},... | collective-permute-start | bytes 786440 | tf_op jit(solution)/shard_map/ppermute | solution.py:176
  72.8 4.1 %collective-permute-start.4 = (bf16[1024,128]{1,0:T(8,128)(2,1)S(1)}, bf16[1024,128]{1,0:T(8,128)(2,1)S(1)}, u32[]{:S(2)}, u32[]{:S(2)}) collective-permute-start(bf16[1024,128]{1,0:T(8,128)(2,1)S(1)} %collective-permute-done.3.refs_3_), channel_id=1, source_target_pairs={{0,1},{1,2},{2,3},{3,4},{4,5},{5,6},{6,7},{7,0},{8,15},{9,8},{10,9... | collective-permute-start | bytes 786440 | tf_op jit(solution)/shard_map/ppermute | solution.py:175
  77.0 2.8 %collective-permute-start.11 = (bf16[256,128]{1,0:T(8,128)(2,1)S(1)}, bf16[256,128]{1,0:T(8,128)(2,1)S(1)}, u32[]{:S(2)}, u32[]{:S(2)}) collective-permute-start(bf16[256,128]{1,0:T(8,128)(2,1)S(1)} %get-tuple-element.15), channel_id=1, source_target_pairs={{0,1},{1,2},{2,3},{3,4},{4,5},{5,6},{6,7},{7,0},{8,15},{9,8},{10,9... | collective-permute-start | bytes 196616 | tf_op jit(solution)/shard_map/ppermute | solution.py:175
  79.8 3.8 %collective-permute-start.10 = (bf16[1024,128]{1,0:T(8,128)(2,1)S(1)}, bf16[1024,128]{1,0:T(8,128)(2,1)S(1)}, u32[]{:S(2)}, u32[]{:S(2)}) collective-permute-start(bf16[1024,128]{1,0:T(8,128)(2,1)S(1)} %collective-permute-done.9), channel_id=1, source_target_pairs={{0,8},{8,0},{1,9},{9,1},{2,10},{10,2},{3,11},{11,3},{4,12},{12,4},... | collective-permute-start | bytes 786440 | tf_op jit(solution)/shard_map/ppermute | solution.py:176
  83.7 1.9 %collective-permute-start.12 = (bf16[3,256,128]{2,1,0:T(8,128)(2,1)S(1)}, bf16[3,256,128]{2,1,0:T(8,128)(2,1)S(1)}, u32[]{:S(2)}, u32[]{:S(2)}) collective-permute-start(bf16[3,256,128]{2,1,0:T(8,128)(2,1)S(1)} %pad_maximum_fusion), channel_id=1, source_target_pairs={{0,8},{8,0},{1,9},{9,1},{2,10},{10,2},{3,11},{11,3},{4,12},{12,4},... | collective-permute-start | bytes 589832 | tf_op jit(solution)/shard_map/ppermute | solution.py:176
  85.7 1.3 %collective-permute-done.12 = bf16[3,256,128]{2,1,0:T(8,128)(2,1)S(1)} collective-permute-done((bf16[3,256,128]{2,1,0:T(8,128)(2,1)S(1)}, bf16[3,256,128]{2,1,0:T(8,128)(2,1)S(1)}, u32[]{:S(2)}, u32[]{:S(2)}) %collective-permute-start.12) | collective-permute-done | bytes 196640 | tf_op jit(solution)/shard_map/ppermute | solution.py:176
  87.1 4.4 %correlate.1 = bf16[2,2,1024,256]{3,2,1,0:T(8,128)(2,1)} custom-call(s32[2]{0:T(128)S(1)} %pad_add_fusion.place_ref, bf16[1024,128]{1,0:T(8,128)(2,1)S(1)} %get-tuple-element.7.refs_0_, bf16[1024,128]{1,0:T(8,128)(2,1)S(1)} %collective-permute-done.1.refs_1_, bf16[1024,128]{1,0:T(8,128)(2,1)S(1)} %collective-permute-done.2.refs_2_, ...), custom_call_target="tpu_custom_call" | custom-call | tf_op jit(solution)/shard_map/correlate/pallas_call | solution.py:198
  (23 shorter events, 2.3 us)
Async XLA Ops:
  0.8 14.0 %collective-permute-start = (bf16[2,64,256]{2,1,0:T(8,128)(2,1)S(1)}, bf16[2,64,256]{2,1,0:T(8,128)(2,1)S(1)}, u32[]{:S(2)}, u32[]{:S(2)}) collective-permute-start(bf16[2,64,256]{2,1,0:T(8,128)(2,1)S(1)} %slice.12), channel_id=1, source_target_pairs={{0,1},{1,2},{2,3},{3,4},{4,5},{5,6},{6,7},{7,8},{8,9},{9,10},{10,1... | collective-permute-start | bytes 196616 | tf_op jit(solution)/shard_map/ppermute | solution.py:144
  14.8 1.2 %copy-start = (f32[512,512]{1,0:T(8,128)S(1)}, f32[512,512]{1,0:T(8,128)}, u32[]{:S(2)}) copy-start(f32[512,512]{1,0:T(8,128)} %constant.26.clone.table_ref) | copy-start | bytes 3145732
  16.1 0.9 %copy-start.1 = (bf16[2,64,1024]{2,1,0:T(8,128)(2,1)S(1)}, bf16[2,64,1024]{2,1,0:T(8,128)(2,1)}, u32[]{:S(2)}) copy-start(bf16[2,64,1024]{2,1,0:T(8,128)(2,1)} %volt_ref.1) | copy-start | bytes 786436
  17.0 0.7 copy-start.2
  19.7 20.1 %all-to-all-start = ((bf16[32,16,256]{2,1,0:T(8,128)(2,1)}), bf16[32,16,256]{2,1,0:T(8,128)(2,1)S(1)}, u32[]{:S(2)}, u32[]{:S(2)}) async-start(bf16[32,16,256]{2,1,0:T(8,128)(2,1)} %bitcast.2), calls=%async_computation | async-start | bytes 524288 | tf_op jit(solution)/shard_map/all_to_all | solution.py:160
  43.0 9.2 %collective-permute-start.1 = (bf16[1024,128]{1,0:T(8,128)(2,1)S(1)}, bf16[1024,128]{1,0:T(8,128)(2,1)S(1)}, u32[]{:S(2)}, u32[]{:S(2)}) collective-permute-start(bf16[1024,128]{1,0:T(8,128)(2,1)S(1)} %get-tuple-element.7.refs_0_), channel_id=1, source_target_pairs={{0,1},{1,2},{2,3},{3,4},{4,5},{5,6},{6,7},{7,0},{8,15},{9,8},{10,9... | collective-permute-start | bytes 786440 | tf_op jit(solution)/shard_map/ppermute | solution.py:175
  48.9 8.3 %collective-permute-start.5 = (bf16[1024,128]{1,0:T(8,128)(2,1)S(1)}, bf16[1024,128]{1,0:T(8,128)(2,1)S(1)}, u32[]{:S(2)}, u32[]{:S(2)}) collective-permute-start(bf16[1024,128]{1,0:T(8,128)(2,1)S(1)} %get-tuple-element.8), channel_id=1, source_target_pairs={{0,1},{1,2},{2,3},{3,4},{4,5},{5,6},{6,7},{7,0},{8,15},{9,8},{10,9... | collective-permute-start | bytes 786440 | tf_op jit(solution)/shard_map/ppermute | solution.py:175
  52.2 8.3 %collective-permute-start.2 = (bf16[1024,128]{1,0:T(8,128)(2,1)S(1)}, bf16[1024,128]{1,0:T(8,128)(2,1)S(1)}, u32[]{:S(2)}, u32[]{:S(2)}) collective-permute-start(bf16[1024,128]{1,0:T(8,128)(2,1)S(1)} %collective-permute-done.1.refs_1_), channel_id=1, source_target_pairs={{0,1},{1,2},{2,3},{3,4},{4,5},{5,6},{6,7},{7,0},{8,15},{9,8},{10,9... | collective-permute-start | bytes 786440 | tf_op jit(solution)/shard_map/ppermute | solution.py:175
  57.3 8.3 %collective-permute-start.7 = (bf16[1024,128]{1,0:T(8,128)(2,1)S(1)}, bf16[1024,128]{1,0:T(8,128)(2,1)S(1)}, u32[]{:S(2)}, u32[]{:S(2)}) collective-permute-start(bf16[1024,128]{1,0:T(8,128)(2,1)S(1)} %collective-permute-done.5), channel_id=1, source_target_pairs={{0,1},{1,2},{2,3},{3,4},{4,5},{5,6},{6,7},{7,0},{8,15},{9,8},{10,9... | collective-permute-start | bytes 786440 | tf_op jit(solution)/shard_map/ppermute | solution.py:175
  60.6 12.3 %collective-permute-start.3 = (bf16[1024,128]{1,0:T(8,128)(2,1)S(1)}, bf16[1024,128]{1,0:T(8,128)(2,1)S(1)}, u32[]{:S(2)}, u32[]{:S(2)}) collective-permute-start(bf16[1024,128]{1,0:T(8,128)(2,1)S(1)} %collective-permute-done.2.refs_2_), channel_id=1, source_target_pairs={{0,1},{1,2},{2,3},{3,4},{4,5},{5,6},{6,7},{7,0},{8,15},{9,8},{10,9... | collective-permute-start | bytes 786440 | tf_op jit(solution)/shard_map/ppermute | solution.py:175
  65.6 11.3 %collective-permute-start.9 = (bf16[1024,128]{1,0:T(8,128)(2,1)S(1)}, bf16[1024,128]{1,0:T(8,128)(2,1)S(1)}, u32[]{:S(2)}, u32[]{:S(2)}) collective-permute-start(bf16[1024,128]{1,0:T(8,128)(2,1)S(1)} %collective-permute-done.7), channel_id=1, source_target_pairs={{0,1},{1,2},{2,3},{3,4},{4,5},{5,6},{6,7},{7,0},{8,15},{9,8},{10,9... | collective-permute-start | bytes 786440 | tf_op jit(solution)/shard_map/ppermute | solution.py:175
  68.4 17.2 %collective-permute-start.6 = (bf16[1024,128]{1,0:T(8,128)(2,1)S(1)}, bf16[1024,128]{1,0:T(8,128)(2,1)S(1)}, u32[]{:S(2)}, u32[]{:S(2)}) collective-permute-start(bf16[1024,128]{1,0:T(8,128)(2,1)S(1)} %collective-permute-done.5), channel_id=1, source_target_pairs={{0,8},{8,0},{1,9},{9,1},{2,10},{10,2},{3,11},{11,3},{4,12},{12,4},... | collective-permute-start | bytes 786440 | tf_op jit(solution)/shard_map/ppermute | solution.py:176
  70.4 15.3 %collective-permute-start.8 = (bf16[1024,128]{1,0:T(8,128)(2,1)S(1)}, bf16[1024,128]{1,0:T(8,128)(2,1)S(1)}, u32[]{:S(2)}, u32[]{:S(2)}) collective-permute-start(bf16[1024,128]{1,0:T(8,128)(2,1)S(1)} %collective-permute-done.7), channel_id=1, source_target_pairs={{0,8},{8,0},{1,9},{9,1},{2,10},{10,2},{3,11},{11,3},{4,12},{12,4},... | collective-permute-start | bytes 786440 | tf_op jit(solution)/shard_map/ppermute | solution.py:176
  72.8 12.8 %collective-permute-start.4 = (bf16[1024,128]{1,0:T(8,128)(2,1)S(1)}, bf16[1024,128]{1,0:T(8,128)(2,1)S(1)}, u32[]{:S(2)}, u32[]{:S(2)}) collective-permute-start(bf16[1024,128]{1,0:T(8,128)(2,1)S(1)} %collective-permute-done.3.refs_3_), channel_id=1, source_target_pairs={{0,1},{1,2},{2,3},{3,4},{4,5},{5,6},{6,7},{7,0},{8,15},{9,8},{10,9... | collective-permute-start | bytes 786440 | tf_op jit(solution)/shard_map/ppermute | solution.py:175
  77.0 6.6 %collective-permute-start.11 = (bf16[256,128]{1,0:T(8,128)(2,1)S(1)}, bf16[256,128]{1,0:T(8,128)(2,1)S(1)}, u32[]{:S(2)}, u32[]{:S(2)}) collective-permute-start(bf16[256,128]{1,0:T(8,128)(2,1)S(1)} %get-tuple-element.15), channel_id=1, source_target_pairs={{0,1},{1,2},{2,3},{3,4},{4,5},{5,6},{6,7},{7,0},{8,15},{9,8},{10,9... | collective-permute-start | bytes 196616 | tf_op jit(solution)/shard_map/ppermute | solution.py:175
  79.8 7.2 %collective-permute-start.10 = (bf16[1024,128]{1,0:T(8,128)(2,1)S(1)}, bf16[1024,128]{1,0:T(8,128)(2,1)S(1)}, u32[]{:S(2)}, u32[]{:S(2)}) collective-permute-start(bf16[1024,128]{1,0:T(8,128)(2,1)S(1)} %collective-permute-done.9), channel_id=1, source_target_pairs={{0,8},{8,0},{1,9},{9,1},{2,10},{10,2},{3,11},{11,3},{4,12},{12,4},... | collective-permute-start | bytes 786440 | tf_op jit(solution)/shard_map/ppermute | solution.py:176
  83.7 3.3 %collective-permute-start.12 = (bf16[3,256,128]{2,1,0:T(8,128)(2,1)S(1)}, bf16[3,256,128]{2,1,0:T(8,128)(2,1)S(1)}, u32[]{:S(2)}, u32[]{:S(2)}) collective-permute-start(bf16[3,256,128]{2,1,0:T(8,128)(2,1)S(1)} %pad_maximum_fusion), channel_id=1, source_target_pairs={{0,8},{8,0},{1,9},{9,1},{2,10},{10,2},{3,11},{11,3},{4,12},{12,4},... | collective-permute-start | bytes 589832 | tf_op jit(solution)/shard_map/ppermute | solution.py:176

commit v2 on v1

v2 whole, which is shorter than its diff:
```python
import functools
import math

import jax
import jax.numpy as jnp
import numpy as np
from jax import lax
from jax.experimental import pallas as pl
from jax.experimental.pallas import tpu as pltpu
from jax.sharding import PartitionSpec as P

VMEM_LIMIT = 40 * 1024 * 1024
LANES = 128


def interleaved_table(channels, group):
    index = np.arange(channels)
    angle = (index[:, None] * index[None, :] % channels) * (2.0 * math.pi / channels)
    cosine, sine = np.cos(angle), np.sin(angle)
    dft = np.stack([np.stack([cosine, sine], 1), np.stack([-sine, cosine], 1)], 1)
    dft = dft / math.sqrt(channels)
    table = np.einsum("kopn,tu->kotpun", dft, np.eye(group))
    table = table.reshape(channels * 2 * group, 2 * group * channels).astype(np.float32)
    high = table.astype(jnp.bfloat16)
    return high, (table - high.astype(np.float32)).astype(jnp.bfloat16)


def product_nt(a, b):
    return lax.dot_general(a, b, (((1,), (1,)), ((), ())), preferred_element_type=jnp.float32)


def channelize_kernel(volt_ref, halo_ref, taps_ref, high_ref, rest_ref, out_ref):
    inputs, samples = volt_ref.shape[1:]
    channels = taps_ref.shape[1]
    wide = jnp.concatenate([taps_ref[...]] * (LANES // channels), 1)
    taps = jnp.concatenate([wide] * (samples // LANES), 1)
    head = halo_ref.shape[2]
    parts = []
    for part in range(2):
        extended = jnp.concatenate([halo_ref[part], volt_ref[part]], 1).astype(jnp.float32)
        rolled = pltpu.roll(extended, channels, 1)
        parts.append(
            taps[0:1] * extended[:, head:]
            + taps[1:2] * rolled[:, head:]
            + taps[2:3] * extended[:, head - LANES : head - LANES + samples]
            + taps[3:4] * rolled[:, head - LANES : head - LANES + samples]
        )
    width = high_ref.shape[1] // 2
    rows = []
    for start in range(0, samples, width):
        rows.append(
            jnp.concatenate([parts[0][:, start : start + width], parts[1][:, start : start + width]], 1)
        )
    frames = jnp.concatenate(rows, 0)
    frames_high = frames.astype(jnp.bfloat16)
    frames_rest = (frames - frames_high.astype(jnp.float32)).astype(jnp.bfloat16)
    high = high_ref[...]
    spectra = product_nt(high, frames_rest) + product_nt(rest_ref[...], frames_high)
    spectra = spectra + product_nt(high, frames_high)
    out_ref[...] = spectra.astype(jnp.bfloat16)


def turn_kernel(place_ref, in_ref, keep_ref, give_ref):
    row, odd = place_ref[0], place_ref[1] % 2 == 1
    pairs = in_ref.shape[1] // 4
    half_lanes = LANES // 2
    low = lax.broadcasted_iota(jnp.int32, (8, LANES), 1) < half_lanes
    for mine, out_ref in ((True, keep_ref), (False, give_ref)):
        half = row if mine else 1 - row
        for pair in range(pairs):
            first = [in_ref[r, half * 2 * pairs + 2 * pair].astype(jnp.float32) for r in range(2)]
            second = [in_ref[r, half * 2 * pairs + 2 * pair + 1].astype(jnp.float32) for r in range(2)]
            pieces = []
            for ch in range(2):
                for g in range(4):
                    for r in range(2):
                        tile = (slice(ch * 8, ch * 8 + 8), slice((g // 2) * LANES, (g // 2 + 1) * LANES))
                        a, b = first[r][tile], second[r][tile]
                        if g % 2 == 0:
                            pieces.append(jnp.where(low, a, pltpu.roll(b, half_lanes, 1)))
                        else:
                            pieces.append(jnp.where(low, pltpu.roll(a, half_lanes, 1), b))
            count = len(pieces) // 2
            block = jnp.concatenate(
                [jnp.where(odd, pieces[(i + count) % (2 * count)], pieces[i]) for i in range(2 * count)], 0
            )
            out_ref[pl.ds(pair * LANES, LANES), :] = block.T.astype(jnp.bfloat16)


def by_channel(one, other):
    low = lax.broadcasted_iota(jnp.int32, one.shape, 1) < LANES // 2
    return jnp.where(low, one, other), jnp.where(low, other, one)


def correlate_kernel(scale, tile_rows, place_ref, k0, k1, k2, k3, k4, g0, g1, g2, g3, s1, s2, s3, f13, f4, out_ref, right_ref):
    row, col = place_ref[0], place_ref[1]
    away = 1 - row
    cols = out_ref.shape[3]
    tile = pl.program_id(0)
    per_half = k0.shape[0] // cols
    odd = col % 2
    lefts = [
        (lambda at: k0[at, :]), (lambda at: k1[at, :]),
        (lambda at: k2[at, :]), (lambda at: k3[at, :]),
        (lambda at: s2[away, at, :]), (lambda at: s1[away, at, :]),
        (lambda at: k4[at, :]), (lambda at: s3[away, at, :]),
    ]

    @pl.when(tile == 0)
    def _():
        at = pl.ds(pl.multiple_of((col % per_half) * cols, cols), cols)
        elsewhere = (row == 0) & (col >= per_half)
        others = [
            (lambda: g0[at, :]), (lambda: g1[at, :]),
            (lambda: g2[at, :]), (lambda: g3[at, :]),
            (lambda: f13[away, cols : 2 * cols, :]), (lambda: f13[away, 0:cols, :]),
            (lambda: f4[away]), (lambda: f13[away, 2 * cols : 3 * cols, :]),
        ]
        source = lax.broadcasted_iota(jnp.int32, (LANES, LANES), 0)
        target = lax.broadcasted_iota(jnp.int32, (LANES, LANES), 1)
        turn = jnp.where(source == target - 4, (target % 8 >= 4).astype(jnp.float32), 0.0)
        turn = turn - jnp.where(source == target + 4, (target % 8 < 4).astype(jnp.float32), 0.0)
        turn = turn.astype(jnp.bfloat16)
        blocks = [jnp.where(elsewhere, other(), own(at)) for own, other in zip(lefts, others)]
        for pair in range(4):
            lanes = slice(pair * LANES, (pair + 1) * LANES)
            for ch, block in enumerate(by_channel(blocks[2 * pair], blocks[2 * pair + 1])):
                right_ref[ch, 0:cols, lanes] = block
                turned = jnp.dot(block, turn, preferred_element_type=jnp.float32)
                right_ref[ch, cols : 2 * cols, lanes] = turned.astype(jnp.bfloat16)

    at = pl.ds(pl.multiple_of(tile * tile_rows, tile_rows), tile_rows)
    channels = ([], [])
    for pair in range(4):
        for ch, block in enumerate(by_channel(lefts[2 * pair](at), lefts[2 * pair + 1](at))):
            channels[ch].append(block)
    row_ids = row * k0.shape[0] + tile * tile_rows + lax.broadcasted_iota(jnp.int32, (tile_rows, cols), 0)
    col_ids = col * cols + lax.broadcasted_iota(jnp.int32, (tile_rows, cols), 1)
    upper = row_ids < col_ids
    for ch in range(2):
        total = product_nt(jnp.concatenate(channels[ch], 1), right_ref[ch]) * scale
        goes_to = jnp.where(odd == 1, 1 - ch, ch)
        out_ref[0, goes_to] = jnp.where(upper, total[:, :cols], 0.0).astype(jnp.bfloat16)
        out_ref[1, goes_to] = jnp.where(upper, total[:, cols:], 0.0).astype(jnp.bfloat16)


def shards(voltages, fir_taps):
    inputs_loc, samples = voltages.shape[1:]
    channels = fir_taps.shape[1]
    group = 4
    chan_size, row_size, col_size = (lax.axis_size(a) for a in ("chan", "row", "col"))
    row, col = lax.axis_index("row"), lax.axis_index("col")
    place = jnp.stack([row, col]).astype(jnp.int32)
    devices = row_size * col_size
    params = pltpu.CompilerParams(vmem_limit_bytes=VMEM_LIMIT)
    whole = pl.BlockSpec(memory_space=pltpu.VMEM)
    scalar = pl.BlockSpec(memory_space=pltpu.SMEM)

    halo = lax.ppermute(
        voltages[:, :, samples - group * channels :],
        ("row", "col"),
        [(i, i + 1) for i in range(devices - 1)],
    )
    high, rest = interleaved_table(channels, group)
    frames_loc = samples // channels
    spectra_shape = (channels * 2 * group, frames_loc // group * inputs_loc)
    fetched = lambda shape: pl.BlockSpec(shape, lambda i: (0,) * len(shape))
    spectra = pl.pallas_call(
        channelize_kernel,
        grid=(1,),
        out_shape=jax.ShapeDtypeStruct(spectra_shape, jnp.bfloat16),
        in_specs=[fetched(voltages.shape), whole, fetched(fir_taps.shape), fetched(high.shape), fetched(rest.shape)],
        out_specs=fetched(spectra_shape),
        compiler_params=params,
        name="channelize",
    )(voltages, halo, fir_taps, jnp.asarray(high), jnp.asarray(rest))
    spectra = spectra.reshape(chan_size, -1, spectra.shape[1])
    turned = lax.all_to_all(spectra, "chan", split_axis=0, concat_axis=0, tiled=True)
    both = lax.all_gather(turned, "row", axis=0)

    half = chan_size * inputs_loc // row_size
    keep, give = pl.pallas_call(
        turn_kernel,
        out_shape=[jax.ShapeDtypeStruct((half, LANES), jnp.bfloat16)] * 2,
        in_specs=[scalar, whole],
        out_specs=[whole] * 2,
        compiler_params=params,
        name="turn",
    )(place, both)

    ahead = [(c, (c + 1) % col_size) for c in range(col_size)]
    behind = [(col_size + c, col_size + (c - 1) % col_size) for c in range(col_size)]
    on_ring = lambda array: lax.ppermute(array, ("row", "col"), ahead + behind)
    on_chip = lambda array: lax.all_gather(array, "row", axis=0)

    cols = chan_size * inputs_loc // col_size
    col_offset = lax.rem(col, half // cols) * cols
    col_part = lambda array: lax.dynamic_slice_in_dim(array, col_offset, cols, 0)
    keeps, gives = [keep], [give]
    for step in range(col_size // 2 - 1):
        keeps.append(on_ring(keeps[-1]))
        gives.append(on_ring(gives[-1]))
    keeps.append(on_ring(keeps[-1]))
    shared = [on_chip(g) for g in gives[1:]]
    far = on_chip(jnp.concatenate([col_part(k) for k in keeps[1:-1]], 0))
    farthest = on_chip(col_part(keeps[-1]))

    tile = 256
    operands = [*keeps, *gives, *shared, far, farthest]
    return pl.pallas_call(
        functools.partial(correlate_kernel, 1.0 / math.sqrt(frames_loc * devices), tile),
        grid=(half // tile,),
        out_shape=jax.ShapeDtypeStruct((2, 2, half, cols), jnp.bfloat16),
        in_specs=[scalar] + [whole] * len(operands),
        out_specs=pl.BlockSpec((2, 2, tile, cols), lambda i: (0, 0, i, 0)),
        scratch_shapes=[pltpu.VMEM((2, 2 * cols, 4 * LANES), jnp.bfloat16)],
        compiler_params=params,
        name="correlate",
    )(place, *operands)


def solution(mesh):
    placed = (P(None, "chan", ("row", "col")), P())
    return jax.shard_map(
        shards, mesh=mesh, in_specs=placed, out_specs=P(None, "chan", "row", "col"), check_vma=False
    )
```

time: 92.1 us -> 88.9 us (0.965)
  starting transfers between devices: 55.1 us -> 39.5 us
  blocking collectives: 2.17 us -> 16.6 us
  waiting for transfers between devices: 22.4 us -> 20.6 us
    all_gather x0 -> x5, blocking collectives: none -> 14.5 us  [shards(): on_chip = lambda array: lax.all_gather(array, 'row', axis=0)]
    ppermute x4 -> x0, starting transfers between devices: 10 us -> none  [shards(): swap = lambda array: lax.ppermute(array, 'row', [(0, 1), (1, 0)])]
    ppermute x8 -> x7, starting transfers between devices: 30.5 us -> 25 us  [shards(): on_ring = lambda array: lax.ppermute(array, ('row', 'col'), ahead + behind)]
    ppermute x4 -> x0, waiting for transfers between devices: 1.35 us -> none  [shards(): swap = lambda array: lax.ppermute(array, 'row', [(0, 1), (1, 0)])]
    unnamed x6 -> x8, local copies, waits for them, and re-layouts: 2.86 us -> 3.71 us
  transfers between devices with their start and end apart: 14 -> 9, of which waited for: 5 -> 3; matrix products, arithmetic and copies ran while one was open for 0% -> 0% of each run, Pallas kernels for 0% -> 0%
where the time goes in v2:
time: 88.9 us; the launch traced here: 88.3 us
  starting transfers between devices  39.5 us (44%)
  waiting for transfers between devices  20.6 us (23%)
  blocking collectives  16.6 us (19%)
  Pallas kernels  6.63 us (7%)
  local copies, waits for them, and re-layouts  4.6 us (5%)
    ppermute x7, starting transfers between devices, shards(): on_ring = lambda array: lax.ppermute(array, ('row', 'col'), ahead + behind)  25 us
    all_gather x5, blocking collectives, shards(): on_chip = lambda array: lax.all_gather(array, 'row', axis=0)  14.5 us
    all_to_all x1, waiting for transfers between devices, shards(): lax.all_to_all(spectra, 'chan', split_axis=0, concat_axis=0, tiled=True)  10.3 us
    all_to_all x1, starting transfers between devices, shards(): lax.all_to_all(spectra, 'chan', split_axis=0, concat_axis=0, tiled=True)  9.67 us
    ppermute x1, waiting for transfers between devices, shards(): lax.ppermute(voltages[:, :, samples - group * channels:], ('row', 'col'),...  9.16 us
    ppermute x1, starting transfers between devices, shards(): lax.ppermute(voltages[:, :, samples - group * channels:], ('row', 'col'),...  4.82 us
    pallas_call x1, Pallas kernels, shards(): pl.pallas_call(functools.partial(correlate_kernel, 1.0 / math.sqrt(frames...  3.99 us
    unnamed x8, local copies, waits for them, and re-layouts  3.71 us
  transfers between devices with their start and end apart: 9, of which 3 were waited for; matrix products, arithmetic and copies ran while one was open for 0% of the time, Pallas kernels for 0%

profile of v2, /device:TPU:1, one launch (start us, length us, event | category | flops | bytes accessed | tf_op | source)
XLA Modules:
  0.0 88.3 jit_solution(15719361592322996203)
XLA Ops:
  0.8 4.8 %collective-permute-start = (bf16[2,64,256]{2,1,0:T(8,128)(2,1)S(1)}, bf16[2,64,256]{2,1,0:T(8,128)(2,1)S(1)}, u32[]{:S(2)}, u32[]{:S(2)}) collective-permute-start(bf16[2,64,256]{2,1,0:T(8,128)(2,1)S(1)} %slice.3), channel_id=1, source_target_pairs={{0,1},{1,2},{2,3},{3,4},{4,5},{5,6},{6,7},{7,8},{8,9},{9,10},{10,1... | collective-permute-start | bytes 196616 | tf_op jit(solution)/shard_map/ppermute | solution.py:159
  5.7 9.2 %collective-permute-done.halo_ref = bf16[2,64,256]{2,1,0:T(8,128)(2,1)S(1)} collective-permute-done((bf16[2,64,256]{2,1,0:T(8,128)(2,1)S(1)}, bf16[2,64,256]{2,1,0:T(8,128)(2,1)S(1)}, u32[]{:S(2)}, u32[]{:S(2)}) %collective-permute-start) | collective-permute-done | bytes 65568 | tf_op jit(solution)/shard_map/ppermute | solution.py:159
  14.8 1.0 %copy-done = bf16[512,512]{1,0:T(8,128)(2,1)S(1)} copy-done((bf16[512,512]{1,0:T(8,128)(2,1)S(1)}, bf16[512,512]{1,0:T(8,128)(2,1)}, u32[]{:S(2)}) %copy-start) | copy-done | bytes 524312
  15.9 1.0 %copy-done.1 = bf16[512,512]{1,0:T(8,128)(2,1)S(1)} copy-done((bf16[512,512]{1,0:T(8,128)(2,1)S(1)}, bf16[512,512]{1,0:T(8,128)(2,1)}, u32[]{:S(2)}) %copy-start.1) | copy-done | bytes 524312
  16.9 0.9 %copy-done.2 = bf16[2,64,1024]{2,1,0:T(8,128)(2,1)S(1)} copy-done((bf16[2,64,1024]{2,1,0:T(8,128)(2,1)S(1)}, bf16[2,64,1024]{2,1,0:T(8,128)(2,1)}, u32[]{:S(2)}) %copy-start.2) | copy-done | bytes 262168
  18.6 1.5 %channelize.1 = bf16[512,256]{1,0:T(8,128)(2,1)} custom-call(bf16[2,64,1024]{2,1,0:T(8,128)(2,1)S(1)} %copy-done.2, bf16[2,64,256]{2,1,0:T(8,128)(2,1)S(1)} %collective-permute-done.halo_ref, f32[4,64]{1,0:T(4,128)S(1)} %copy-done.3, bf16[512,512]{1,0:T(8,128)(2,1)S(1)} %copy-done.1, bf16[512,512]{1,0:T(8,128)(2,1)S(1)} %copy-done), custom_call_target="tpu_custom_call" | custom-call | tf_op jit(solution)/shard_map/channelize/pallas_call | solution.py:168
  20.1 9.7 %all-to-all-start = ((bf16[32,16,256]{2,1,0:T(8,128)(2,1)}), bf16[32,16,256]{2,1,0:T(8,128)(2,1)S(1)}, u32[]{:S(2)}, u32[]{:S(2)}) async-start(bf16[32,16,256]{2,1,0:T(8,128)(2,1)} %bitcast.2), calls=%async_computation | async-start | bytes 524288 | tf_op jit(solution)/shard_map/all_to_all | solution.py:178
  29.9 10.3 %all-to-all-done = bf16[32,16,256]{2,1,0:T(8,128)(2,1)S(1)} async-done(((bf16[32,16,256]{2,1,0:T(8,128)(2,1)}), bf16[32,16,256]{2,1,0:T(8,128)(2,1)S(1)}, u32[]{:S(2)}, u32[]{:S(2)}) %all-to-all-start) | async-done | bytes 262176 | tf_op jit(solution)/shard_map/all_to_all | solution.py:178
  40.2 2.2 %all-gather = bf16[64,16,256]{2,1,0:T(8,128)(2,1)S(1)} all-gather(bf16[32,16,256]{2,1,0:T(8,128)(2,1)S(1)} %all-to-all-done), channel_id=2, replica_groups=mesh['chan'=32,'row'=2,'col'=8] {'row'}, dimensions={0}, use_global_device_ids=true | all-gather | bytes 786432 | tf_op jit(solution)/shard_map/all_gather | solution.py:179
  42.3 1.1 %turn.1 = (bf16[1024,128]{1,0:T(8,128)(2,1)S(1)}, bf16[1024,128]{1,0:T(8,128)(2,1)S(1)}) custom-call(s32[2]{0:T(128)S(1)} %pad_add_fusion.place_ref, bf16[2,32,16,256]{3,2,1,0:T(8,128)(2,1)S(1)} %bitcast.9), custom_call_target="tpu_custom_call" | custom-call | tf_op jit(solution)/shard_map/turn/pallas_call | solution.py:182
  43.5 5.9 %collective-permute-start.1 = (bf16[1024,128]{1,0:T(8,128)(2,1)S(1)}, bf16[1024,128]{1,0:T(8,128)(2,1)S(1)}, u32[]{:S(2)}, u32[]{:S(2)}) collective-permute-start(bf16[1024,128]{1,0:T(8,128)(2,1)S(1)} %get-tuple-element.7.k0), channel_id=1, source_target_pairs={{0,1},{1,2},{2,3},{3,4},{4,5},{5,6},{6,7},{7,0},{8,15},{9,8},{10,9... | collective-permute-start | bytes 786440 | tf_op jit(solution)/shard_map/ppermute | solution.py:193
  49.4 2.2 %collective-permute-start.5 = (bf16[1024,128]{1,0:T(8,128)(2,1)S(1)}, bf16[1024,128]{1,0:T(8,128)(2,1)S(1)}, u32[]{:S(2)}, u32[]{:S(2)}) collective-permute-start(bf16[1024,128]{1,0:T(8,128)(2,1)S(1)} %get-tuple-element.8.g0), channel_id=1, source_target_pairs={{0,1},{1,2},{2,3},{3,4},{4,5},{5,6},{6,7},{7,0},{8,15},{9,8},{10,9... | collective-permute-start | bytes 786440 | tf_op jit(solution)/shard_map/ppermute | solution.py:193
  51.5 1.1 %collective-permute-done.1.k1 = bf16[1024,128]{1,0:T(8,128)(2,1)S(1)} collective-permute-done((bf16[1024,128]{1,0:T(8,128)(2,1)S(1)}, bf16[1024,128]{1,0:T(8,128)(2,1)S(1)}, u32[]{:S(2)}, u32[]{:S(2)}) %collective-permute-start.1) | collective-permute-done | bytes 262176 | tf_op jit(solution)/shard_map/ppermute | solution.py:193
  52.7 5.0 %collective-permute-start.2 = (bf16[1024,128]{1,0:T(8,128)(2,1)S(1)}, bf16[1024,128]{1,0:T(8,128)(2,1)S(1)}, u32[]{:S(2)}, u32[]{:S(2)}) collective-permute-start(bf16[1024,128]{1,0:T(8,128)(2,1)S(1)} %collective-permute-done.1.k1), channel_id=1, source_target_pairs={{0,1},{1,2},{2,3},{3,4},{4,5},{5,6},{6,7},{7,0},{8,15},{9,8},{10,9... | collective-permute-start | bytes 786440 | tf_op jit(solution)/shard_map/ppermute | solution.py:193
  57.7 2.8 %collective-permute-start.6 = (bf16[1024,128]{1,0:T(8,128)(2,1)S(1)}, bf16[1024,128]{1,0:T(8,128)(2,1)S(1)}, u32[]{:S(2)}, u32[]{:S(2)}) collective-permute-start(bf16[1024,128]{1,0:T(8,128)(2,1)S(1)} %collective-permute-done.5.g1), channel_id=1, source_target_pairs={{0,1},{1,2},{2,3},{3,4},{4,5},{5,6},{6,7},{7,0},{8,15},{9,8},{10,9... | collective-permute-start | bytes 786440 | tf_op jit(solution)/shard_map/ppermute | solution.py:193
  60.5 2.2 %all-gather.1 = bf16[2048,128]{1,0:T(8,128)(2,1)S(1)} all-gather(bf16[1024,128]{1,0:T(8,128)(2,1)S(1)} %collective-permute-done.5.g1), channel_id=3, replica_groups=mesh['chan'=32,'row'=2,'col'=8] {'row'}, dimensions={0}, use_global_device_ids=true | all-gather | bytes 786432 | tf_op jit(solution)/shard_map/all_gather | solution.py:194
  62.7 3.3 %collective-permute-start.3 = (bf16[1024,128]{1,0:T(8,128)(2,1)S(1)}, bf16[1024,128]{1,0:T(8,128)(2,1)S(1)}, u32[]{:S(2)}, u32[]{:S(2)}) collective-permute-start(bf16[1024,128]{1,0:T(8,128)(2,1)S(1)} %collective-permute-done.2.k2), channel_id=1, source_target_pairs={{0,1},{1,2},{2,3},{3,4},{4,5},{5,6},{6,7},{7,0},{8,15},{9,8},{10,9... | collective-permute-start | bytes 786440 | tf_op jit(solution)/shard_map/ppermute | solution.py:193
  66.0 2.8 %collective-permute-start.7 = (bf16[1024,128]{1,0:T(8,128)(2,1)S(1)}, bf16[1024,128]{1,0:T(8,128)(2,1)S(1)}, u32[]{:S(2)}, u32[]{:S(2)}) collective-permute-start(bf16[1024,128]{1,0:T(8,128)(2,1)S(1)} %collective-permute-done.6.g2), channel_id=1, source_target_pairs={{0,1},{1,2},{2,3},{3,4},{4,5},{5,6},{6,7},{7,0},{8,15},{9,8},{10,9... | collective-permute-start | bytes 786440 | tf_op jit(solution)/shard_map/ppermute | solution.py:193
  68.8 3.3 %all-gather.2 = bf16[2048,128]{1,0:T(8,128)(2,1)S(1)} all-gather(bf16[1024,128]{1,0:T(8,128)(2,1)S(1)} %collective-permute-done.6.g2), channel_id=4, replica_groups=mesh['chan'=32,'row'=2,'col'=8] {'row'}, dimensions={0}, use_global_device_ids=true | all-gather | bytes 786432 | tf_op jit(solution)/shard_map/all_gather | solution.py:194
  72.2 3.1 %collective-permute-start.4 = (bf16[1024,128]{1,0:T(8,128)(2,1)S(1)}, bf16[1024,128]{1,0:T(8,128)(2,1)S(1)}, u32[]{:S(2)}, u32[]{:S(2)}) collective-permute-start(bf16[1024,128]{1,0:T(8,128)(2,1)S(1)} %collective-permute-done.3.k3), channel_id=1, source_target_pairs={{0,1},{1,2},{2,3},{3,4},{4,5},{5,6},{6,7},{7,0},{8,15},{9,8},{10,9... | collective-permute-start | bytes 786440 | tf_op jit(solution)/shard_map/ppermute | solution.py:193
  75.3 2.1 %all-gather.4 = bf16[1536,128]{1,0:T(8,128)(2,1)S(1)} all-gather(bf16[768,128]{1,0:T(8,128)(2,1)S(1)} %pad_maximum_fusion), channel_id=6, replica_groups=mesh['chan'=32,'row'=2,'col'=8] {'row'}, dimensions={0}, use_global_device_ids=true | all-gather | bytes 589824 | tf_op jit(solution)/shard_map/all_gather | solution.py:194
  77.4 2.2 %all-gather.3 = bf16[2048,128]{1,0:T(8,128)(2,1)S(1)} all-gather(bf16[1024,128]{1,0:T(8,128)(2,1)S(1)} %collective-permute-done.7.g3), channel_id=5, replica_groups=mesh['chan'=32,'row'=2,'col'=8] {'row'}, dimensions={0}, use_global_device_ids=true | all-gather | bytes 786432 | tf_op jit(solution)/shard_map/all_gather | solution.py:194
  79.6 4.7 %all-gather.5 = bf16[512,128]{1,0:T(8,128)(2,1)S(1)} all-gather(bf16[256,128]{1,0:T(8,128)(2,1)S(1)} %constant_dynamic-slice_fusion), channel_id=7, replica_groups=mesh['chan'=32,'row'=2,'col'=8] {'row'}, dimensions={0}, use_global_device_ids=true | all-gather | bytes 196608 | tf_op jit(solution)/shard_map/all_gather | solution.py:194
  84.3 4.0 %correlate.1 = bf16[2,2,1024,256]{3,2,1,0:T(8,128)(2,1)} custom-call(s32[2]{0:T(128)S(1)} %pad_add_fusion.place_ref, bf16[1024,128]{1,0:T(8,128)(2,1)S(1)} %get-tuple-element.7.k0, bf16[1024,128]{1,0:T(8,128)(2,1)S(1)} %collective-permute-done.1.k1, bf16[1024,128]{1,0:T(8,128)(2,1)S(1)} %collective-permute-done.2.k2, ...), custom_call_target="tpu_custom_call" | custom-call | tf_op jit(solution)/shard_map/correlate/pallas_call | solution.py:210
  (18 shorter events, 1.7 us)
Async XLA Ops:
  0.8 14.0 %collective-permute-start = (bf16[2,64,256]{2,1,0:T(8,128)(2,1)S(1)}, bf16[2,64,256]{2,1,0:T(8,128)(2,1)S(1)}, u32[]{:S(2)}, u32[]{:S(2)}) collective-permute-start(bf16[2,64,256]{2,1,0:T(8,128)(2,1)S(1)} %slice.3), channel_id=1, source_target_pairs={{0,1},{1,2},{2,3},{3,4},{4,5},{5,6},{6,7},{7,8},{8,9},{9,10},{10,1... | collective-permute-start | bytes 196616 | tf_op jit(solution)/shard_map/ppermute | solution.py:159
  14.8 1.0 %copy-start = (bf16[512,512]{1,0:T(8,128)(2,1)S(1)}, bf16[512,512]{1,0:T(8,128)(2,1)}, u32[]{:S(2)}) copy-start(bf16[512,512]{1,0:T(8,128)(2,1)} %constant.24.clone.rest_ref) | copy-start | bytes 1572868
  15.9 1.0 %copy-start.1 = (bf16[512,512]{1,0:T(8,128)(2,1)S(1)}, bf16[512,512]{1,0:T(8,128)(2,1)}, u32[]{:S(2)}) copy-start(bf16[512,512]{1,0:T(8,128)(2,1)} %constant.23.clone.high_ref) | copy-start | bytes 1572868
  16.9 0.9 %copy-start.2 = (bf16[2,64,1024]{2,1,0:T(8,128)(2,1)S(1)}, bf16[2,64,1024]{2,1,0:T(8,128)(2,1)}, u32[]{:S(2)}) copy-start(bf16[2,64,1024]{2,1,0:T(8,128)(2,1)} %volt_ref.1) | copy-start | bytes 786436
  17.9 0.7 copy-start.3
  20.1 20.1 %all-to-all-start = ((bf16[32,16,256]{2,1,0:T(8,128)(2,1)}), bf16[32,16,256]{2,1,0:T(8,128)(2,1)S(1)}, u32[]{:S(2)}, u32[]{:S(2)}) async-start(bf16[32,16,256]{2,1,0:T(8,128)(2,1)} %bitcast.2), calls=%async_computation | async-start | bytes 524288 | tf_op jit(solution)/shard_map/all_to_all | solution.py:178
  43.5 9.2 %collective-permute-start.1 = (bf16[1024,128]{1,0:T(8,128)(2,1)S(1)}, bf16[1024,128]{1,0:T(8,128)(2,1)S(1)}, u32[]{:S(2)}, u32[]{:S(2)}) collective-permute-start(bf16[1024,128]{1,0:T(8,128)(2,1)S(1)} %get-tuple-element.7.k0), channel_id=1, source_target_pairs={{0,1},{1,2},{2,3},{3,4},{4,5},{5,6},{6,7},{7,0},{8,15},{9,8},{10,9... | collective-permute-start | bytes 786440 | tf_op jit(solution)/shard_map/ppermute | solution.py:193
  49.4 8.3 %collective-permute-start.5 = (bf16[1024,128]{1,0:T(8,128)(2,1)S(1)}, bf16[1024,128]{1,0:T(8,128)(2,1)S(1)}, u32[]{:S(2)}, u32[]{:S(2)}) collective-permute-start(bf16[1024,128]{1,0:T(8,128)(2,1)S(1)} %get-tuple-element.8.g0), channel_id=1, source_target_pairs={{0,1},{1,2},{2,3},{3,4},{4,5},{5,6},{6,7},{7,0},{8,15},{9,8},{10,9... | collective-permute-start | bytes 786440 | tf_op jit(solution)/shard_map/ppermute | solution.py:193
  52.7 10.0 %collective-permute-start.2 = (bf16[1024,128]{1,0:T(8,128)(2,1)S(1)}, bf16[1024,128]{1,0:T(8,128)(2,1)S(1)}, u32[]{:S(2)}, u32[]{:S(2)}) collective-permute-start(bf16[1024,128]{1,0:T(8,128)(2,1)S(1)} %collective-permute-done.1.k1), channel_id=1, source_target_pairs={{0,1},{1,2},{2,3},{3,4},{4,5},{5,6},{6,7},{7,0},{8,15},{9,8},{10,9... | collective-permute-start | bytes 786440 | tf_op jit(solution)/shard_map/ppermute | solution.py:193
  57.7 8.3 %collective-permute-start.6 = (bf16[1024,128]{1,0:T(8,128)(2,1)S(1)}, bf16[1024,128]{1,0:T(8,128)(2,1)S(1)}, u32[]{:S(2)}, u32[]{:S(2)}) collective-permute-start(bf16[1024,128]{1,0:T(8,128)(2,1)S(1)} %collective-permute-done.5.g1), channel_id=1, source_target_pairs={{0,1},{1,2},{2,3},{3,4},{4,5},{5,6},{6,7},{7,0},{8,15},{9,8},{10,9... | collective-permute-start | bytes 786440 | tf_op jit(solution)/shard_map/ppermute | solution.py:193
  62.7 9.5 %collective-permute-start.3 = (bf16[1024,128]{1,0:T(8,128)(2,1)S(1)}, bf16[1024,128]{1,0:T(8,128)(2,1)S(1)}, u32[]{:S(2)}, u32[]{:S(2)}) collective-permute-start(bf16[1024,128]{1,0:T(8,128)(2,1)S(1)} %collective-permute-done.2.k2), channel_id=1, source_target_pairs={{0,1},{1,2},{2,3},{3,4},{4,5},{5,6},{6,7},{7,0},{8,15},{9,8},{10,9... | collective-permute-start | bytes 786440 | tf_op jit(solution)/shard_map/ppermute | solution.py:193
  66.0 11.3 %collective-permute-start.7 = (bf16[1024,128]{1,0:T(8,128)(2,1)S(1)}, bf16[1024,128]{1,0:T(8,128)(2,1)S(1)}, u32[]{:S(2)}, u32[]{:S(2)}) collective-permute-start(bf16[1024,128]{1,0:T(8,128)(2,1)S(1)} %collective-permute-done.6.g2), channel_id=1, source_target_pairs={{0,1},{1,2},{2,3},{3,4},{4,5},{5,6},{6,7},{7,0},{8,15},{9,8},{10,9... | collective-permute-start | bytes 786440 | tf_op jit(solution)/shard_map/ppermute | solution.py:193
  72.2 7.4 %collective-permute-start.4 = (bf16[1024,128]{1,0:T(8,128)(2,1)S(1)}, bf16[1024,128]{1,0:T(8,128)(2,1)S(1)}, u32[]{:S(2)}, u32[]{:S(2)}) collective-permute-start(bf16[1024,128]{1,0:T(8,128)(2,1)S(1)} %collective-permute-done.3.k3), channel_id=1, source_target_pairs={{0,1},{1,2},{2,3},{3,4},{4,5},{5,6},{6,7},{7,0},{8,15},{9,8},{10,9... | collective-permute-start | bytes 786440 | tf_op jit(solution)/shard_map/ppermute | solution.py:193

commit v3 on v2

--- a/solution.py
+++ b/solution.py
@@ -10,6 +10,7 @@
 from jax.sharding import PartitionSpec as P
 
 VMEM_LIMIT = 40 * 1024 * 1024
+WIDE_VMEM_LIMIT = 60 * 1024 * 1024
 LANES = 128
 
 
@@ -29,35 +30,64 @@
     return lax.dot_general(a, b, (((1,), (1,)), ((), ())), preferred_element_type=jnp.float32)
 
 
-def channelize_kernel(volt_ref, halo_ref, taps_ref, high_ref, rest_ref, out_ref):
-    inputs, samples = volt_ref.shape[1:]
-    channels = taps_ref.shape[1]
-    wide = jnp.concatenate([taps_ref[...]] * (LANES // channels), 1)
-    taps = jnp.concatenate([wide] * (samples // LANES), 1)
-    head = halo_ref.shape[2]
+def filtered_groups(extended, taps, head, width):
+    samples = extended[0].shape[1] - head
+    channels = LANES // 2
     parts = []
-    for part in range(2):
-        extended = jnp.concatenate([halo_ref[part], volt_ref[part]], 1).astype(jnp.float32)
-        rolled = pltpu.roll(extended, channels, 1)
+    for wide in extended:
+        rolled = pltpu.roll(wide, channels, 1)
         parts.append(
-            taps[0:1] * extended[:, head:]
-            + taps[1:2] * rolled[:, head:]
-            + taps[2:3] * extended[:, head - LANES : head - LANES + samples]
-            + taps[3:4] * rolled[:, head - LANES : head - LANES + samples]
+            taps[0:1, :samples] * wide[:, head:]
+            + taps[1:2, :samples] * rolled[:, head:]
+            + taps[2:3, :samples] * wide[:, head - LANES : head - LANES + samples]
+            + taps[3:4, :samples] * rolled[:, head - LANES : head - LANES + samples]
         )
-    width = high_ref.shape[1] // 2
-    rows = []
-    for start in range(0, samples, width):
-        rows.append(
-            jnp.concatenate([parts[0][:, start : start + width], parts[1][:, start : start + width]], 1)
-        )
-    frames = jnp.concatenate(rows, 0)
+    rows = [
+        jnp.concatenate([p[:, start : start + width] for p in parts], 1) for start in range(0, samples, width)
+    ]
+    return jnp.concatenate(rows, 0)
+
+
+def transformed(frames, high, rest):
     frames_high = frames.astype(jnp.bfloat16)
     frames_rest = (frames - frames_high.astype(jnp.float32)).astype(jnp.bfloat16)
-    high = high_ref[...]
-    spectra = product_nt(high, frames_rest) + product_nt(rest_ref[...], frames_high)
-    spectra = spectra + product_nt(high, frames_high)
-    out_ref[...] = spectra.astype(jnp.bfloat16)
+    spectra = product_nt(high, frames_rest) + product_nt(rest, frames_high)
+    return (spectra + product_nt(high, frames_high)).astype(jnp.bfloat16)
+
+
+def later_kernel(
+    volt_hbm, taps_hbm, high_hbm, rest_hbm, volt_out, taps_out, high_out, rest_out, late_out, volt_ref, taps_ref, sems
+):
+    copies = [
+        pltpu.make_async_copy(source, target, sems.at[i])
+        for i, (source, target) in enumerate(
+            ((volt_hbm, volt_ref), (taps_hbm, taps_ref), (high_hbm, high_out), (rest_hbm, rest_out))
+        )
+    ]
+    for copy in copies:
+        copy.start()
+    copies[0].wait()
+    copies[1].wait()
+    samples = volt_ref.shape[2]
+    wide = jnp.concatenate([taps_ref[...]] * (LANES // taps_ref.shape[1]), 1)
+    taps = jnp.concatenate([wide] * (samples // 2 // LANES), 1)
+    taps_out[...] = taps
+    volt_out[...] = volt_ref[:, :, : samples // 2]
+    width = high_out.shape[1] // 2
+    extended = [volt_ref[part, :, samples // 2 - width :].astype(jnp.float32) for part in range(2)]
+    frames = filtered_groups(extended, taps, width, width)
+    copies[2].wait()
+    copies[3].wait()
+    late_out[...] = transformed(frames, high_out[...], rest_out[...])
+
+
+def first_kernel(volt_ref, halo_ref, taps_ref, high_ref, rest_ref, late_ref, out_ref):
+    extended = [
+        jnp.concatenate([halo_ref[part], volt_ref[part]], 1).astype(jnp.float32) for part in range(2)
+    ]
+    frames = filtered_groups(extended, taps_ref[...], halo_ref.shape[2], high_ref.shape[1] // 2)
+    out_ref[:, :LANES] = transformed(frames, high_ref[...], rest_ref[...])
+    out_ref[:, LANES:] = late_ref[...]
 
 
 def turn_kernel(place_ref, in_ref, keep_ref, give_ref):
@@ -164,16 +194,33 @@
     high, rest = interleaved_table(channels, group)
     frames_loc = samples // channels
     spectra_shape = (channels * 2 * group, frames_loc // group * inputs_loc)
-    fetched = lambda shape: pl.BlockSpec(shape, lambda i: (0,) * len(shape))
+    in_hbm = pl.BlockSpec(memory_space=pltpu.HBM)
+    like = lambda array: jax.ShapeDtypeStruct(array.shape, array.dtype)
+    early = jax.ShapeDtypeStruct((2, inputs_loc, samples // 2), jnp.bfloat16)
+    taps_wide = jax.ShapeDtypeStruct((fir_taps.shape[0], samples // 2), jnp.float32)
+    late = jax.ShapeDtypeStruct((spectra_shape[0], spectra_shape[1] // 2), jnp.bfloat16)
+    volt_early, taps, high, rest, late = pl.pallas_call(
+        later_kernel,
+        out_shape=[early, taps_wide, like(high), like(rest), late],
+        in_specs=[in_hbm] * 4,
+        out_specs=[whole] * 5,
+        scratch_shapes=[
+            pltpu.VMEM(voltages.shape, jnp.bfloat16),
+            pltpu.VMEM(fir_taps.shape, jnp.float32),
+            pltpu.SemaphoreType.DMA((4,)),
+        ],
+        cost_estimate=pl.CostEstimate(flops=500_000_000, bytes_accessed=3_000_000, transcendentals=0),
+        compiler_params=pltpu.CompilerParams(vmem_limit_bytes=WIDE_VMEM_LIMIT),
+        name="later_frames",
+    )(voltages, fir_taps, jnp.asarray(high), jnp.asarray(rest))
     spectra = pl.pallas_call(
-        channelize_kernel,
-        grid=(1,),
+        first_kernel,
         out_shape=jax.ShapeDtypeStruct(spectra_shape, jnp.bfloat16),
-        in_specs=[fetched(voltages.shape), whole, fetched(fir_taps.shape), fetched(high.shape), fetched(rest.shape)],
-        out_specs=fetched(spectra_shape),
+        in_specs=[whole] * 6,
+        out_specs=whole,
         compiler_params=params,
-        name="channelize",
-    )(voltages, halo, fir_taps, jnp.asarray(high), jnp.asarray(rest))
+        name="first_frames",
+    )(volt_early, halo, taps, high, rest, late)
     spectra = spectra.reshape(chan_size, -1, spectra.shape[1])
     turned = lax.all_to_all(spectra, "chan", split_axis=0, concat_axis=0, tiled=True)
     both = lax.all_gather(turned, "row", axis=0)

time: 88.9 us -> 89.7 us (level)
  waiting for transfers between devices: 20.6 us -> 17.5 us
  Pallas kernels: 6.63 us -> 9.06 us
    ppermute x1, waiting for transfers between devices: 9.16 us -> 6.59 us  [shards(): lax.ppermute(voltages[:, :, samples - group * channels:], ('row', 'col'),...]
    pallas_call x1 -> x2, Pallas kernels: 1.54 us -> 3.97 us  [the longest x1 2.56 us: shards(): pl.pallas_call(later_kernel, out_shape=[early, taps_wide, like(high), lik...]
    unnamed x8 -> x10, local copies, waits for them, and re-layouts: 3.71 us -> 4.59 us
  transfers between devices with their start and end apart: 9 -> 9, of which waited for: 3 -> 3; matrix products, arithmetic and copies ran while one was open for 0% -> 0% of each run, Pallas kernels for 0% -> 3%
where the time goes in v3:
time: 89.7 us; the launch traced here: 89 us
  starting transfers between devices  40.1 us (45%)
  waiting for transfers between devices  17.5 us (20%)
  blocking collectives  16.6 us (19%)
  Pallas kernels  9.06 us (10%)
  local copies, waits for them, and re-layouts  5.47 us (6%)
    ppermute x7, starting transfers between devices, shards(): on_ring = lambda array: lax.ppermute(array, ('row', 'col'), ahead + behind)  25.6 us
    all_gather x5, blocking collectives, shards(): on_chip = lambda array: lax.all_gather(array, 'row', axis=0)  14.5 us
    all_to_all x1, waiting for transfers between devices, shards(): lax.all_to_all(spectra, 'chan', split_axis=0, concat_axis=0, tiled=True)  10.1 us
    all_to_all x1, starting transfers between devices, shards(): lax.all_to_all(spectra, 'chan', split_axis=0, concat_axis=0, tiled=True)  9.67 us
    ppermute x1, waiting for transfers between devices, shards(): lax.ppermute(voltages[:, :, samples - group * channels:], ('row', 'col'),...  6.59 us
    ppermute x1, starting transfers between devices, shards(): lax.ppermute(voltages[:, :, samples - group * channels:], ('row', 'col'),...  4.82 us
    unnamed x10, local copies, waits for them, and re-layouts  4.59 us
    pallas_call x1, Pallas kernels, shards(): pl.pallas_call(functools.partial(correlate_kernel, 1.0 / math.sqrt(frames...  3.99 us
  transfers between devices with their start and end apart: 9, of which 3 were waited for; matrix products, arithmetic and copies ran while one was open for 0% of the time, Pallas kernels for 3%

profile of v3, /device:TPU:1, one launch (start us, length us, event | category | flops | bytes accessed | tf_op | source)
XLA Modules:
  0.0 89.0 jit_solution(17067473443946965150)
XLA Ops:
  0.8 4.8 %collective-permute-start = (bf16[2,64,256]{2,1,0:T(8,128)(2,1)S(1)}, bf16[2,64,256]{2,1,0:T(8,128)(2,1)S(1)}, u32[]{:S(2)}, u32[]{:S(2)}) collective-permute-start(bf16[2,64,256]{2,1,0:T(8,128)(2,1)S(1)} %slice.3), channel_id=1, source_target_pairs={{0,1},{1,2},{2,3},{3,4},{4,5},{5,6},{6,7},{7,8},{8,9},{9,10},{10,1... | collective-permute-start | bytes 196616 | tf_op jit(solution)/shard_map/ppermute | solution.py:189
  5.7 2.6 %later_frames.1 = (bf16[2,64,512]{2,1,0:T(8,128)(2,1)}, f32[4,512]{1,0:T(4,128)}, bf16[512,512]{1,0:T(8,128)(2,1)}, bf16[512,512]{1,0:T(8,128)(2,1)}, bf16[512,128]{1,0:T(8,128)(2,1)}) custom-call(bf16[2,64,1024]{2,1,0:T(8,128)(2,1)} %volt_hbm.1, f32[4,64]{1,0:T(4,128)} %taps_hbm.1, bf16[512,512]{1,0:T(8,128)(2,1)} %constant.23.clone.high_hbm, ...), custom_call_target="tpu_custom_call" | custom-call | flops 500000000 | bytes 3000000 | tf_op jit(solution)/shard_map/later_frames/pallas_call | solution.py:202
  8.2 6.6 %collective-permute-done.halo_ref = bf16[2,64,256]{2,1,0:T(8,128)(2,1)S(1)} collective-permute-done((bf16[2,64,256]{2,1,0:T(8,128)(2,1)S(1)}, bf16[2,64,256]{2,1,0:T(8,128)(2,1)S(1)}, u32[]{:S(2)}, u32[]{:S(2)}) %collective-permute-start) | collective-permute-done | bytes 65568 | tf_op jit(solution)/shard_map/ppermute | solution.py:189
  14.8 1.0 %copy-done = bf16[512,512]{1,0:T(8,128)(2,1)S(1)} copy-done((bf16[512,512]{1,0:T(8,128)(2,1)S(1)}, bf16[512,512]{1,0:T(8,128)(2,1)}, u32[]{:S(2)}) %copy-start) | copy-done | bytes 524312
  15.9 1.0 %copy-done.1 = bf16[512,512]{1,0:T(8,128)(2,1)S(1)} copy-done((bf16[512,512]{1,0:T(8,128)(2,1)S(1)}, bf16[512,512]{1,0:T(8,128)(2,1)}, u32[]{:S(2)}) %copy-start.1) | copy-done | bytes 524312
  16.9 0.9 %copy-done.2 = bf16[2,64,512]{2,1,0:T(8,128)(2,1)S(1)} copy-done((bf16[2,64,512]{2,1,0:T(8,128)(2,1)S(1)}, bf16[2,64,512]{2,1,0:T(8,128)(2,1)}, u32[]{:S(2)}) %copy-start.2) | copy-done | bytes 131096
  19.4 1.4 %first_frames.1 = bf16[512,256]{1,0:T(8,128)(2,1)} custom-call(bf16[2,64,512]{2,1,0:T(8,128)(2,1)S(1)} %copy-done.2, bf16[2,64,256]{2,1,0:T(8,128)(2,1)S(1)} %collective-permute-done.halo_ref, f32[4,512]{1,0:T(4,128)S(1)} %copy-done.4, bf16[512,512]{1,0:T(8,128)(2,1)S(1)} %copy-done, bf16[512,512]{1,0:T(8,128)(2,1)S(1)} %copy-done.1, ...), custom_call_target="tpu_custom_call" | custom-call | tf_op jit(solution)/shard_map/first_frames/pallas_call | solution.py:216
  20.8 9.7 %all-to-all-start = ((bf16[32,16,256]{2,1,0:T(8,128)(2,1)}), bf16[32,16,256]{2,1,0:T(8,128)(2,1)S(1)}, u32[]{:S(2)}, u32[]{:S(2)}) async-start(bf16[32,16,256]{2,1,0:T(8,128)(2,1)} %bitcast.2), calls=%async_computation | async-start | bytes 524288 | tf_op jit(solution)/shard_map/all_to_all | solution.py:225
  30.6 10.1 %all-to-all-done = bf16[32,16,256]{2,1,0:T(8,128)(2,1)S(1)} async-done(((bf16[32,16,256]{2,1,0:T(8,128)(2,1)}), bf16[32,16,256]{2,1,0:T(8,128)(2,1)S(1)}, u32[]{:S(2)}, u32[]{:S(2)}) %all-to-all-start) | async-done | bytes 262176 | tf_op jit(solution)/shard_map/all_to_all | solution.py:225
  40.7 2.2 %all-gather = bf16[64,16,256]{2,1,0:T(8,128)(2,1)S(1)} all-gather(bf16[32,16,256]{2,1,0:T(8,128)(2,1)S(1)} %all-to-all-done), channel_id=2, replica_groups=mesh['chan'=32,'row'=2,'col'=8] {'row'}, dimensions={0}, use_global_device_ids=true | all-gather | bytes 786432 | tf_op jit(solution)/shard_map/all_gather | solution.py:226
  42.9 1.1 %turn.1 = (bf16[1024,128]{1,0:T(8,128)(2,1)S(1)}, bf16[1024,128]{1,0:T(8,128)(2,1)S(1)}) custom-call(s32[2]{0:T(128)S(1)} %pad_add_fusion.place_ref, bf16[2,32,16,256]{3,2,1,0:T(8,128)(2,1)S(1)} %bitcast.9), custom_call_target="tpu_custom_call" | custom-call | tf_op jit(solution)/shard_map/turn/pallas_call | solution.py:229
  44.0 6.1 %collective-permute-start.1 = (bf16[1024,128]{1,0:T(8,128)(2,1)S(1)}, bf16[1024,128]{1,0:T(8,128)(2,1)S(1)}, u32[]{:S(2)}, u32[]{:S(2)}) collective-permute-start(bf16[1024,128]{1,0:T(8,128)(2,1)S(1)} %get-tuple-element.17.k0), channel_id=1, source_target_pairs={{0,1},{1,2},{2,3},{3,4},{4,5},{5,6},{6,7},{7,0},{8,15},{9,8},{10,9... | collective-permute-start | bytes 786440 | tf_op jit(solution)/shard_map/ppermute | solution.py:240
  50.1 2.6 %collective-permute-start.5 = (bf16[1024,128]{1,0:T(8,128)(2,1)S(1)}, bf16[1024,128]{1,0:T(8,128)(2,1)S(1)}, u32[]{:S(2)}, u32[]{:S(2)}) collective-permute-start(bf16[1024,128]{1,0:T(8,128)(2,1)S(1)} %get-tuple-element.18.g0), channel_id=1, source_target_pairs={{0,1},{1,2},{2,3},{3,4},{4,5},{5,6},{6,7},{7,0},{8,15},{9,8},{10,9... | collective-permute-start | bytes 786440 | tf_op jit(solution)/shard_map/ppermute | solution.py:240
  53.4 5.0 %collective-permute-start.2 = (bf16[1024,128]{1,0:T(8,128)(2,1)S(1)}, bf16[1024,128]{1,0:T(8,128)(2,1)S(1)}, u32[]{:S(2)}, u32[]{:S(2)}) collective-permute-start(bf16[1024,128]{1,0:T(8,128)(2,1)S(1)} %collective-permute-done.1.k1), channel_id=1, source_target_pairs={{0,1},{1,2},{2,3},{3,4},{4,5},{5,6},{6,7},{7,0},{8,15},{9,8},{10,9... | collective-permute-start | bytes 786440 | tf_op jit(solution)/shard_map/ppermute | solution.py:240
  58.4 2.8 %collective-permute-start.6 = (bf16[1024,128]{1,0:T(8,128)(2,1)S(1)}, bf16[1024,128]{1,0:T(8,128)(2,1)S(1)}, u32[]{:S(2)}, u32[]{:S(2)}) collective-permute-start(bf16[1024,128]{1,0:T(8,128)(2,1)S(1)} %collective-permute-done.5.g1), channel_id=1, source_target_pairs={{0,1},{1,2},{2,3},{3,4},{4,5},{5,6},{6,7},{7,0},{8,15},{9,8},{10,9... | collective-permute-start | bytes 786440 | tf_op jit(solution)/shard_map/ppermute | solution.py:240
  61.2 2.2 %all-gather.1 = bf16[2048,128]{1,0:T(8,128)(2,1)S(1)} all-gather(bf16[1024,128]{1,0:T(8,128)(2,1)S(1)} %collective-permute-done.5.g1), channel_id=3, replica_groups=mesh['chan'=32,'row'=2,'col'=8] {'row'}, dimensions={0}, use_global_device_ids=true | all-gather | bytes 786432 | tf_op jit(solution)/shard_map/all_gather | solution.py:241
  63.4 3.3 %collective-permute-start.3 = (bf16[1024,128]{1,0:T(8,128)(2,1)S(1)}, bf16[1024,128]{1,0:T(8,128)(2,1)S(1)}, u32[]{:S(2)}, u32[]{:S(2)}) collective-permute-start(bf16[1024,128]{1,0:T(8,128)(2,1)S(1)} %collective-permute-done.2.k2), channel_id=1, source_target_pairs={{0,1},{1,2},{2,3},{3,4},{4,5},{5,6},{6,7},{7,0},{8,15},{9,8},{10,9... | collective-permute-start | bytes 786440 | tf_op jit(solution)/shard_map/ppermute | solution.py:240
  66.8 2.8 %collective-permute-start.7 = (bf16[1024,128]{1,0:T(8,128)(2,1)S(1)}, bf16[1024,128]{1,0:T(8,128)(2,1)S(1)}, u32[]{:S(2)}, u32[]{:S(2)}) collective-permute-start(bf16[1024,128]{1,0:T(8,128)(2,1)S(1)} %collective-permute-done.6.g2), channel_id=1, source_target_pairs={{0,1},{1,2},{2,3},{3,4},{4,5},{5,6},{6,7},{7,0},{8,15},{9,8},{10,9... | collective-permute-start | bytes 786440 | tf_op jit(solution)/shard_map/ppermute | solution.py:240
  69.6 3.3 %all-gather.2 = bf16[2048,128]{1,0:T(8,128)(2,1)S(1)} all-gather(bf16[1024,128]{1,0:T(8,128)(2,1)S(1)} %collective-permute-done.6.g2), channel_id=4, replica_groups=mesh['chan'=32,'row'=2,'col'=8] {'row'}, dimensions={0}, use_global_device_ids=true | all-gather | bytes 786432 | tf_op jit(solution)/shard_map/all_gather | solution.py:241
  72.9 3.1 %collective-permute-start.4 = (bf16[1024,128]{1,0:T(8,128)(2,1)S(1)}, bf16[1024,128]{1,0:T(8,128)(2,1)S(1)}, u32[]{:S(2)}, u32[]{:S(2)}) collective-permute-start(bf16[1024,128]{1,0:T(8,128)(2,1)S(1)} %collective-permute-done.3.k3), channel_id=1, source_target_pairs={{0,1},{1,2},{2,3},{3,4},{4,5},{5,6},{6,7},{7,0},{8,15},{9,8},{10,9... | collective-permute-start | bytes 786440 | tf_op jit(solution)/shard_map/ppermute | solution.py:240
  76.0 2.1 %all-gather.4 = bf16[1536,128]{1,0:T(8,128)(2,1)S(1)} all-gather(bf16[768,128]{1,0:T(8,128)(2,1)S(1)} %pad_maximum_fusion), channel_id=6, replica_groups=mesh['chan'=32,'row'=2,'col'=8] {'row'}, dimensions={0}, use_global_device_ids=true | all-gather | bytes 589824 | tf_op jit(solution)/shard_map/all_gather | solution.py:241
  78.1 2.2 %all-gather.3 = bf16[2048,128]{1,0:T(8,128)(2,1)S(1)} all-gather(bf16[1024,128]{1,0:T(8,128)(2,1)S(1)} %collective-permute-done.7.g3), channel_id=5, replica_groups=mesh['chan'=32,'row'=2,'col'=8] {'row'}, dimensions={0}, use_global_device_ids=true | all-gather | bytes 786432 | tf_op jit(solution)/shard_map/all_gather | solution.py:241
  80.3 4.7 %all-gather.5 = bf16[512,128]{1,0:T(8,128)(2,1)S(1)} all-gather(bf16[256,128]{1,0:T(8,128)(2,1)S(1)} %constant_dynamic-slice_fusion), channel_id=7, replica_groups=mesh['chan'=32,'row'=2,'col'=8] {'row'}, dimensions={0}, use_global_device_ids=true | all-gather | bytes 196608 | tf_op jit(solution)/shard_map/all_gather | solution.py:241
  85.0 4.0 %correlate.1 = bf16[2,2,1024,256]{3,2,1,0:T(8,128)(2,1)} custom-call(s32[2]{0:T(128)S(1)} %pad_add_fusion.place_ref, bf16[1024,128]{1,0:T(8,128)(2,1)S(1)} %get-tuple-element.17.k0, bf16[1024,128]{1,0:T(8,128)(2,1)S(1)} %collective-permute-done.1.k1, bf16[1024,128]{1,0:T(8,128)(2,1)S(1)} %collective-permute-done.2.k2, ...), custom_call_target="tpu_custom_call" | custom-call | tf_op jit(solution)/shard_map/correlate/pallas_call | solution.py:257
  (21 shorter events, 3.4 us)
Async XLA Ops:
  0.8 14.0 %collective-permute-start = (bf16[2,64,256]{2,1,0:T(8,128)(2,1)S(1)}, bf16[2,64,256]{2,1,0:T(8,128)(2,1)S(1)}, u32[]{:S(2)}, u32[]{:S(2)}) collective-permute-start(bf16[2,64,256]{2,1,0:T(8,128)(2,1)S(1)} %slice.3), channel_id=1, source_target_pairs={{0,1},{1,2},{2,3},{3,4},{4,5},{5,6},{6,7},{7,8},{8,9},{9,10},{10,1... | collective-permute-start | bytes 196616 | tf_op jit(solution)/shard_map/ppermute | solution.py:189
  14.8 1.0 %copy-start = (bf16[512,512]{1,0:T(8,128)(2,1)S(1)}, bf16[512,512]{1,0:T(8,128)(2,1)}, u32[]{:S(2)}) copy-start(bf16[512,512]{1,0:T(8,128)(2,1)} %get-tuple-element.14.high_ref) | copy-start | bytes 1572868
  15.9 1.0 %copy-start.1 = (bf16[512,512]{1,0:T(8,128)(2,1)S(1)}, bf16[512,512]{1,0:T(8,128)(2,1)}, u32[]{:S(2)}) copy-start(bf16[512,512]{1,0:T(8,128)(2,1)} %get-tuple-element.15.rest_ref) | copy-start | bytes 1572868
  16.9 0.9 %copy-start.2 = (bf16[2,64,512]{2,1,0:T(8,128)(2,1)S(1)}, bf16[2,64,512]{2,1,0:T(8,128)(2,1)}, u32[]{:S(2)}) copy-start(bf16[2,64,512]{2,1,0:T(8,128)(2,1)} %get-tuple-element.12.volt_ref) | copy-start | bytes 393220
  17.8 0.9 %copy-start.3 = (bf16[512,128]{1,0:T(8,128)(2,1)S(1)}, bf16[512,128]{1,0:T(8,128)(2,1)}, u32[]{:S(2)}) copy-start(bf16[512,128]{1,0:T(8,128)(2,1)} %get-tuple-element.16.late_ref) | copy-start | bytes 393220
  18.7 0.7 copy-start.4
  20.8 19.9 %all-to-all-start = ((bf16[32,16,256]{2,1,0:T(8,128)(2,1)}), bf16[32,16,256]{2,1,0:T(8,128)(2,1)S(1)}, u32[]{:S(2)}, u32[]{:S(2)}) async-start(bf16[32,16,256]{2,1,0:T(8,128)(2,1)} %bitcast.2), calls=%async_computation | async-start | bytes 524288 | tf_op jit(solution)/shard_map/all_to_all | solution.py:225
  44.0 9.4 %collective-permute-start.1 = (bf16[1024,128]{1,0:T(8,128)(2,1)S(1)}, bf16[1024,128]{1,0:T(8,128)(2,1)S(1)}, u32[]{:S(2)}, u32[]{:S(2)}) collective-permute-start(bf16[1024,128]{1,0:T(8,128)(2,1)S(1)} %get-tuple-element.17.k0), channel_id=1, source_target_pairs={{0,1},{1,2},{2,3},{3,4},{4,5},{5,6},{6,7},{7,0},{8,15},{9,8},{10,9... | collective-permute-start | bytes 786440 | tf_op jit(solution)/shard_map/ppermute | solution.py:240
  50.1 8.3 %collective-permute-start.5 = (bf16[1024,128]{1,0:T(8,128)(2,1)S(1)}, bf16[1024,128]{1,0:T(8,128)(2,1)S(1)}, u32[]{:S(2)}, u32[]{:S(2)}) collective-permute-start(bf16[1024,128]{1,0:T(8,128)(2,1)S(1)} %get-tuple-element.18.g0), channel_id=1, source_target_pairs={{0,1},{1,2},{2,3},{3,4},{4,5},{5,6},{6,7},{7,0},{8,15},{9,8},{10,9... | collective-permute-start | bytes 786440 | tf_op jit(solution)/shard_map/ppermute | solution.py:240
  53.4 10.0 %collective-permute-start.2 = (bf16[1024,128]{1,0:T(8,128)(2,1)S(1)}, bf16[1024,128]{1,0:T(8,128)(2,1)S(1)}, u32[]{:S(2)}, u32[]{:S(2)}) collective-permute-start(bf16[1024,128]{1,0:T(8,128)(2,1)S(1)} %collective-permute-done.1.k1), channel_id=1, source_target_pairs={{0,1},{1,2},{2,3},{3,4},{4,5},{5,6},{6,7},{7,0},{8,15},{9,8},{10,9... | collective-permute-start | bytes 786440 | tf_op jit(solution)/shard_map/ppermute | solution.py:240
  58.4 8.3 %collective-permute-start.6 = (bf16[1024,128]{1,0:T(8,128)(2,1)S(1)}, bf16[1024,128]{1,0:T(8,128)(2,1)S(1)}, u32[]{:S(2)}, u32[]{:S(2)}) collective-permute-start(bf16[1024,128]{1,0:T(8,128)(2,1)S(1)} %collective-permute-done.5.g1), channel_id=1, source_target_pairs={{0,1},{1,2},{2,3},{3,4},{4,5},{5,6},{6,7},{7,0},{8,15},{9,8},{10,9... | collective-permute-start | bytes 786440 | tf_op jit(solution)/shard_map/ppermute | solution.py:240
  63.4 9.5 %collective-permute-start.3 = (bf16[1024,128]{1,0:T(8,128)(2,1)S(1)}, bf16[1024,128]{1,0:T(8,128)(2,1)S(1)}, u32[]{:S(2)}, u32[]{:S(2)}) collective-permute-start(bf16[1024,128]{1,0:T(8,128)(2,1)S(1)} %collective-permute-done.2.k2), channel_id=1, source_target_pairs={{0,1},{1,2},{2,3},{3,4},{4,5},{5,6},{6,7},{7,0},{8,15},{9,8},{10,9... | collective-permute-start | bytes 786440 | tf_op jit(solution)/shard_map/ppermute | solution.py:240
  66.8 11.3 %collective-permute-start.7 = (bf16[1024,128]{1,0:T(8,128)(2,1)S(1)}, bf16[1024,128]{1,0:T(8,128)(2,1)S(1)}, u32[]{:S(2)}, u32[]{:S(2)}) collective-permute-start(bf16[1024,128]{1,0:T(8,128)(2,1)S(1)} %collective-permute-done.6.g2), channel_id=1, source_target_pairs={{0,1},{1,2},{2,3},{3,4},{4,5},{5,6},{6,7},{7,0},{8,15},{9,8},{10,9... | collective-permute-start | bytes 786440 | tf_op jit(solution)/shard_map/ppermute | solution.py:240
  72.9 7.4 %collective-permute-start.4 = (bf16[1024,128]{1,0:T(8,128)(2,1)S(1)}, bf16[1024,128]{1,0:T(8,128)(2,1)S(1)}, u32[]{:S(2)}, u32[]{:S(2)}) collective-permute-start(bf16[1024,128]{1,0:T(8,128)(2,1)S(1)} %collective-permute-done.3.k3), channel_id=1, source_target_pairs={{0,1},{1,2},{2,3},{3,4},{4,5},{5,6},{6,7},{7,0},{8,15},{9,8},{10,9... | collective-permute-start | bytes 786440 | tf_op jit(solution)/shard_map/ppermute | solution.py:240

commit v4 on v3

--- a/solution.py
+++ b/solution.py
@@ -10,7 +10,7 @@
 from jax.sharding import PartitionSpec as P
 
 VMEM_LIMIT = 40 * 1024 * 1024
-WIDE_VMEM_LIMIT = 60 * 1024 * 1024
+WIDE_VMEM_LIMIT = 40 * 1024 * 1024
 LANES = 128
 
 
@@ -90,31 +90,33 @@
     out_ref[:, LANES:] = late_ref[...]
 
 
-def turn_kernel(place_ref, in_ref, keep_ref, give_ref):
-    row, odd = place_ref[0], place_ref[1] % 2 == 1
-    pairs = in_ref.shape[1] // 4
+def turn_kernel(place_ref, in_ref, out_ref):
+    swapped = (place_ref[0] + place_ref[1]) % 2 == 1
+    blocks = out_ref.shape[0] // LANES
     half_lanes = LANES // 2
     low = lax.broadcasted_iota(jnp.int32, (8, LANES), 1) < half_lanes
-    for mine, out_ref in ((True, keep_ref), (False, give_ref)):
-        half = row if mine else 1 - row
-        for pair in range(pairs):
-            first = [in_ref[r, half * 2 * pairs + 2 * pair].astype(jnp.float32) for r in range(2)]
-            second = [in_ref[r, half * 2 * pairs + 2 * pair + 1].astype(jnp.float32) for r in range(2)]
-            pieces = []
-            for ch in range(2):
-                for g in range(4):
-                    for r in range(2):
-                        tile = (slice(ch * 8, ch * 8 + 8), slice((g // 2) * LANES, (g // 2 + 1) * LANES))
-                        a, b = first[r][tile], second[r][tile]
-                        if g % 2 == 0:
-                            pieces.append(jnp.where(low, a, pltpu.roll(b, half_lanes, 1)))
-                        else:
-                            pieces.append(jnp.where(low, pltpu.roll(a, half_lanes, 1), b))
-            count = len(pieces) // 2
-            block = jnp.concatenate(
-                [jnp.where(odd, pieces[(i + count) % (2 * count)], pieces[i]) for i in range(2 * count)], 0
-            )
-            out_ref[pl.ds(pair * LANES, LANES), :] = block.T.astype(jnp.bfloat16)
+    for block in range(blocks):
+        pieces = []
+        for half in range(2):
+            source = 4 * (half * blocks + block)
+            first = [in_ref[source + r].astype(jnp.float32) for r in range(2)]
+            second = [in_ref[source + 2 + r].astype(jnp.float32) for r in range(2)]
+            for g in range(4):
+                lanes = slice((g // 2) * LANES, (g // 2 + 1) * LANES)
+                for r in range(2):
+                    a, b = first[r][:, lanes], second[r][:, lanes]
+                    if g % 2 == 0:
+                        pieces.append(jnp.where(low, a, pltpu.roll(b, half_lanes, 1)))
+                    else:
+                        pieces.append(jnp.where(low, pltpu.roll(a, half_lanes, 1), b))
+        count = len(pieces) // 2
+        rows = [jnp.where(swapped, pieces[(i + count) % (2 * count)], pieces[i]) for i in range(2 * count)]
+        out_ref[pl.ds(block * LANES, LANES), :] = jnp.concatenate(rows, 0).T.astype(jnp.bfloat16)
+
+
+def half_of(own, other, flip):
+    low = lax.broadcasted_iota(jnp.int32, own.shape, 1) < LANES // 2
+    return jnp.where(low != flip, own, other)
 
 
 def by_channel(one, other):
@@ -122,56 +124,77 @@
     return jnp.where(low, one, other), jnp.where(low, other, one)
 
 
-def correlate_kernel(scale, tile_rows, place_ref, k0, k1, k2, k3, k4, g0, g1, g2, g3, s1, s2, s3, f13, f4, out_ref, right_ref):
+def correlate_kernel(
+    scale, tile_rows, place_ref, a0, a1, a2, a3, b0, b1, b2, b3, s1, s2, s3, far, last, out_hbm, out_ref, right_ref, sems
+):
     row, col = place_ref[0], place_ref[1]
     away = 1 - row
     cols = out_ref.shape[3]
-    tile = pl.program_id(0)
-    per_half = k0.shape[0] // cols
-    odd = col % 2
+    half_rows = a0.shape[0]
+    per_half = half_rows // cols
+    odd = [(col + k) % 2 == 1 for k in range(5)]
+    flip_last = (col + row) % 2 == 1
     lefts = [
-        (lambda at: k0[at, :]), (lambda at: k1[at, :]),
-        (lambda at: k2[at, :]), (lambda at: k3[at, :]),
-        (lambda at: s2[away, at, :]), (lambda at: s1[away, at, :]),
-        (lambda at: k4[at, :]), (lambda at: s3[away, at, :]),
-    ]
-
-    @pl.when(tile == 0)
-    def _():
-        at = pl.ds(pl.multiple_of((col % per_half) * cols, cols), cols)
-        elsewhere = (row == 0) & (col >= per_half)
-        others = [
-            (lambda: g0[at, :]), (lambda: g1[at, :]),
-            (lambda: g2[at, :]), (lambda: g3[at, :]),
-            (lambda: f13[away, cols : 2 * cols, :]), (lambda: f13[away, 0:cols, :]),
-            (lambda: f4[away]), (lambda: f13[away, 2 * cols : 3 * cols, :]),
-        ]
-        source = lax.broadcasted_iota(jnp.int32, (LANES, LANES), 0)
-        target = lax.broadcasted_iota(jnp.int32, (LANES, LANES), 1)
-        turn = jnp.where(source == target - 4, (target % 8 >= 4).astype(jnp.float32), 0.0)
-        turn = turn - jnp.where(source == target + 4, (target % 8 < 4).astype(jnp.float32), 0.0)
-        turn = turn.astype(jnp.bfloat16)
-        blocks = [jnp.where(elsewhere, other(), own(at)) for own, other in zip(lefts, others)]
+        (lambda at: half_of(a0[at, :], b0[at, :], odd[0])),
+        (lambda at: half_of(a1[at, :], b1[at, :], odd[1])),
+        (lambda at: half_of(a2[at, :], b2[at, :], odd[2])),
+        (lambda at: half_of(a3[at, :], b3[at, :], odd[3])),
+        (lambda at: s2[away, at, :]),
+        (lambda at: s1[away, at, :]),
+        (lambda at: half_of(last[0, at, :], last[1, at, :], flip_last)),
+        (lambda at: s3[away, at, :]),
+    ]
+
+    at = pl.ds(pl.multiple_of((col % per_half) * cols, cols), cols)
+    elsewhere = (row == 0) & (col >= per_half)
+    others = [
+        (lambda: half_of(a0[at, :], b0[at, :], ~odd[0])),
+        (lambda: half_of(a1[at, :], b1[at, :], ~odd[1])),
+        (lambda: half_of(a2[at, :], b2[at, :], ~odd[2])),
+        (lambda: half_of(a3[at, :], b3[at, :], ~odd[3])),
+        (lambda: far[away, cols : 2 * cols, :]),
+        (lambda: far[away, 0:cols, :]),
+        (lambda: half_of(last[0, at, :], last[1, at, :], ~flip_last)),
+        (lambda: far[away, 2 * cols : 3 * cols, :]),
+    ]
+    target = lax.broadcasted_iota(jnp.int32, (LANES, LANES), 0)
+    source = lax.rem(
+        lax.broadcasted_iota(jnp.int32, (LANES, LANES), 1) + jnp.where(elsewhere, LANES // 2, 0), LANES
+    )
+    same = (source == target).astype(jnp.bfloat16)
+    turn = jnp.where(target == source - 4, (source % 8 >= 4).astype(jnp.float32), 0.0)
+    turn = turn - jnp.where(target == source + 4, (source % 8 < 4).astype(jnp.float32), 0.0)
+    turn = -turn.astype(jnp.bfloat16)
+    blocks = [jnp.where(elsewhere, other(), own(at)) for own, other in zip(lefts, others)]
+    for pair in range(4):
+        lanes = slice(pair * LANES, (pair + 1) * LANES)
+        first, second = by_channel(blocks[2 * pair], blocks[2 * pair + 1])
+        for ch, block in enumerate((jnp.where(elsewhere, second, first), jnp.where(elsewhere, first, second))):
+            right_ref[ch, lanes, 0:cols] = product_nt(same, block).astype(jnp.bfloat16)
+            right_ref[ch, lanes, cols : 2 * cols] = product_nt(turn, block).astype(jnp.bfloat16)
+
+    copies = []
+    for start in range(0, half_rows, tile_rows):
+        here = slice(start, start + tile_rows)
+        channels = ([], [])
         for pair in range(4):
-            lanes = slice(pair * LANES, (pair + 1) * LANES)
-            for ch, block in enumerate(by_channel(blocks[2 * pair], blocks[2 * pair + 1])):
-                right_ref[ch, 0:cols, lanes] = block
-                turned = jnp.dot(block, turn, preferred_element_type=jnp.float32)
-                right_ref[ch, cols : 2 * cols, lanes] = turned.astype(jnp.bfloat16)
-
-    at = pl.ds(pl.multiple_of(tile * tile_rows, tile_rows), tile_rows)
-    channels = ([], [])
-    for pair in range(4):
-        for ch, block in enumerate(by_channel(lefts[2 * pair](at), lefts[2 * pair + 1](at))):
-            channels[ch].append(block)
-    row_ids = row * k0.shape[0] + tile * tile_rows + lax.broadcasted_iota(jnp.int32, (tile_rows, cols), 0)
-    col_ids = col * cols + lax.broadcasted_iota(jnp.int32, (tile_rows, cols), 1)
-    upper = row_ids < col_ids
-    for ch in range(2):
-        total = product_nt(jnp.concatenate(channels[ch], 1), right_ref[ch]) * scale
-        goes_to = jnp.where(odd == 1, 1 - ch, ch)
-        out_ref[0, goes_to] = jnp.where(upper, total[:, :cols], 0.0).astype(jnp.bfloat16)
-        out_ref[1, goes_to] = jnp.where(upper, total[:, cols:], 0.0).astype(jnp.bfloat16)
+            for ch, block in enumerate(by_channel(lefts[2 * pair](here), lefts[2 * pair + 1](here))):
+                channels[ch].append(block)
+        row_ids = row * half_rows + start + lax.broadcasted_iota(jnp.int32, (tile_rows, cols), 0)
+        col_ids = col * cols + lax.broadcasted_iota(jnp.int32, (tile_rows, cols), 1)
+        upper = row_ids < col_ids
+        for ch in range(2):
+            left = jnp.concatenate(channels[ch], 1)
+            total = jnp.dot(left, right_ref[ch], preferred_element_type=jnp.float32) * scale
+            goes_to = jnp.where(flip_last, 1 - ch, ch)
+            out_ref[0, goes_to, here, :] = jnp.where(upper, total[:, :cols], 0.0).astype(jnp.bfloat16)
+            out_ref[1, goes_to, here, :] = jnp.where(upper, total[:, cols:], 0.0).astype(jnp.bfloat16)
+        copies.append(
+            pltpu.make_async_copy(out_ref.at[:, :, here, :], out_hbm.at[:, :, here, :], sems.at[len(copies)])
+        )
+        copies[-1].start()
+    for copy in copies:
+        copy.wait()
 
 
 def shards(voltages, fir_taps):
@@ -221,19 +244,18 @@
         compiler_params=params,
         name="first_frames",
     )(volt_early, halo, taps, high, rest, late)
-    spectra = spectra.reshape(chan_size, -1, spectra.shape[1])
-    turned = lax.all_to_all(spectra, "chan", split_axis=0, concat_axis=0, tiled=True)
-    both = lax.all_gather(turned, "row", axis=0)
+    spectra = spectra.reshape(chan_size * row_size, -1, spectra.shape[1])
+    turned = lax.all_to_all(spectra, ("chan", "row"), split_axis=0, concat_axis=0, tiled=True)
 
     half = chan_size * inputs_loc // row_size
-    keep, give = pl.pallas_call(
+    own = pl.pallas_call(
         turn_kernel,
-        out_shape=[jax.ShapeDtypeStruct((half, LANES), jnp.bfloat16)] * 2,
+        out_shape=jax.ShapeDtypeStruct((half, LANES), jnp.bfloat16),
         in_specs=[scalar, whole],
-        out_specs=[whole] * 2,
+        out_specs=whole,
         compiler_params=params,
         name="turn",
-    )(place, both)
+    )(place, turned)
 
     ahead = [(c, (c + 1) % col_size) for c in range(col_size)]
     behind = [(col_size + c, col_size + (c - 1) % col_size) for c in range(col_size)]
@@ -243,24 +265,31 @@
     cols = chan_size * inputs_loc // col_size
     col_offset = lax.rem(col, half // cols) * cols
     col_part = lambda array: lax.dynamic_slice_in_dim(array, col_offset, cols, 0)
-    keeps, gives = [keep], [give]
+    owns, others = [own], [lax.dynamic_index_in_dim(on_chip(own), 1 - row, 0, keepdims=False)]
     for step in range(col_size // 2 - 1):
-        keeps.append(on_ring(keeps[-1]))
-        gives.append(on_ring(gives[-1]))
-    keeps.append(on_ring(keeps[-1]))
-    shared = [on_chip(g) for g in gives[1:]]
-    far = on_chip(jnp.concatenate([col_part(k) for k in keeps[1:-1]], 0))
-    farthest = on_chip(col_part(keeps[-1]))
+        owns.append(on_ring(owns[-1]))
+        others.append(on_ring(others[-1]))
+    last = on_chip(on_ring(owns[-1]))
+    shared, far = [], []
+    for step in range(1, col_size // 2):
+        odd = lax.rem(col + step, 2) == 1
+        shared.append(on_chip(half_of(owns[step], others[step], ~odd)))
+        far.append(half_of(col_part(owns[step]), col_part(others[step]), odd))
+    far = on_chip(jnp.concatenate(far, 0))
 
     tile = 256
-    operands = [*keeps, *gives, *shared, far, farthest]
+    operands = [*owns, *others, *shared, far, last]
+    out_shape = (2, 2, half, cols)
     return pl.pallas_call(
         functools.partial(correlate_kernel, 1.0 / math.sqrt(frames_loc * devices), tile),
-        grid=(half // tile,),
-        out_shape=jax.ShapeDtypeStruct((2, 2, half, cols), jnp.bfloat16),
+        out_shape=jax.ShapeDtypeStruct(out_shape, jnp.bfloat16),
         in_specs=[scalar] + [whole] * len(operands),
-        out_specs=pl.BlockSpec((2, 2, tile, cols), lambda i: (0, 0, i, 0)),
-        scratch_shapes=[pltpu.VMEM((2, 2 * cols, 4 * LANES), jnp.bfloat16)],
+        out_specs=pl.BlockSpec(memory_space=pl.ANY),
+        scratch_shapes=[
+            pltpu.VMEM(out_shape, jnp.bfloat16),
+            pltpu.VMEM((2, 4 * LANES, 2 * cols), jnp.bfloat16),
+            pltpu.SemaphoreType.DMA((half // tile,)),
+        ],
         compiler_params=params,
         name="correlate",
     )(place, *operands)

time: 89.7 us -> 86.1 us (0.960)
  Pallas kernels: 9.06 us -> 6.25 us
  blocking collectives: 16.6 us -> 14.1 us
  waiting for transfers between devices: 17.5 us -> 18.9 us
  starting transfers between devices: 40.1 us -> 41.1 us
  local copies, waits for them, and re-layouts: 5.47 us -> 4.57 us
    all_to_all x1, waiting for transfers between devices: 10.1 us -> 13 us  [shards(): lax.all_to_all(spectra, ('chan', 'row'), split_axis=0, concat_axis=0, til...]
    all_gather x1 -> x0, blocking collectives: 2.17 us -> none  [shards(): both = lax.all_gather(turned, 'row', axis=0)]
    ppermute x1, waiting for transfers between devices: 6.59 us -> 4.56 us  [shards(): lax.ppermute(voltages[:, :, samples - group * channels:], ('row', 'col'),...]
    pallas_call x1, Pallas kernels: 2.56 us -> 0.88 us  [shards(): pl.pallas_call(later_kernel, out_shape=[early, taps_wide, like(high), lik...]
    pallas_call x1, Pallas kernels: 3.99 us -> 3.06 us  [shards(): pl.pallas_call(functools.partial(correlate_kernel, 1.0 / math.sqrt(frames...]
    unnamed x10 -> x8, local copies, waits for them, and re-layouts: 4.59 us -> 3.71 us
    all_gather x5 -> x6, blocking collectives: 14.5 us -> 14.1 us  [shards(): on_chip = lambda array: lax.all_gather(array, 'row', axis=0)]
  transfers between devices with their start and end apart: 9 -> 9, of which waited for: 3 -> 3; matrix products, arithmetic and copies ran while one was open for 0% -> 0% of each run, Pallas kernels for 3% -> 1%
where the time goes in v4:
time: 86.1 us; the launch traced here: 85.5 us
  starting transfers between devices  41.1 us (48%)
  waiting for transfers between devices  18.9 us (22%)
  blocking collectives  14.1 us (16%)
  Pallas kernels  6.25 us (7%)
  local copies, waits for them, and re-layouts  4.57 us (5%)
    ppermute x7, starting transfers between devices, shards(): on_ring = lambda array: lax.ppermute(array, ('row', 'col'), ahead + behind)  26.1 us
    all_gather x6, blocking collectives, shards(): on_chip = lambda array: lax.all_gather(array, 'row', axis=0)  14.1 us
    all_to_all x1, waiting for transfers between devices, shards(): lax.all_to_all(spectra, ('chan', 'row'), split_axis=0, concat_axis=0, til...  13 us
    all_to_all x1, starting transfers between devices, shards(): lax.all_to_all(spectra, ('chan', 'row'), split_axis=0, concat_axis=0, til...  10.2 us
    ppermute x1, starting transfers between devices, shards(): lax.ppermute(voltages[:, :, samples - group * channels:], ('row', 'col'),...  4.82 us
    ppermute x1, waiting for transfers between devices, shards(): lax.ppermute(voltages[:, :, samples - group * channels:], ('row', 'col'),...  4.56 us
    unnamed x8, local copies, waits for them, and re-layouts  3.71 us
    pallas_call x1, Pallas kernels, shards(): pl.pallas_call(functools.partial(correlate_kernel, 1.0 / math.sqrt(frames...  3.06 us
  transfers between devices with their start and end apart: 9, of which 3 were waited for; matrix products, arithmetic and copies ran while one was open for 0% of the time, Pallas kernels for 1%

profile of v4, /device:TPU:1, one launch (start us, length us, event | category | flops | bytes accessed | tf_op | source)
XLA Modules:
  0.0 85.5 jit_solution(13614850048835498855)
XLA Ops:
  0.8 4.8 %collective-permute-start = (bf16[2,64,256]{2,1,0:T(8,128)(2,1)S(1)}, bf16[2,64,256]{2,1,0:T(8,128)(2,1)S(1)}, u32[]{:S(2)}, u32[]{:S(2)}) collective-permute-start(bf16[2,64,256]{2,1,0:T(8,128)(2,1)S(1)} %slice.3), channel_id=1, source_target_pairs={{0,1},{1,2},{2,3},{3,4},{4,5},{5,6},{6,7},{7,8},{8,9},{9,10},{10,1... | collective-permute-start | bytes 196616 | tf_op jit(solution)/shard_map/ppermute | solution.py:212
  5.7 0.9 %copy-done = bf16[2,64,1024]{2,1,0:T(8,128)(2,1)S(1)} copy-done((bf16[2,64,1024]{2,1,0:T(8,128)(2,1)S(1)}, bf16[2,64,1024]{2,1,0:T(8,128)(2,1)}, u32[]{:S(2)}) %copy-start) | copy-done | bytes 262168
  7.3 1.0 %copy-done.2 = bf16[512,512]{1,0:T(8,128)(2,1)S(1)} copy-done((bf16[512,512]{1,0:T(8,128)(2,1)S(1)}, bf16[512,512]{1,0:T(8,128)(2,1)}, u32[]{:S(2)}) %copy-start.2) | copy-done | bytes 524312
  8.4 1.0 %copy-done.3 = bf16[512,512]{1,0:T(8,128)(2,1)S(1)} copy-done((bf16[512,512]{1,0:T(8,128)(2,1)S(1)}, bf16[512,512]{1,0:T(8,128)(2,1)}, u32[]{:S(2)}) %copy-start.3) | copy-done | bytes 524312
  10.3 4.6 %collective-permute-done.halo_ref = bf16[2,64,256]{2,1,0:T(8,128)(2,1)S(1)} collective-permute-done((bf16[2,64,256]{2,1,0:T(8,128)(2,1)S(1)}, bf16[2,64,256]{2,1,0:T(8,128)(2,1)S(1)}, u32[]{:S(2)}, u32[]{:S(2)}) %collective-permute-start) | collective-permute-done | bytes 65568 | tf_op jit(solution)/shard_map/ppermute | solution.py:212
  14.8 1.4 %first_frames.1 = bf16[512,256]{1,0:T(8,128)(2,1)} custom-call(bf16[2,64,512]{2,1,0:T(8,128)(2,1)S(1)} %get-tuple-element.10.volt_ref, bf16[2,64,256]{2,1,0:T(8,128)(2,1)S(1)} %collective-permute-done.halo_ref, f32[4,512]{1,0:T(4,128)S(1)} %get-tuple-element.11.taps_ref, bf16[512,512]{1,0:T(8,128)(2,1)S(1)} %get-tuple-element.12.high_ref, ...), custom_call_target="tpu_custom_call" | custom-call | tf_op jit(solution)/shard_map/first_frames/pallas_call | solution.py:239
  16.2 10.2 %all-to-all-start = ((bf16[64,8,256]{2,1,0:T(8,128)(2,1)}), bf16[64,8,256]{2,1,0:T(8,128)(2,1)S(1)}, u32[]{:S(2)}, u32[]{:S(2)}) async-start(bf16[64,8,256]{2,1,0:T(8,128)(2,1)} %bitcast.2), calls=%async_computation | async-start | bytes 524288 | tf_op jit(solution)/shard_map/all_to_all | solution.py:248
  26.6 13.0 %all-to-all-done.in_ref = bf16[64,8,256]{2,1,0:T(8,128)(2,1)S(1)} async-done(((bf16[64,8,256]{2,1,0:T(8,128)(2,1)}), bf16[64,8,256]{2,1,0:T(8,128)(2,1)S(1)}, u32[]{:S(2)}, u32[]{:S(2)}) %all-to-all-start) | async-done | bytes 262176 | tf_op jit(solution)/shard_map/all_to_all | solution.py:248
  39.6 0.9 %turn.1.a0 = bf16[1024,128]{1,0:T(8,128)(2,1)S(1)} custom-call(s32[2]{0:T(128)S(1)} %pad_add_fusion.place_ref, bf16[64,8,256]{2,1,0:T(8,128)(2,1)S(1)} %all-to-all-done.in_ref), custom_call_target="tpu_custom_call" | custom-call | tf_op jit(solution)/shard_map/turn/pallas_call | solution.py:251
  40.6 4.6 %collective-permute-start.1 = (bf16[1024,128]{1,0:T(8,128)(2,1)S(1)}, bf16[1024,128]{1,0:T(8,128)(2,1)S(1)}, u32[]{:S(2)}, u32[]{:S(2)}) collective-permute-start(bf16[1024,128]{1,0:T(8,128)(2,1)S(1)} %turn.1.a0), channel_id=1, source_target_pairs={{0,1},{1,2},{2,3},{3,4},{4,5},{5,6},{6,7},{7,0},{8,15},{9,8},{10,9... | collective-permute-start | bytes 786440 | tf_op jit(solution)/shard_map/ppermute | solution.py:262
  45.2 2.2 %all-gather = bf16[2048,128]{1,0:T(8,128)(2,1)S(1)} all-gather(bf16[1024,128]{1,0:T(8,128)(2,1)S(1)} %turn.1.a0), channel_id=2, replica_groups=mesh['chan'=32,'row'=2,'col'=8] {'row'}, dimensions={0}, use_global_device_ids=true | all-gather | bytes 786432 | tf_op jit(solution)/shard_map/all_gather | solution.py:263
  47.4 3.6 %collective-permute-start.4 = (bf16[1024,128]{1,0:T(8,128)(2,1)S(1)}, bf16[1024,128]{1,0:T(8,128)(2,1)S(1)}, u32[]{:S(2)}, u32[]{:S(2)}) collective-permute-start(bf16[1024,128]{1,0:T(8,128)(2,1)S(1)} %dynamic-slice_bitcast_fusion.b0), channel_id=1, source_target_pairs={{0,1},{1,2},{2,3},{3,4},{4,5},{5,6},{6,7},{7,0},{8,15},{9,8},{10,9... | collective-permute-start | bytes 786440 | tf_op jit(solution)/shard_map/ppermute | solution.py:262
  51.1 2.4 %collective-permute-start.2 = (bf16[1024,128]{1,0:T(8,128)(2,1)S(1)}, bf16[1024,128]{1,0:T(8,128)(2,1)S(1)}, u32[]{:S(2)}, u32[]{:S(2)}) collective-permute-start(bf16[1024,128]{1,0:T(8,128)(2,1)S(1)} %collective-permute-done.1.a1), channel_id=1, source_target_pairs={{0,1},{1,2},{2,3},{3,4},{4,5},{5,6},{6,7},{7,0},{8,15},{9,8},{10,9... | collective-permute-start | bytes 786440 | tf_op jit(solution)/shard_map/ppermute | solution.py:262
  53.5 1.3 %collective-permute-done.4.b1 = bf16[1024,128]{1,0:T(8,128)(2,1)S(1)} collective-permute-done((bf16[1024,128]{1,0:T(8,128)(2,1)S(1)}, bf16[1024,128]{1,0:T(8,128)(2,1)S(1)}, u32[]{:S(2)}, u32[]{:S(2)}) %collective-permute-start.4) | collective-permute-done | bytes 262176 | tf_op jit(solution)/shard_map/ppermute | solution.py:262
  54.8 4.5 %collective-permute-start.5 = (bf16[1024,128]{1,0:T(8,128)(2,1)S(1)}, bf16[1024,128]{1,0:T(8,128)(2,1)S(1)}, u32[]{:S(2)}, u32[]{:S(2)}) collective-permute-start(bf16[1024,128]{1,0:T(8,128)(2,1)S(1)} %collective-permute-done.4.b1), channel_id=1, source_target_pairs={{0,1},{1,2},{2,3},{3,4},{4,5},{5,6},{6,7},{7,0},{8,15},{9,8},{10,9... | collective-permute-start | bytes 786440 | tf_op jit(solution)/shard_map/ppermute | solution.py:262
  59.4 2.2 %all-gather.1 = bf16[2048,128]{1,0:T(8,128)(2,1)S(1)} all-gather(bf16[1024,128]{1,0:T(8,128)(2,1)S(1)} %broadcast_select_fusion.2), channel_id=3, replica_groups=mesh['chan'=32,'row'=2,'col'=8] {'row'}, dimensions={0}, use_global_device_ids=true | all-gather | bytes 786432 | tf_op jit(solution)/shard_map/all_gather | solution.py:263
  61.6 4.0 %collective-permute-start.3 = (bf16[1024,128]{1,0:T(8,128)(2,1)S(1)}, bf16[1024,128]{1,0:T(8,128)(2,1)S(1)}, u32[]{:S(2)}, u32[]{:S(2)}) collective-permute-start(bf16[1024,128]{1,0:T(8,128)(2,1)S(1)} %collective-permute-done.2.a2), channel_id=1, source_target_pairs={{0,1},{1,2},{2,3},{3,4},{4,5},{5,6},{6,7},{7,0},{8,15},{9,8},{10,9... | collective-permute-start | bytes 786440 | tf_op jit(solution)/shard_map/ppermute | solution.py:262
  65.7 2.0 %collective-permute-start.6 = (bf16[1024,128]{1,0:T(8,128)(2,1)S(1)}, bf16[1024,128]{1,0:T(8,128)(2,1)S(1)}, u32[]{:S(2)}, u32[]{:S(2)}) collective-permute-start(bf16[1024,128]{1,0:T(8,128)(2,1)S(1)} %collective-permute-done.5.b2), channel_id=1, source_target_pairs={{0,1},{1,2},{2,3},{3,4},{4,5},{5,6},{6,7},{7,0},{8,15},{9,8},{10,9... | collective-permute-start | bytes 786440 | tf_op jit(solution)/shard_map/ppermute | solution.py:262
  67.7 2.5 %all-gather.2 = bf16[2048,128]{1,0:T(8,128)(2,1)S(1)} all-gather(bf16[1024,128]{1,0:T(8,128)(2,1)S(1)} %broadcast_select_fusion.1), channel_id=4, replica_groups=mesh['chan'=32,'row'=2,'col'=8] {'row'}, dimensions={0}, use_global_device_ids=true | all-gather | bytes 786432 | tf_op jit(solution)/shard_map/all_gather | solution.py:263
  70.3 4.9 %collective-permute-start.7 = (bf16[1024,128]{1,0:T(8,128)(2,1)S(1)}, bf16[1024,128]{1,0:T(8,128)(2,1)S(1)}, u32[]{:S(2)}, u32[]{:S(2)}) collective-permute-start(bf16[1024,128]{1,0:T(8,128)(2,1)S(1)} %collective-permute-done.3.a3), channel_id=1, source_target_pairs={{0,1},{1,2},{2,3},{3,4},{4,5},{5,6},{6,7},{7,0},{8,15},{9,8},{10,9... | collective-permute-start | bytes 786440 | tf_op jit(solution)/shard_map/ppermute | solution.py:262
  75.2 2.5 %all-gather.4 = bf16[1536,128]{1,0:T(8,128)(2,1)S(1)} all-gather(bf16[768,128]{1,0:T(8,128)(2,1)S(1)} %pad_maximum_fusion), channel_id=6, replica_groups=mesh['chan'=32,'row'=2,'col'=8] {'row'}, dimensions={0}, use_global_device_ids=true | all-gather | bytes 589824 | tf_op jit(solution)/shard_map/all_gather | solution.py:263
  77.7 2.2 %all-gather.3 = bf16[2048,128]{1,0:T(8,128)(2,1)S(1)} all-gather(bf16[1024,128]{1,0:T(8,128)(2,1)S(1)} %broadcast_select_fusion), channel_id=5, replica_groups=mesh['chan'=32,'row'=2,'col'=8] {'row'}, dimensions={0}, use_global_device_ids=true | all-gather | bytes 786432 | tf_op jit(solution)/shard_map/all_gather | solution.py:263
  79.9 2.6 %all-gather.5 = bf16[2048,128]{1,0:T(8,128)(2,1)S(1)} all-gather(bf16[1024,128]{1,0:T(8,128)(2,1)S(1)} %collective-permute-done.7), channel_id=7, replica_groups=mesh['chan'=32,'row'=2,'col'=8] {'row'}, dimensions={0}, use_global_device_ids=true | all-gather | bytes 786432 | tf_op jit(solution)/shard_map/all_gather | solution.py:263
  82.5 3.1 %correlate.1 = bf16[2,2,1024,256]{3,2,1,0:T(8,128)(2,1)} custom-call(s32[2]{0:T(128)S(1)} %pad_add_fusion.place_ref, bf16[1024,128]{1,0:T(8,128)(2,1)S(1)} %turn.1.a0, bf16[1024,128]{1,0:T(8,128)(2,1)S(1)} %collective-permute-done.1.a1, bf16[1024,128]{1,0:T(8,128)(2,1)S(1)} %collective-permute-done.2.a2, bf16[1024,128]{1,0:T(8,128)(2,1)S(1)} %collective-permute-done.3.a3, ...), custom_call_target="tpu_custom_call" | custom-call | tf_op jit(solution)/shard_map/correlate/pallas_call | solution.py:283
  (28 shorter events, 2.7 us)
Async XLA Ops:
  0.8 14.0 %collective-permute-start = (bf16[2,64,256]{2,1,0:T(8,128)(2,1)S(1)}, bf16[2,64,256]{2,1,0:T(8,128)(2,1)S(1)}, u32[]{:S(2)}, u32[]{:S(2)}) collective-permute-start(bf16[2,64,256]{2,1,0:T(8,128)(2,1)S(1)} %slice.3), channel_id=1, source_target_pairs={{0,1},{1,2},{2,3},{3,4},{4,5},{5,6},{6,7},{7,8},{8,9},{9,10},{10,1... | collective-permute-start | bytes 196616 | tf_op jit(solution)/shard_map/ppermute | solution.py:212
  5.7 1.0 %copy-start = (bf16[2,64,1024]{2,1,0:T(8,128)(2,1)S(1)}, bf16[2,64,1024]{2,1,0:T(8,128)(2,1)}, u32[]{:S(2)}) copy-start(bf16[2,64,1024]{2,1,0:T(8,128)(2,1)} %volt_hbm.1) | copy-start | bytes 786436
  6.6 0.7 copy-start.1
  7.3 1.0 %copy-start.2 = (bf16[512,512]{1,0:T(8,128)(2,1)S(1)}, bf16[512,512]{1,0:T(8,128)(2,1)}, u32[]{:S(2)}) copy-start(bf16[512,512]{1,0:T(8,128)(2,1)} %constant.43.clone.rest_hbm) | copy-start | bytes 1572868
  8.3 1.0 %copy-start.3 = (bf16[512,512]{1,0:T(8,128)(2,1)S(1)}, bf16[512,512]{1,0:T(8,128)(2,1)}, u32[]{:S(2)}) copy-start(bf16[512,512]{1,0:T(8,128)(2,1)} %constant.42.clone.high_hbm) | copy-start | bytes 1572868
  16.2 23.4 %all-to-all-start = ((bf16[64,8,256]{2,1,0:T(8,128)(2,1)}), bf16[64,8,256]{2,1,0:T(8,128)(2,1)S(1)}, u32[]{:S(2)}, u32[]{:S(2)}) async-start(bf16[64,8,256]{2,1,0:T(8,128)(2,1)} %bitcast.2), calls=%async_computation | async-start | bytes 524288 | tf_op jit(solution)/shard_map/all_to_all | solution.py:248
  40.6 10.5 %collective-permute-start.1 = (bf16[1024,128]{1,0:T(8,128)(2,1)S(1)}, bf16[1024,128]{1,0:T(8,128)(2,1)S(1)}, u32[]{:S(2)}, u32[]{:S(2)}) collective-permute-start(bf16[1024,128]{1,0:T(8,128)(2,1)S(1)} %turn.1.a0), channel_id=1, source_target_pairs={{0,1},{1,2},{2,3},{3,4},{4,5},{5,6},{6,7},{7,0},{8,15},{9,8},{10,9... | collective-permute-start | bytes 786440 | tf_op jit(solution)/shard_map/ppermute | solution.py:262
  47.4 7.4 %collective-permute-start.4 = (bf16[1024,128]{1,0:T(8,128)(2,1)S(1)}, bf16[1024,128]{1,0:T(8,128)(2,1)S(1)}, u32[]{:S(2)}, u32[]{:S(2)}) collective-permute-start(bf16[1024,128]{1,0:T(8,128)(2,1)S(1)} %dynamic-slice_bitcast_fusion.b0), channel_id=1, source_target_pairs={{0,1},{1,2},{2,3},{3,4},{4,5},{5,6},{6,7},{7,0},{8,15},{9,8},{10,9... | collective-permute-start | bytes 786440 | tf_op jit(solution)/shard_map/ppermute | solution.py:262
  51.1 10.5 %collective-permute-start.2 = (bf16[1024,128]{1,0:T(8,128)(2,1)S(1)}, bf16[1024,128]{1,0:T(8,128)(2,1)S(1)}, u32[]{:S(2)}, u32[]{:S(2)}) collective-permute-start(bf16[1024,128]{1,0:T(8,128)(2,1)S(1)} %collective-permute-done.1.a1), channel_id=1, source_target_pairs={{0,1},{1,2},{2,3},{3,4},{4,5},{5,6},{6,7},{7,0},{8,15},{9,8},{10,9... | collective-permute-start | bytes 786440 | tf_op jit(solution)/shard_map/ppermute | solution.py:262
  54.8 10.9 %collective-permute-start.5 = (bf16[1024,128]{1,0:T(8,128)(2,1)S(1)}, bf16[1024,128]{1,0:T(8,128)(2,1)S(1)}, u32[]{:S(2)}, u32[]{:S(2)}) collective-permute-start(bf16[1024,128]{1,0:T(8,128)(2,1)S(1)} %collective-permute-done.4.b1), channel_id=1, source_target_pairs={{0,1},{1,2},{2,3},{3,4},{4,5},{5,6},{6,7},{7,0},{8,15},{9,8},{10,9... | collective-permute-start | bytes 786440 | tf_op jit(solution)/shard_map/ppermute | solution.py:262
  61.6 8.6 %collective-permute-start.3 = (bf16[1024,128]{1,0:T(8,128)(2,1)S(1)}, bf16[1024,128]{1,0:T(8,128)(2,1)S(1)}, u32[]{:S(2)}, u32[]{:S(2)}) collective-permute-start(bf16[1024,128]{1,0:T(8,128)(2,1)S(1)} %collective-permute-done.2.a2), channel_id=1, source_target_pairs={{0,1},{1,2},{2,3},{3,4},{4,5},{5,6},{6,7},{7,0},{8,15},{9,8},{10,9... | collective-permute-start | bytes 786440 | tf_op jit(solution)/shard_map/ppermute | solution.py:262
  65.7 9.5 %collective-permute-start.6 = (bf16[1024,128]{1,0:T(8,128)(2,1)S(1)}, bf16[1024,128]{1,0:T(8,128)(2,1)S(1)}, u32[]{:S(2)}, u32[]{:S(2)}) collective-permute-start(bf16[1024,128]{1,0:T(8,128)(2,1)S(1)} %collective-permute-done.5.b2), channel_id=1, source_target_pairs={{0,1},{1,2},{2,3},{3,4},{4,5},{5,6},{6,7},{7,0},{8,15},{9,8},{10,9... | collective-permute-start | bytes 786440 | tf_op jit(solution)/shard_map/ppermute | solution.py:262
  70.3 9.6 %collective-permute-start.7 = (bf16[1024,128]{1,0:T(8,128)(2,1)S(1)}, bf16[1024,128]{1,0:T(8,128)(2,1)S(1)}, u32[]{:S(2)}, u32[]{:S(2)}) collective-permute-start(bf16[1024,128]{1,0:T(8,128)(2,1)S(1)} %collective-permute-done.3.a3), channel_id=1, source_target_pairs={{0,1},{1,2},{2,3},{3,4},{4,5},{5,6},{6,7},{7,0},{8,15},{9,8},{10,9... | collective-permute-start | bytes 786440 | tf_op jit(solution)/shard_map/ppermute | solution.py:262

commit v5 on v4

v5 whole, which is shorter than its diff:
```python
import functools
import math

import jax
import jax.numpy as jnp
import numpy as np
from jax import lax
from jax.experimental import pallas as pl
from jax.experimental.pallas import tpu as pltpu
from jax.sharding import PartitionSpec as P

VMEM_LIMIT = 40 * 1024 * 1024
LANES = 128


def interleaved_table(channels, group):
    index = np.arange(channels)
    angle = (index[:, None] * index[None, :] % channels) * (2.0 * math.pi / channels)
    cosine, sine = np.cos(angle), np.sin(angle)
    dft = np.stack([np.stack([cosine, sine], 1), np.stack([-sine, cosine], 1)], 1)
    dft = dft / math.sqrt(channels)
    table = np.einsum("kopn,tu->kotpun", dft, np.eye(group))
    table = table.reshape(channels * 2 * group, 2 * group * channels).astype(np.float32)
    high = table.astype(jnp.bfloat16)
    return high, (table - high.astype(np.float32)).astype(jnp.bfloat16)


def product_nt(a, b):
    return lax.dot_general(a, b, (((1,), (1,)), ((), ())), preferred_element_type=jnp.float32)


def filtered_groups(extended, taps, head, width):
    samples = extended[0].shape[1] - head
    channels = LANES // 2
    parts = []
    for wide in extended:
        rolled = pltpu.roll(wide, channels, 1)
        parts.append(
            taps[0:1, :samples] * wide[:, head:]
            + taps[1:2, :samples] * rolled[:, head:]
            + taps[2:3, :samples] * wide[:, head - LANES : head - LANES + samples]
            + taps[3:4, :samples] * rolled[:, head - LANES : head - LANES + samples]
        )
    rows = [
        jnp.concatenate([p[:, start : start + width] for p in parts], 1) for start in range(0, samples, width)
    ]
    return jnp.concatenate(rows, 0)


def transformed(frames, high, rest):
    frames_high = frames.astype(jnp.bfloat16)
    frames_rest = (frames - frames_high.astype(jnp.float32)).astype(jnp.bfloat16)
    spectra = product_nt(high, frames_rest) + product_nt(rest, frames_high)
    return (spectra + product_nt(high, frames_high)).astype(jnp.bfloat16)


def later_kernel(volt_hbm, taps_hbm, table_hbm, volt_out, taps_out, table_out, late_out, volt_ref, taps_ref, sems):
    copies = [
        pltpu.make_async_copy(source, target, sems.at[i])
        for i, (source, target) in enumerate(
            ((volt_hbm, volt_ref), (taps_hbm, taps_ref), (table_hbm, table_out))
        )
    ]
    for copy in copies:
        copy.start()
    copies[0].wait()
    copies[1].wait()
    samples = volt_ref.shape[2]
    width = table_out.shape[2] // 2
    wide = jnp.concatenate([taps_ref[...]] * (LANES // taps_ref.shape[1]), 1)
    taps = jnp.concatenate([wide] * (samples // LANES), 1)
    taps_out[...] = taps[:, :width]
    volt_out[...] = volt_ref[:, :, :width]
    extended = [volt_ref[part].astype(jnp.float32) for part in range(2)]
    frames = filtered_groups(extended, taps, width, width)
    first = jnp.zeros((volt_ref.shape[1], frames.shape[1]), jnp.float32)
    copies[2].wait()
    late_out[...] = transformed(jnp.concatenate([first, frames], 0), table_out[0], table_out[1])


def first_kernel(volt_ref, halo_ref, taps_ref, table_ref, late_ref, out_ref):
    extended = [
        jnp.concatenate([halo_ref[part], volt_ref[part]], 1).astype(jnp.float32) for part in range(2)
    ]
    frames = filtered_groups(extended, taps_ref[...], halo_ref.shape[2], table_ref.shape[2] // 2)
    frames = jnp.concatenate([frames, jnp.zeros((LANES - frames.shape[0], frames.shape[1]), jnp.float32)], 0)
    first = transformed(frames, table_ref[0], table_ref[1])
    out_ref[:, :LANES] = first + late_ref[:, :LANES]
    out_ref[:, LANES:] = late_ref[:, LANES:]


def turn_kernel(in_ref, *out_refs):
    row, odd = lax.axis_index("row"), lax.axis_index("col") % 2 == 1
    pairs = in_ref.shape[1] // 4
    half_lanes = LANES // 2
    low = lax.broadcasted_iota(jnp.int32, (8, LANES), 1) < half_lanes
    for half, out_ref in zip((row, 1 - row), out_refs):
        for pair in range(pairs):
            first = [in_ref[r, half * 2 * pairs + 2 * pair].astype(jnp.float32) for r in range(2)]
            second = [in_ref[r, half * 2 * pairs + 2 * pair + 1].astype(jnp.float32) for r in range(2)]
            pieces = []
            for ch in range(2):
                for g in range(4):
                    for r in range(2):
                        tile = (slice(ch * 8, ch * 8 + 8), slice((g // 2) * LANES, (g // 2 + 1) * LANES))
                        a, b = first[r][tile], second[r][tile]
                        if g % 2 == 0:
                            pieces.append(jnp.where(low, a, pltpu.roll(b, half_lanes, 1)))
                        else:
                            pieces.append(jnp.where(low, pltpu.roll(a, half_lanes, 1), b))
            count = len(pieces) // 2
            block = jnp.concatenate(
                [jnp.where(odd, pieces[(i + count) % (2 * count)], pieces[i]) for i in range(2 * count)], 0
            )
            out_ref[pl.ds(pair * LANES, LANES), :] = block.T.astype(jnp.bfloat16)


def by_channel(one, other):
    low = lax.broadcasted_iota(jnp.int32, one.shape, 1) < LANES // 2
    return jnp.where(low, one, other), jnp.where(low, other, one)


def correlate_kernel(
    scale, tile_rows, k0, k1, k2, k3, k4, g0, g1, g2, g3, s1, s2, s3, far, c4, out_hbm, out_ref, right_ref, sems
):
    row, col = lax.axis_index("row"), lax.axis_index("col")
    away = 1 - row
    cols = out_ref.shape[3]
    half_rows = k0.shape[0]
    per_half = half_rows // cols
    odd = col % 2 == 1
    lefts = [
        (lambda at: k0[at, :]),
        (lambda at: k1[at, :]),
        (lambda at: k2[at, :]),
        (lambda at: k3[at, :]),
        (lambda at: s2[away, at, :]),
        (lambda at: s1[away, at, :]),
        (lambda at: k4[at, :]),
        (lambda at: s3[away, at, :]),
    ]

    at = pl.ds(pl.multiple_of((col % per_half) * cols, cols), cols)
    elsewhere = (row == 0) & (col >= per_half)
    others = [
        (lambda: g0[at, :]),
        (lambda: g1[at, :]),
        (lambda: g2[at, :]),
        (lambda: g3[at, :]),
        (lambda: far[away, cols : 2 * cols, :]),
        (lambda: far[away, 0:cols, :]),
        (lambda: c4[away]),
        (lambda: far[away, 2 * cols : 3 * cols, :]),
    ]
    target = lax.broadcasted_iota(jnp.int32, (LANES, LANES), 0)
    source = lax.broadcasted_iota(jnp.int32, (LANES, LANES), 1)
    same = (source == target).astype(jnp.bfloat16)
    turn = jnp.where(target == source + 4, 1.0, 0.0) * (source % 8 < 4).astype(jnp.float32)
    turn = turn - jnp.where(target == source - 4, 1.0, 0.0) * (source % 8 >= 4).astype(jnp.float32)
    turn = turn.astype(jnp.bfloat16)
    blocks = [jnp.where(elsewhere, other(), own(at)) for own, other in zip(lefts, others)]
    for pair in range(4):
        lanes = slice(pair * LANES, (pair + 1) * LANES)
        for ch, block in enumerate(by_channel(blocks[2 * pair], blocks[2 * pair + 1])):
            right_ref[ch, lanes, 0:cols] = product_nt(same, block).astype(jnp.bfloat16)
            right_ref[ch, lanes, cols : 2 * cols] = product_nt(turn, block).astype(jnp.bfloat16)

    copies = []
    for start in range(0, half_rows, tile_rows):
        here = slice(start, start + tile_rows)
        channels = ([], [])
        for pair in range(4):
            for ch, block in enumerate(by_channel(lefts[2 * pair](here), lefts[2 * pair + 1](here))):
                channels[ch].append(block)
        row_ids = row * half_rows + start + lax.broadcasted_iota(jnp.int32, (tile_rows, cols), 0)
        col_ids = col * cols + lax.broadcasted_iota(jnp.int32, (tile_rows, cols), 1)
        upper = row_ids < col_ids
        for ch in range(2):
            left = jnp.concatenate(channels[ch], 1)
            total = jnp.dot(left, right_ref[ch], preferred_element_type=jnp.float32) * scale
            goes_to = jnp.where(odd, 1 - ch, ch)
            out_ref[0, goes_to, here, :] = jnp.where(upper, total[:, :cols], 0.0).astype(jnp.bfloat16)
            out_ref[1, goes_to, here, :] = jnp.where(upper, total[:, cols:], 0.0).astype(jnp.bfloat16)
        copies.append(
            pltpu.make_async_copy(out_ref.at[:, :, here, :], out_hbm.at[:, :, here, :], sems.at[len(copies)])
        )
        copies[-1].start()
    for copy in copies:
        copy.wait()


def shards(voltages, fir_taps):
    inputs_loc, samples = voltages.shape[1:]
    channels = fir_taps.shape[1]
    group = 4
    chan_size, row_size, col_size = (lax.axis_size(a) for a in ("chan", "row", "col"))
    row, col = lax.axis_index("row"), lax.axis_index("col")
    devices = row_size * col_size
    params = pltpu.CompilerParams(vmem_limit_bytes=VMEM_LIMIT)
    whole = pl.BlockSpec(memory_space=pltpu.VMEM)

    halo = lax.ppermute(
        voltages[:, :, samples - group * channels :],
        ("row", "col"),
        [(i, i + 1) for i in range(devices - 1)],
    )
    table = np.stack(interleaved_table(channels, group))
    frames_loc = samples // channels
    spectra_shape = (channels * 2 * group, frames_loc // group * inputs_loc)
    in_hbm = pl.BlockSpec(memory_space=pltpu.HBM)
    volt_early, taps, table, late = pl.pallas_call(
        later_kernel,
        out_shape=[
            jax.ShapeDtypeStruct((2, inputs_loc, group * channels), jnp.bfloat16),
            jax.ShapeDtypeStruct((fir_taps.shape[0], group * channels), jnp.float32),
            jax.ShapeDtypeStruct(table.shape, jnp.bfloat16),
            jax.ShapeDtypeStruct(spectra_shape, jnp.bfloat16),
        ],
        in_specs=[in_hbm] * 3,
        out_specs=[whole] * 4,
        scratch_shapes=[
            pltpu.VMEM(voltages.shape, jnp.bfloat16),
            pltpu.VMEM(fir_taps.shape, jnp.float32),
            pltpu.SemaphoreType.DMA((3,)),
        ],
        cost_estimate=pl.CostEstimate(flops=500_000_000, bytes_accessed=3_000_000, transcendentals=0),
        compiler_params=params,
        name="later_frames",
    )(voltages, fir_taps, jnp.asarray(table))
    spectra = pl.pallas_call(
        first_kernel,
        out_shape=jax.ShapeDtypeStruct(spectra_shape, jnp.bfloat16),
        in_specs=[whole] * 5,
        out_specs=whole,
        compiler_params=params,
        name="first_frames",
    )(volt_early, halo, taps, table, late)
    spectra = spectra.reshape(chan_size, -1, spectra.shape[1])
    turned = lax.all_to_all(spectra, "chan", split_axis=0, concat_axis=0, tiled=True)
    both = lax.all_gather(turned, "row", axis=0)

    half = chan_size * inputs_loc // row_size
    keep, give = pl.pallas_call(
        turn_kernel,
        out_shape=[jax.ShapeDtypeStruct((half, LANES), jnp.bfloat16)] * 2,
        in_specs=[whole],
        out_specs=[whole] * 2,
        compiler_params=params,
        name="turn",
    )(both)

    ahead = [(c, (c + 1) % col_size) for c in range(col_size)]
    behind = [(col_size + c, col_size + (c - 1) % col_size) for c in range(col_size)]
    on_ring = lambda array: lax.ppermute(array, ("row", "col"), ahead + behind)
    on_chip = lambda array: lax.all_gather(array, "row", axis=0)

    cols = chan_size * inputs_loc // col_size
    col_offset = lax.rem(col, half // cols) * cols
    col_part = lambda array: lax.dynamic_slice_in_dim(array, col_offset, cols, 0)
    keeps, gives = [keep], [give]
    for step in range(col_size // 2 - 1):
        keeps.append(on_ring(keeps[-1]))
        gives.append(on_ring(gives[-1]))
    keeps.append(on_ring(keeps[-1]))
    shared = [on_chip(g) for g in gives[1:]]
    far = on_chip(jnp.concatenate([col_part(k) for k in keeps[1:-1]], 0))
    last_cols = on_chip(col_part(keeps[-1]))

    tile = 256
    operands = [*keeps, *gives, *shared, far, last_cols]
    out_shape = (2, 2, half, cols)
    return pl.pallas_call(
        functools.partial(correlate_kernel, 1.0 / math.sqrt(frames_loc * devices), tile),
        out_shape=jax.ShapeDtypeStruct(out_shape, jnp.bfloat16),
        in_specs=[whole] * len(operands),
        out_specs=pl.BlockSpec(memory_space=pl.ANY),
        scratch_shapes=[
            pltpu.VMEM(out_shape, jnp.bfloat16),
            pltpu.VMEM((2, 4 * LANES, 2 * cols), jnp.bfloat16),
            pltpu.SemaphoreType.DMA((half // tile,)),
        ],
        compiler_params=params,
        name="correlate",
    )(*operands)


def solution(mesh):
    placed = (P(None, "chan", ("row", "col")), P())
    return jax.shard_map(
        shards, mesh=mesh, in_specs=placed, out_specs=P(None, "chan", "row", "col"), check_vma=False
    )
```

time: 86.1 us -> 82 us (0.952)
  blocking collectives: 14.1 us -> 36.3 us
  waiting for transfers between devices: 18.9 us -> 5.37 us
  starting transfers between devices: 41.1 us -> 31.3 us
  Pallas kernels: 6.25 us -> 4.59 us
    all_to_all x0 -> x1, blocking collectives: none -> 20.1 us  [shards(): lax.all_to_all(spectra, 'chan', split_axis=0, concat_axis=0, tiled=True)]
    all_to_all x1 -> x0, waiting for transfers between devices: 13 us -> none  [shards(): lax.all_to_all(spectra, ('chan', 'row'), split_axis=0, concat_axis=0, til...]
    all_to_all x1 -> x0, starting transfers between devices: 10.2 us -> none  [shards(): lax.all_to_all(spectra, ('chan', 'row'), split_axis=0, concat_axis=0, til...]
    all_gather x0 -> x1, blocking collectives: none -> 2.17 us  [shards(): both = lax.all_gather(turned, 'row', axis=0)]
    ppermute x7, waiting for transfers between devices: 1.31 us -> 0.02 us  [shards(): on_ring = lambda array: lax.ppermute(array, ('row', 'col'), ahead + behind)]
    unnamed x8 -> x6, local copies, waits for them, and re-layouts: 3.71 us -> 2.85 us
    all_gather x6 -> x5, blocking collectives: 14.1 us -> 14 us  [shards(): on_chip = lambda array: lax.all_gather(array, 'row', axis=0)]
  transfers between devices with their start and end apart: 9 -> 8, of which waited for: 3 -> 1; matrix products, arithmetic and copies ran while one was open for 0% -> 0% of each run, Pallas kernels for 1% -> 1%
where the time goes in v5:
time: 82 us; the launch traced here: 81.5 us
  blocking collectives  36.3 us (44%)
  starting transfers between devices  31.3 us (38%)
  waiting for transfers between devices  5.37 us (7%)
  Pallas kernels  4.59 us (6%)
  local copies, waits for them, and re-layouts  3.73 us (5%)
    ppermute x7, starting transfers between devices, shards(): on_ring = lambda array: lax.ppermute(array, ('row', 'col'), ahead + behind)  26.5 us
    all_to_all x1, blocking collectives, shards(): lax.all_to_all(spectra, 'chan', split_axis=0, concat_axis=0, tiled=True)  20.1 us
    all_gather x5, blocking collectives, shards(): on_chip = lambda array: lax.all_gather(array, 'row', axis=0)  14 us
    ppermute x1, waiting for transfers between devices, shards(): lax.ppermute(voltages[:, :, samples - group * channels:], ('row', 'col'),...  5.35 us
    ppermute x1, starting transfers between devices, shards(): lax.ppermute(voltages[:, :, samples - group * channels:], ('row', 'col'),...  4.82 us
    unnamed x6, local copies, waits for them, and re-layouts  2.85 us
    pallas_call x1, Pallas kernels, shards(): pl.pallas_call(functools.partial(correlate_kernel, 1.0 / math.sqrt(frames...  2.43 us
    all_gather x1, blocking collectives, shards(): both = lax.all_gather(turned, 'row', axis=0)  2.17 us
  transfers between devices with their start and end apart: 8, of which 1 were waited for; matrix products, arithmetic and copies ran while one was open for 0% of the time, Pallas kernels for 1%

profile of v5, /device:TPU:1, one launch (start us, length us, event | category | flops | bytes accessed | tf_op | source)
XLA Modules:
  0.0 81.5 jit_solution(1355533449998051162)
XLA Ops:
  0.0 0.8 %slice.3 = bf16[2,64,256]{2,1,0:T(8,128)(2,1)S(1)} slice(bf16[2,64,1024]{2,1,0:T(8,128)(2,1)} %volt_hbm.1), slice={[0:2], [0:64], [768:1024]} | slice | bytes 131072 | tf_op jit(solution)/shard_map/slice | solution.py:203
  0.8 4.8 %collective-permute-start = (bf16[2,64,256]{2,1,0:T(8,128)(2,1)S(1)}, bf16[2,64,256]{2,1,0:T(8,128)(2,1)S(1)}, u32[]{:S(2)}, u32[]{:S(2)}) collective-permute-start(bf16[2,64,256]{2,1,0:T(8,128)(2,1)S(1)} %slice.3), channel_id=1, source_target_pairs={{0,1},{1,2},{2,3},{3,4},{4,5},{5,6},{6,7},{7,8},{8,9},{9,10},{10,1... | collective-permute-start | bytes 196616 | tf_op jit(solution)/shard_map/ppermute | solution.py:202
  5.7 0.9 %copy-done = bf16[2,64,1024]{2,1,0:T(8,128)(2,1)S(1)} copy-done((bf16[2,64,1024]{2,1,0:T(8,128)(2,1)S(1)}, bf16[2,64,1024]{2,1,0:T(8,128)(2,1)}, u32[]{:S(2)}) %copy-start) | copy-done | bytes 262168
  6.6 0.7 copy-done.1
  7.3 1.2 %copy-done.2 = bf16[2,512,512]{2,1,0:T(8,128)(2,1)S(1)} copy-done((bf16[2,512,512]{2,1,0:T(8,128)(2,1)S(1)}, bf16[2,512,512]{2,1,0:T(8,128)(2,1)}, u32[]{:S(2)}) %copy-start.2) | copy-done | bytes 1048600
  8.5 0.9 %later_frames.1 = (bf16[2,64,256]{2,1,0:T(8,128)(2,1)S(1)}, f32[4,256]{1,0:T(4,128)S(1)}, bf16[2,512,512]{2,1,0:T(8,128)(2,1)S(1)}, bf16[512,256]{1,0:T(8,128)(2,1)S(1)}) custom-call(bf16[2,64,1024]{2,1,0:T(8,128)(2,1)S(1)} %copy-done, f32[4,64]{1,0:T(4,128)S(1)} %copy-done.1, bf16[2,512,512]{2,1,0:T(8,128)(2,1)S(1)} %copy-done.2), custom_call_target="tpu_custom_call" | custom-call | flops 500000000 | bytes 3000000 | tf_op jit(solution)/shard_map/later_frames/pallas_call | solution.py:211
  9.5 5.4 %collective-permute-done.halo_ref = bf16[2,64,256]{2,1,0:T(8,128)(2,1)S(1)} collective-permute-done((bf16[2,64,256]{2,1,0:T(8,128)(2,1)S(1)}, bf16[2,64,256]{2,1,0:T(8,128)(2,1)S(1)}, u32[]{:S(2)}, u32[]{:S(2)}) %collective-permute-start) | collective-permute-done | bytes 65568 | tf_op jit(solution)/shard_map/ppermute | solution.py:202
  14.8 0.7 first_frames.1
  15.5 20.1 %all_to_all.5 = bf16[32,16,256]{2,1,0:T(8,128)(2,1)S(1)} all-to-all(bf16[32,16,256]{2,1,0:T(8,128)(2,1)S(1)} %bitcast.12), channel_id=1, replica_groups=mesh['chan'=32,'row'=2,'col'=8] {'chan'}, dimensions={0} | all-to-all | bytes 524288 | tf_op jit(solution)/shard_map/all_to_all | solution.py:239
  35.6 2.2 %all-gather = bf16[64,16,256]{2,1,0:T(8,128)(2,1)S(1)} all-gather(bf16[32,16,256]{2,1,0:T(8,128)(2,1)S(1)} %all_to_all.5), channel_id=2, replica_groups=mesh['chan'=32,'row'=2,'col'=8] {'row'}, dimensions={0}, use_global_device_ids=true | all-gather | bytes 786432 | tf_op jit(solution)/shard_map/all_gather | solution.py:240
  37.8 0.6 turn.1
  38.4 5.7 %collective-permute-start.1 = (bf16[1024,128]{1,0:T(8,128)(2,1)S(1)}, bf16[1024,128]{1,0:T(8,128)(2,1)S(1)}, u32[]{:S(2)}, u32[]{:S(2)}) collective-permute-start(bf16[1024,128]{1,0:T(8,128)(2,1)S(1)} %get-tuple-element.15.k0), channel_id=1, source_target_pairs={{0,1},{1,2},{2,3},{3,4},{4,5},{5,6},{6,7},{7,0},{8,15},{9,8},{10,9... | collective-permute-start | bytes 786440 | tf_op jit(solution)/shard_map/ppermute | solution.py:254
  44.1 3.6 %collective-permute-start.5 = (bf16[1024,128]{1,0:T(8,128)(2,1)S(1)}, bf16[1024,128]{1,0:T(8,128)(2,1)S(1)}, u32[]{:S(2)}, u32[]{:S(2)}) collective-permute-start(bf16[1024,128]{1,0:T(8,128)(2,1)S(1)} %get-tuple-element.16.g0), channel_id=1, source_target_pairs={{0,1},{1,2},{2,3},{3,4},{4,5},{5,6},{6,7},{7,0},{8,15},{9,8},{10,9... | collective-permute-start | bytes 786440 | tf_op jit(solution)/shard_map/ppermute | solution.py:254
  47.8 4.7 %collective-permute-start.2 = (bf16[1024,128]{1,0:T(8,128)(2,1)S(1)}, bf16[1024,128]{1,0:T(8,128)(2,1)S(1)}, u32[]{:S(2)}, u32[]{:S(2)}) collective-permute-start(bf16[1024,128]{1,0:T(8,128)(2,1)S(1)} %collective-permute-done.1.k1), channel_id=1, source_target_pairs={{0,1},{1,2},{2,3},{3,4},{4,5},{5,6},{6,7},{7,0},{8,15},{9,8},{10,9... | collective-permute-start | bytes 786440 | tf_op jit(solution)/shard_map/ppermute | solution.py:254
  52.4 3.6 %collective-permute-start.6 = (bf16[1024,128]{1,0:T(8,128)(2,1)S(1)}, bf16[1024,128]{1,0:T(8,128)(2,1)S(1)}, u32[]{:S(2)}, u32[]{:S(2)}) collective-permute-start(bf16[1024,128]{1,0:T(8,128)(2,1)S(1)} %collective-permute-done.5.g1), channel_id=1, source_target_pairs={{0,1},{1,2},{2,3},{3,4},{4,5},{5,6},{6,7},{7,0},{8,15},{9,8},{10,9... | collective-permute-start | bytes 786440 | tf_op jit(solution)/shard_map/ppermute | solution.py:254
  56.1 2.2 %all-gather.1 = bf16[2048,128]{1,0:T(8,128)(2,1)S(1)} all-gather(bf16[1024,128]{1,0:T(8,128)(2,1)S(1)} %collective-permute-done.5.g1), channel_id=3, replica_groups=mesh['chan'=32,'row'=2,'col'=8] {'row'}, dimensions={0}, use_global_device_ids=true | all-gather | bytes 786432 | tf_op jit(solution)/shard_map/all_gather | solution.py:255
  58.3 2.5 %collective-permute-start.3 = (bf16[1024,128]{1,0:T(8,128)(2,1)S(1)}, bf16[1024,128]{1,0:T(8,128)(2,1)S(1)}, u32[]{:S(2)}, u32[]{:S(2)}) collective-permute-start(bf16[1024,128]{1,0:T(8,128)(2,1)S(1)} %collective-permute-done.2.k2), channel_id=1, source_target_pairs={{0,1},{1,2},{2,3},{3,4},{4,5},{5,6},{6,7},{7,0},{8,15},{9,8},{10,9... | collective-permute-start | bytes 786440 | tf_op jit(solution)/shard_map/ppermute | solution.py:254
  60.8 3.6 %collective-permute-start.7 = (bf16[1024,128]{1,0:T(8,128)(2,1)S(1)}, bf16[1024,128]{1,0:T(8,128)(2,1)S(1)}, u32[]{:S(2)}, u32[]{:S(2)}) collective-permute-start(bf16[1024,128]{1,0:T(8,128)(2,1)S(1)} %collective-permute-done.6.g2), channel_id=1, source_target_pairs={{0,1},{1,2},{2,3},{3,4},{4,5},{5,6},{6,7},{7,0},{8,15},{9,8},{10,9... | collective-permute-start | bytes 786440 | tf_op jit(solution)/shard_map/ppermute | solution.py:254
  64.4 2.8 %all-gather.2 = bf16[2048,128]{1,0:T(8,128)(2,1)S(1)} all-gather(bf16[1024,128]{1,0:T(8,128)(2,1)S(1)} %collective-permute-done.6.g2), channel_id=4, replica_groups=mesh['chan'=32,'row'=2,'col'=8] {'row'}, dimensions={0}, use_global_device_ids=true | all-gather | bytes 786432 | tf_op jit(solution)/shard_map/all_gather | solution.py:255
  67.2 2.8 %collective-permute-start.4 = (bf16[1024,128]{1,0:T(8,128)(2,1)S(1)}, bf16[1024,128]{1,0:T(8,128)(2,1)S(1)}, u32[]{:S(2)}, u32[]{:S(2)}) collective-permute-start(bf16[1024,128]{1,0:T(8,128)(2,1)S(1)} %collective-permute-done.3.k3), channel_id=1, source_target_pairs={{0,1},{1,2},{2,3},{3,4},{4,5},{5,6},{6,7},{7,0},{8,15},{9,8},{10,9... | collective-permute-start | bytes 786440 | tf_op jit(solution)/shard_map/ppermute | solution.py:254
  70.0 2.6 %all-gather.4 = bf16[1536,128]{1,0:T(8,128)(2,1)S(1)} all-gather(bf16[768,128]{1,0:T(8,128)(2,1)S(1)} %pad_maximum_fusion), channel_id=6, replica_groups=mesh['chan'=32,'row'=2,'col'=8] {'row'}, dimensions={0}, use_global_device_ids=true | all-gather | bytes 589824 | tf_op jit(solution)/shard_map/all_gather | solution.py:255
  72.7 2.2 %all-gather.3 = bf16[2048,128]{1,0:T(8,128)(2,1)S(1)} all-gather(bf16[1024,128]{1,0:T(8,128)(2,1)S(1)} %collective-permute-done.7.g3), channel_id=5, replica_groups=mesh['chan'=32,'row'=2,'col'=8] {'row'}, dimensions={0}, use_global_device_ids=true | all-gather | bytes 786432 | tf_op jit(solution)/shard_map/all_gather | solution.py:255
  74.9 4.2 %all-gather.5 = bf16[512,128]{1,0:T(8,128)(2,1)S(1)} all-gather(bf16[256,128]{1,0:T(8,128)(2,1)S(1)} %constant_dynamic-slice_fusion), channel_id=7, replica_groups=mesh['chan'=32,'row'=2,'col'=8] {'row'}, dimensions={0}, use_global_device_ids=true | all-gather | bytes 196608 | tf_op jit(solution)/shard_map/all_gather | solution.py:255
  79.1 2.4 %correlate.1 = bf16[2,2,1024,256]{3,2,1,0:T(8,128)(2,1)} custom-call(bf16[1024,128]{1,0:T(8,128)(2,1)S(1)} %get-tuple-element.15.k0, bf16[1024,128]{1,0:T(8,128)(2,1)S(1)} %collective-permute-done.1.k1, bf16[1024,128]{1,0:T(8,128)(2,1)S(1)} %collective-permute-done.2.k2, bf16[1024,128]{1,0:T(8,128)(2,1)S(1)} %collective-permute-done.3.k3, ...), custom_call_target="tpu_custom_call" | custom-call | tf_op jit(solution)/shard_map/correlate/pallas_call | solution.py:272
  (15 shorter events, 0.1 us)
Async XLA Ops:
  0.8 14.0 %collective-permute-start = (bf16[2,64,256]{2,1,0:T(8,128)(2,1)S(1)}, bf16[2,64,256]{2,1,0:T(8,128)(2,1)S(1)}, u32[]{:S(2)}, u32[]{:S(2)}) collective-permute-start(bf16[2,64,256]{2,1,0:T(8,128)(2,1)S(1)} %slice.3), channel_id=1, source_target_pairs={{0,1},{1,2},{2,3},{3,4},{4,5},{5,6},{6,7},{7,8},{8,9},{9,10},{10,1... | collective-permute-start | bytes 196616 | tf_op jit(solution)/shard_map/ppermute | solution.py:202
  5.7 1.0 %copy-start = (bf16[2,64,1024]{2,1,0:T(8,128)(2,1)S(1)}, bf16[2,64,1024]{2,1,0:T(8,128)(2,1)}, u32[]{:S(2)}) copy-start(bf16[2,64,1024]{2,1,0:T(8,128)(2,1)} %volt_hbm.1) | copy-start | bytes 786436
  6.6 0.7 copy-start.1
  7.3 1.2 %copy-start.2 = (bf16[2,512,512]{2,1,0:T(8,128)(2,1)S(1)}, bf16[2,512,512]{2,1,0:T(8,128)(2,1)}, u32[]{:S(2)}) copy-start(bf16[2,512,512]{2,1,0:T(8,128)(2,1)} %constant.16.clone.table_hbm) | copy-start | bytes 3145732
  38.4 9.4 %collective-permute-start.1 = (bf16[1024,128]{1,0:T(8,128)(2,1)S(1)}, bf16[1024,128]{1,0:T(8,128)(2,1)S(1)}, u32[]{:S(2)}, u32[]{:S(2)}) collective-permute-start(bf16[1024,128]{1,0:T(8,128)(2,1)S(1)} %get-tuple-element.15.k0), channel_id=1, source_target_pairs={{0,1},{1,2},{2,3},{3,4},{4,5},{5,6},{6,7},{7,0},{8,15},{9,8},{10,9... | collective-permute-start | bytes 786440 | tf_op jit(solution)/shard_map/ppermute | solution.py:254
  44.1 8.3 %collective-permute-start.5 = (bf16[1024,128]{1,0:T(8,128)(2,1)S(1)}, bf16[1024,128]{1,0:T(8,128)(2,1)S(1)}, u32[]{:S(2)}, u32[]{:S(2)}) collective-permute-start(bf16[1024,128]{1,0:T(8,128)(2,1)S(1)} %get-tuple-element.16.g0), channel_id=1, source_target_pairs={{0,1},{1,2},{2,3},{3,4},{4,5},{5,6},{6,7},{7,0},{8,15},{9,8},{10,9... | collective-permute-start | bytes 786440 | tf_op jit(solution)/shard_map/ppermute | solution.py:254
  47.8 10.5 %collective-permute-start.2 = (bf16[1024,128]{1,0:T(8,128)(2,1)S(1)}, bf16[1024,128]{1,0:T(8,128)(2,1)S(1)}, u32[]{:S(2)}, u32[]{:S(2)}) collective-permute-start(bf16[1024,128]{1,0:T(8,128)(2,1)S(1)} %collective-permute-done.1.k1), channel_id=1, source_target_pairs={{0,1},{1,2},{2,3},{3,4},{4,5},{5,6},{6,7},{7,0},{8,15},{9,8},{10,9... | collective-permute-start | bytes 786440 | tf_op jit(solution)/shard_map/ppermute | solution.py:254
  52.4 8.3 %collective-permute-start.6 = (bf16[1024,128]{1,0:T(8,128)(2,1)S(1)}, bf16[1024,128]{1,0:T(8,128)(2,1)S(1)}, u32[]{:S(2)}, u32[]{:S(2)}) collective-permute-start(bf16[1024,128]{1,0:T(8,128)(2,1)S(1)} %collective-permute-done.5.g1), channel_id=1, source_target_pairs={{0,1},{1,2},{2,3},{3,4},{4,5},{5,6},{6,7},{7,0},{8,15},{9,8},{10,9... | collective-permute-start | bytes 786440 | tf_op jit(solution)/shard_map/ppermute | solution.py:254
  58.3 9.0 %collective-permute-start.3 = (bf16[1024,128]{1,0:T(8,128)(2,1)S(1)}, bf16[1024,128]{1,0:T(8,128)(2,1)S(1)}, u32[]{:S(2)}, u32[]{:S(2)}) collective-permute-start(bf16[1024,128]{1,0:T(8,128)(2,1)S(1)} %collective-permute-done.2.k2), channel_id=1, source_target_pairs={{0,1},{1,2},{2,3},{3,4},{4,5},{5,6},{6,7},{7,0},{8,15},{9,8},{10,9... | collective-permute-start | bytes 786440 | tf_op jit(solution)/shard_map/ppermute | solution.py:254
  60.8 11.9 %collective-permute-start.7 = (bf16[1024,128]{1,0:T(8,128)(2,1)S(1)}, bf16[1024,128]{1,0:T(8,128)(2,1)S(1)}, u32[]{:S(2)}, u32[]{:S(2)}) collective-permute-start(bf16[1024,128]{1,0:T(8,128)(2,1)S(1)} %collective-permute-done.6.g2), channel_id=1, source_target_pairs={{0,1},{1,2},{2,3},{3,4},{4,5},{5,6},{6,7},{7,0},{8,15},{9,8},{10,9... | collective-permute-start | bytes 786440 | tf_op jit(solution)/shard_map/ppermute | solution.py:254
  67.2 7.6 %collective-permute-start.4 = (bf16[1024,128]{1,0:T(8,128)(2,1)S(1)}, bf16[1024,128]{1,0:T(8,128)(2,1)S(1)}, u32[]{:S(2)}, u32[]{:S(2)}) collective-permute-start(bf16[1024,128]{1,0:T(8,128)(2,1)S(1)} %collective-permute-done.3.k3), channel_id=1, source_target_pairs={{0,1},{1,2},{2,3},{3,4},{4,5},{5,6},{6,7},{7,0},{8,15},{9,8},{10,9... | collective-permute-start | bytes 786440 | tf_op jit(solution)/shard_map/ppermute | solution.py:254

commit v6 on v5

--- a/solution.py
+++ b/solution.py
@@ -11,6 +11,7 @@
 
 VMEM_LIMIT = 40 * 1024 * 1024
 LANES = 128
+NEAR_FLOPS = 4_000_000_000
 
 
 def interleaved_table(channels, group):
@@ -120,14 +121,41 @@
     return jnp.where(low, one, other), jnp.where(low, other, one)
 
 
+def place_of_columns(cols, half_rows):
+    row, col = lax.axis_index("row"), lax.axis_index("col")
+    per_half = half_rows // cols
+    at = pl.ds(pl.multiple_of((col % per_half) * cols, cols), cols)
+    return row, col, at, (row == 0) & (col >= per_half)
+
+
+def put_columns(one, other, right_ref, first_lane):
+    cols = one.shape[0]
+    target = lax.broadcasted_iota(jnp.int32, (LANES, LANES), 0)
+    source = lax.broadcasted_iota(jnp.int32, (LANES, LANES), 1)
+    same = (source == target).astype(jnp.bfloat16)
+    turn = jnp.where(target == source + 4, 1.0, 0.0) * (source % 8 < 4).astype(jnp.float32)
+    turn = turn - jnp.where(target == source - 4, 1.0, 0.0) * (source % 8 >= 4).astype(jnp.float32)
+    turn = turn.astype(jnp.bfloat16)
+    lanes = slice(first_lane, first_lane + LANES)
+    for ch, block in enumerate(by_channel(one, other)):
+        right_ref[ch, lanes, 0:cols] = product_nt(same, block).astype(jnp.bfloat16)
+        right_ref[ch, lanes, cols : 2 * cols] = product_nt(turn, block).astype(jnp.bfloat16)
+
+
+def near_columns_kernel(k0, k1, k2, k3, g0, g1, g2, g3, right_ref):
+    _, _, at, elsewhere = place_of_columns(right_ref.shape[2] // 2, k0.shape[0])
+    near = [jnp.where(elsewhere, g[at, :], k[at, :]) for k, g in ((k0, g0), (k1, g1), (k2, g2), (k3, g3))]
+    put_columns(near[0], near[1], right_ref, 0)
+    put_columns(near[2], near[3], right_ref, LANES)
+
+
 def correlate_kernel(
-    scale, tile_rows, k0, k1, k2, k3, k4, g0, g1, g2, g3, s1, s2, s3, far, c4, out_hbm, out_ref, right_ref, sems
+    scale, tile_rows, k0, k1, k2, k3, k4, near, s1, s2, s3, far, out_hbm, out_ref, right_ref, sems
 ):
-    row, col = lax.axis_index("row"), lax.axis_index("col")
-    away = 1 - row
     cols = out_ref.shape[3]
     half_rows = k0.shape[0]
-    per_half = half_rows // cols
+    row, col, at, elsewhere = place_of_columns(cols, half_rows)
+    away = 1 - row
     odd = col % 2 == 1
     lefts = [
         (lambda at: k0[at, :]),
@@ -140,33 +168,19 @@
         (lambda at: s3[away, at, :]),
     ]
 
-    at = pl.ds(pl.multiple_of((col % per_half) * cols, cols), cols)
-    elsewhere = (row == 0) & (col >= per_half)
-    others = [
-        (lambda: g0[at, :]),
-        (lambda: g1[at, :]),
-        (lambda: g2[at, :]),
-        (lambda: g3[at, :]),
-        (lambda: far[away, cols : 2 * cols, :]),
-        (lambda: far[away, 0:cols, :]),
-        (lambda: c4[away]),
-        (lambda: far[away, 2 * cols : 3 * cols, :]),
-    ]
-    target = lax.broadcasted_iota(jnp.int32, (LANES, LANES), 0)
-    source = lax.broadcasted_iota(jnp.int32, (LANES, LANES), 1)
-    same = (source == target).astype(jnp.bfloat16)
-    turn = jnp.where(target == source + 4, 1.0, 0.0) * (source % 8 < 4).astype(jnp.float32)
-    turn = turn - jnp.where(target == source - 4, 1.0, 0.0) * (source % 8 >= 4).astype(jnp.float32)
-    turn = turn.astype(jnp.bfloat16)
-    blocks = [jnp.where(elsewhere, other(), own(at)) for own, other in zip(lefts, others)]
-    for pair in range(4):
-        lanes = slice(pair * LANES, (pair + 1) * LANES)
-        for ch, block in enumerate(by_channel(blocks[2 * pair], blocks[2 * pair + 1])):
-            right_ref[ch, lanes, 0:cols] = product_nt(same, block).astype(jnp.bfloat16)
-            right_ref[ch, lanes, cols : 2 * cols] = product_nt(turn, block).astype(jnp.bfloat16)
-
-    copies = []
-    for start in range(0, half_rows, tile_rows):
+    def prepare():
+        theirs = [far[cols * n : cols * (n + 1), :] for n in (1, 0, 3, 2)]
+        blocks = [jnp.where(elsewhere, other, own(at)) for own, other in zip(lefts[4:], theirs)]
+        put_columns(blocks[0], blocks[1], right_ref, 0)
+        put_columns(blocks[2], blocks[3], right_ref, LANES)
+
+    def copy_of(start):
+        here = slice(start, start + tile_rows)
+        return pltpu.make_async_copy(
+            out_ref.at[:, :, here, :], out_hbm.at[:, :, here, :], sems.at[start // tile_rows]
+        )
+
+    def products(start):
         here = slice(start, start + tile_rows)
         channels = ([], [])
         for pair in range(4):
@@ -177,16 +191,42 @@
         upper = row_ids < col_ids
         for ch in range(2):
             left = jnp.concatenate(channels[ch], 1)
-            total = jnp.dot(left, right_ref[ch], preferred_element_type=jnp.float32) * scale
+            total = jnp.dot(left[:, : 2 * LANES], near[ch], preferred_element_type=jnp.float32)
+            total = total + jnp.dot(left[:, 2 * LANES :], right_ref[ch], preferred_element_type=jnp.float32)
+            total = total * scale
             goes_to = jnp.where(odd, 1 - ch, ch)
             out_ref[0, goes_to, here, :] = jnp.where(upper, total[:, :cols], 0.0).astype(jnp.bfloat16)
             out_ref[1, goes_to, here, :] = jnp.where(upper, total[:, cols:], 0.0).astype(jnp.bfloat16)
-        copies.append(
-            pltpu.make_async_copy(out_ref.at[:, :, here, :], out_hbm.at[:, :, here, :], sems.at[len(copies)])
-        )
-        copies[-1].start()
-    for copy in copies:
-        copy.wait()
+        copy_of(start).start()
+
+    starts = range(0, half_rows, tile_rows)
+    reach = (col + 1) * cols - row * half_rows
+
+    @pl.when(reach >= half_rows)
+    def _():
+        prepare()
+        for start in starts:
+            products(start)
+
+    @pl.when(reach < half_rows)
+    def _():
+        for start in starts:
+
+            @pl.when(reach <= start)
+            def _():
+                here = slice(start, start + tile_rows)
+                out_ref[:, :, here, :] = jnp.zeros((2, 2, tile_rows, cols), jnp.bfloat16)
+                copy_of(start).start()
+
+        @pl.when(reach > 0)
+        def _():
+            prepare()
+
+        for start in starts:
+            pl.when(reach > start)(functools.partial(products, start))
+
+    for start in starts:
+        copy_of(start).wait()
 
 
 def shards(voltages, fir_taps):
@@ -249,25 +289,53 @@
         name="turn",
     )(both)
 
-    ahead = [(c, (c + 1) % col_size) for c in range(col_size)]
-    behind = [(col_size + c, col_size + (c - 1) % col_size) for c in range(col_size)]
-    on_ring = lambda array: lax.ppermute(array, ("row", "col"), ahead + behind)
+    late = col_size // 2
+    later, every = range(late, col_size), range(col_size)
+
+    def pairs_of(distance, reach, wanted, up):
+        core, sign = (0, 1) if up else (1, -1)
+        hops = []
+        for plane in range(col_size):
+            if any((plane + sign * d) % col_size in wanted for d in range(distance, reach + 1)):
+                source = (plane + sign * (distance - 1)) % col_size
+                hops.append((core * col_size + source, core * col_size + (source + sign) % col_size))
+        return hops
+
+    def keep_on(array, distance):
+        hops = pairs_of(distance, late, every, True) + pairs_of(distance, late, later, False)
+        return lax.ppermute(array, ("row", "col"), hops)
+
+    def give_on(array, distance):
+        hops = pairs_of(distance, late - 1, later, True) + pairs_of(distance, late - 1, every, False)
+        return lax.ppermute(array, ("row", "col"), hops)
+
     on_chip = lambda array: lax.all_gather(array, "row", axis=0)
 
     cols = chan_size * inputs_loc // col_size
-    col_offset = lax.rem(col, half // cols) * cols
-    col_part = lambda array: lax.dynamic_slice_in_dim(array, col_offset, cols, 0)
+    col_slice = lambda array, at: lax.dynamic_slice_in_dim(array, lax.rem(at, half // cols) * cols, cols, 0)
     keeps, gives = [keep], [give]
-    for step in range(col_size // 2 - 1):
-        keeps.append(on_ring(keeps[-1]))
-        gives.append(on_ring(gives[-1]))
-    keeps.append(on_ring(keeps[-1]))
+    for step in range(late - 1):
+        keeps.append(keep_on(keeps[-1], step + 1))
+        gives.append(give_on(gives[-1], step + 1))
+    far = lax.ppermute(
+        jnp.concatenate([col_slice(k, col + col_size - 1) for k in keeps], 0),
+        ("row", "col"),
+        [(col_size + (c + 1) % col_size, c) for c in later],
+    )
+    keeps.append(keep_on(keeps[-1], late))
     shared = [on_chip(g) for g in gives[1:]]
-    far = on_chip(jnp.concatenate([col_part(k) for k in keeps[1:-1]], 0))
-    last_cols = on_chip(col_part(keeps[-1]))
 
     tile = 256
-    operands = [*keeps, *gives, *shared, far, last_cols]
+    near = pl.pallas_call(
+        near_columns_kernel,
+        out_shape=jax.ShapeDtypeStruct((2, 2 * LANES, 2 * cols), jnp.bfloat16),
+        in_specs=[whole] * 8,
+        out_specs=whole,
+        cost_estimate=pl.CostEstimate(flops=NEAR_FLOPS, bytes_accessed=1_500_000, transcendentals=0),
+        compiler_params=params,
+        name="near_columns",
+    )(*keeps[:-1], *gives)
+    operands = [*keeps, near, *shared, far]
     out_shape = (2, 2, half, cols)
     return pl.pallas_call(
         functools.partial(correlate_kernel, 1.0 / math.sqrt(frames_loc * devices), tile),
@@ -276,7 +344,7 @@
         out_specs=pl.BlockSpec(memory_space=pl.ANY),
         scratch_shapes=[
             pltpu.VMEM(out_shape, jnp.bfloat16),
-            pltpu.VMEM((2, 4 * LANES, 2 * cols), jnp.bfloat16),
+            pltpu.VMEM((2, 2 * LANES, 2 * cols), jnp.bfloat16),
             pltpu.SemaphoreType.DMA((half // tile,)),
         ],
         compiler_params=params,

time: 82 us -> 78.3 us (0.955)
  blocking collectives: 36.3 us -> 28.9 us
  starting transfers between devices: 31.3 us -> 35 us
    all_gather x5 -> x3, blocking collectives: 14 us -> 6.54 us  [shards(): on_chip = lambda array: lax.all_gather(array, 'row', axis=0)]
    ppermute x7 -> x8, starting transfers between devices: 26.5 us -> 30.2 us  [the longest x4 16.8 us: keep_on(): return lax.ppermute(array, ('row', 'col'), hops)]
    pallas_call x1, Pallas kernels: 2.43 us -> 1.38 us  [shards(): pl.pallas_call(functools.partial(correlate_kernel, 1.0 / math.sqrt(frames...]
  transfers between devices with their start and end apart: 8 -> 9, of which waited for: 1 -> 2; matrix products, arithmetic and copies ran while one was open for 0% -> 0% of each run, Pallas kernels for 1% -> 2%
where the time goes in v6:
time: 78.3 us; the launch traced here: 77.8 us
  starting transfers between devices  35 us (45%)
  blocking collectives  28.9 us (37%)
  waiting for transfers between devices  6.13 us (8%)
  Pallas kernels  3.86 us (5%)
  local copies, waits for them, and re-layouts  3.74 us (5%)
    all_to_all x1, blocking collectives, shards(): lax.all_to_all(spectra, 'chan', split_axis=0, concat_axis=0, tiled=True)  20.1 us
    ppermute x4, starting transfers between devices, keep_on(): return lax.ppermute(array, ('row', 'col'), hops)  16.8 us
    ppermute x3, starting transfers between devices, give_on(): return lax.ppermute(array, ('row', 'col'), hops)  10.9 us
    all_gather x3, blocking collectives, shards(): on_chip = lambda array: lax.all_gather(array, 'row', axis=0)  6.54 us
    ppermute x1, waiting for transfers between devices, shards(): lax.ppermute(voltages[:, :, samples - group * channels:], ('row', 'col'),...  5.35 us
    ppermute x1, starting transfers between devices, shards(): lax.ppermute(voltages[:, :, samples - group * channels:], ('row', 'col'),...  4.82 us
    unnamed x6, local copies, waits for them, and re-layouts  2.85 us
    ppermute x1, starting transfers between devices, shards(): lax.ppermute(jnp.concatenate([col_slice(k, col + col_size - 1) for k in k...  2.54 us
  transfers between devices with their start and end apart: 9, of which 2 were waited for; matrix products, arithmetic and copies ran while one was open for 0% of the time, Pallas kernels for 2%

profile of v6, /device:TPU:1, one launch (start us, length us, event | category | flops | bytes accessed | tf_op | source)
XLA Modules:
  0.0 77.8 jit_solution(30985244369502109)
XLA Ops:
  0.0 0.8 %slice.3 = bf16[2,64,256]{2,1,0:T(8,128)(2,1)S(1)} slice(bf16[2,64,1024]{2,1,0:T(8,128)(2,1)} %volt_hbm.1), slice={[0:2], [0:64], [768:1024]} | slice | bytes 131072 | tf_op jit(solution)/shard_map/slice | solution.py:243
  0.8 4.8 %collective-permute-start = (bf16[2,64,256]{2,1,0:T(8,128)(2,1)S(1)}, bf16[2,64,256]{2,1,0:T(8,128)(2,1)S(1)}, u32[]{:S(2)}, u32[]{:S(2)}) collective-permute-start(bf16[2,64,256]{2,1,0:T(8,128)(2,1)S(1)} %slice.3), channel_id=1, source_target_pairs={{0,1},{1,2},{2,3},{3,4},{4,5},{5,6},{6,7},{7,8},{8,9},{9,10},{10,1... | collective-permute-start | bytes 196616 | tf_op jit(solution)/shard_map/ppermute | solution.py:242
  5.7 0.9 %copy-done = bf16[2,64,1024]{2,1,0:T(8,128)(2,1)S(1)} copy-done((bf16[2,64,1024]{2,1,0:T(8,128)(2,1)S(1)}, bf16[2,64,1024]{2,1,0:T(8,128)(2,1)}, u32[]{:S(2)}) %copy-start) | copy-done | bytes 262168
  6.6 0.7 copy-done.1
  7.3 1.2 %copy-done.2 = bf16[2,512,512]{2,1,0:T(8,128)(2,1)S(1)} copy-done((bf16[2,512,512]{2,1,0:T(8,128)(2,1)S(1)}, bf16[2,512,512]{2,1,0:T(8,128)(2,1)}, u32[]{:S(2)}) %copy-start.2) | copy-done | bytes 1048600
  8.5 0.9 %later_frames.1 = (bf16[2,64,256]{2,1,0:T(8,128)(2,1)S(1)}, f32[4,256]{1,0:T(4,128)S(1)}, bf16[2,512,512]{2,1,0:T(8,128)(2,1)S(1)}, bf16[512,256]{1,0:T(8,128)(2,1)S(1)}) custom-call(bf16[2,64,1024]{2,1,0:T(8,128)(2,1)S(1)} %copy-done, f32[4,64]{1,0:T(4,128)S(1)} %copy-done.1, bf16[2,512,512]{2,1,0:T(8,128)(2,1)S(1)} %copy-done.2), custom_call_target="tpu_custom_call" | custom-call | flops 500000000 | bytes 3000000 | tf_op jit(solution)/shard_map/later_frames/pallas_call | solution.py:251
  9.5 5.4 %collective-permute-done.halo_ref = bf16[2,64,256]{2,1,0:T(8,128)(2,1)S(1)} collective-permute-done((bf16[2,64,256]{2,1,0:T(8,128)(2,1)S(1)}, bf16[2,64,256]{2,1,0:T(8,128)(2,1)S(1)}, u32[]{:S(2)}, u32[]{:S(2)}) %collective-permute-start) | collective-permute-done | bytes 65568 | tf_op jit(solution)/shard_map/ppermute | solution.py:242
  14.8 0.7 first_frames.1
  15.5 20.1 %all_to_all.5 = bf16[32,16,256]{2,1,0:T(8,128)(2,1)S(1)} all-to-all(bf16[32,16,256]{2,1,0:T(8,128)(2,1)S(1)} %bitcast.9), channel_id=1, replica_groups=mesh['chan'=32,'row'=2,'col'=8] {'chan'}, dimensions={0} | all-to-all | bytes 524288 | tf_op jit(solution)/shard_map/all_to_all | solution.py:279
  35.6 2.2 %all-gather = bf16[64,16,256]{2,1,0:T(8,128)(2,1)S(1)} all-gather(bf16[32,16,256]{2,1,0:T(8,128)(2,1)S(1)} %all_to_all.5), channel_id=2, replica_groups=mesh['chan'=32,'row'=2,'col'=8] {'row'}, dimensions={0}, use_global_device_ids=true | all-gather | bytes 786432 | tf_op jit(solution)/shard_map/all_gather | solution.py:280
  37.8 0.6 turn.1
  38.4 5.7 %collective-permute-start.1 = (bf16[1024,128]{1,0:T(8,128)(2,1)S(1)}, bf16[1024,128]{1,0:T(8,128)(2,1)S(1)}, u32[]{:S(2)}, u32[]{:S(2)}) collective-permute-start(bf16[1024,128]{1,0:T(8,128)(2,1)S(1)} %get-tuple-element.15.k0), channel_id=1, source_target_pairs={{0,1},{1,2},{2,3},{3,4},{4,5},{5,6},{6,7},{7,0},{8,15},{9,8},{10,9... | collective-permute-start | bytes 786440 | tf_op jit(solution)/shard_map/ppermute | solution.py:306
  44.1 3.6 %collective-permute-start.5 = (bf16[1024,128]{1,0:T(8,128)(2,1)S(1)}, bf16[1024,128]{1,0:T(8,128)(2,1)S(1)}, u32[]{:S(2)}, u32[]{:S(2)}) collective-permute-start(bf16[1024,128]{1,0:T(8,128)(2,1)S(1)} %get-tuple-element.16.g0), channel_id=1, source_target_pairs={{1,2},{2,3},{3,4},{4,5},{5,6},{6,7},{8,15},{9,8},{10,9},{11,10},{1... | collective-permute-start | bytes 786440 | tf_op jit(solution)/shard_map/ppermute | solution.py:310
  47.8 4.7 %collective-permute-start.2 = (bf16[1024,128]{1,0:T(8,128)(2,1)S(1)}, bf16[1024,128]{1,0:T(8,128)(2,1)S(1)}, u32[]{:S(2)}, u32[]{:S(2)}) collective-permute-start(bf16[1024,128]{1,0:T(8,128)(2,1)S(1)} %collective-permute-done.1.k1), channel_id=1, source_target_pairs={{1,2},{2,3},{3,4},{4,5},{5,6},{6,7},{7,0},{0,1},{15,14},{8,15},{9,... | collective-permute-start | bytes 786440 | tf_op jit(solution)/shard_map/ppermute | solution.py:306
  52.5 3.6 %collective-permute-start.6 = (bf16[1024,128]{1,0:T(8,128)(2,1)S(1)}, bf16[1024,128]{1,0:T(8,128)(2,1)S(1)}, u32[]{:S(2)}, u32[]{:S(2)}) collective-permute-start(bf16[1024,128]{1,0:T(8,128)(2,1)S(1)} %collective-permute-done.5.g1), channel_id=1, source_target_pairs={{2,3},{3,4},{4,5},{5,6},{6,7},{15,14},{8,15},{9,8},{10,9},{11,10},... | collective-permute-start | bytes 786440 | tf_op jit(solution)/shard_map/ppermute | solution.py:310
  56.1 2.2 %all-gather.1 = bf16[2048,128]{1,0:T(8,128)(2,1)S(1)} all-gather(bf16[1024,128]{1,0:T(8,128)(2,1)S(1)} %collective-permute-done.5.g1), channel_id=3, replica_groups=mesh['chan'=32,'row'=2,'col'=8] {'row'}, dimensions={0}, use_global_device_ids=true | all-gather | bytes 786432 | tf_op jit(solution)/shard_map/all_gather | solution.py:312
  58.3 2.5 %collective-permute-start.3 = (bf16[1024,128]{1,0:T(8,128)(2,1)S(1)}, bf16[1024,128]{1,0:T(8,128)(2,1)S(1)}, u32[]{:S(2)}, u32[]{:S(2)}) collective-permute-start(bf16[1024,128]{1,0:T(8,128)(2,1)S(1)} %collective-permute-done.2.k2), channel_id=1, source_target_pairs={{2,3},{3,4},{4,5},{5,6},{6,7},{7,0},{0,1},{1,2},{14,13},{15,14},{8... | collective-permute-start | bytes 786440 | tf_op jit(solution)/shard_map/ppermute | solution.py:306
  60.8 3.6 %collective-permute-start.7 = (bf16[1024,128]{1,0:T(8,128)(2,1)S(1)}, bf16[1024,128]{1,0:T(8,128)(2,1)S(1)}, u32[]{:S(2)}, u32[]{:S(2)}) collective-permute-start(bf16[1024,128]{1,0:T(8,128)(2,1)S(1)} %collective-permute-done.6.g2), channel_id=1, source_target_pairs={{3,4},{4,5},{5,6},{6,7},{14,13},{15,14},{8,15},{9,8},{10,9},{11,10... | collective-permute-start | bytes 786440 | tf_op jit(solution)/shard_map/ppermute | solution.py:310
  64.4 2.2 %all-gather.2 = bf16[2048,128]{1,0:T(8,128)(2,1)S(1)} all-gather(bf16[1024,128]{1,0:T(8,128)(2,1)S(1)} %collective-permute-done.6.g2), channel_id=4, replica_groups=mesh['chan'=32,'row'=2,'col'=8] {'row'}, dimensions={0}, use_global_device_ids=true | all-gather | bytes 786432 | tf_op jit(solution)/shard_map/all_gather | solution.py:312
  66.6 2.5 %collective-permute-start.8 = (bf16[1024,128]{1,0:T(8,128)(2,1)S(1)}, bf16[1024,128]{1,0:T(8,128)(2,1)S(1)}, u32[]{:S(2)}, u32[]{:S(2)}) collective-permute-start(bf16[1024,128]{1,0:T(8,128)(2,1)S(1)} %pad_maximum_fusion), channel_id=1, source_target_pairs={{13,4},{14,5},{15,6},{8,7},{29,20},{30,21},{31,22},{24,23},{45,36}... | collective-permute-start | bytes 786440 | tf_op jit(solution)/shard_map/ppermute | solution.py:320
  69.2 3.9 %collective-permute-start.4 = (bf16[1024,128]{1,0:T(8,128)(2,1)S(1)}, bf16[1024,128]{1,0:T(8,128)(2,1)S(1)}, u32[]{:S(2)}, u32[]{:S(2)}) collective-permute-start(bf16[1024,128]{1,0:T(8,128)(2,1)S(1)} %collective-permute-done.3.k3), channel_id=1, source_target_pairs={{3,4},{4,5},{5,6},{6,7},{7,0},{0,1},{1,2},{2,3},{13,12},{14,13},{1... | collective-permute-start | bytes 786440 | tf_op jit(solution)/shard_map/ppermute | solution.py:306
  73.1 2.2 %all-gather.3 = bf16[2048,128]{1,0:T(8,128)(2,1)S(1)} all-gather(bf16[1024,128]{1,0:T(8,128)(2,1)S(1)} %collective-permute-done.7.g3), channel_id=5, replica_groups=mesh['chan'=32,'row'=2,'col'=8] {'row'}, dimensions={0}, use_global_device_ids=true | all-gather | bytes 786432 | tf_op jit(solution)/shard_map/all_gather | solution.py:312
  75.6 0.8 collective-permute-done.4.k4
  76.4 1.4 %correlate.1 = bf16[2,2,1024,256]{3,2,1,0:T(8,128)(2,1)} custom-call(bf16[1024,128]{1,0:T(8,128)(2,1)S(1)} %get-tuple-element.15.k0, bf16[1024,128]{1,0:T(8,128)(2,1)S(1)} %collective-permute-done.1.k1, bf16[1024,128]{1,0:T(8,128)(2,1)S(1)} %collective-permute-done.2.k2, bf16[1024,128]{1,0:T(8,128)(2,1)S(1)} %collective-permute-done.3.k3, ...), custom_call_target="tpu_custom_call" | custom-call | tf_op jit(solution)/shard_map/correlate/pallas_call | solution.py:340
  (16 shorter events, 0.4 us)
Async XLA Ops:
  0.8 14.0 %collective-permute-start = (bf16[2,64,256]{2,1,0:T(8,128)(2,1)S(1)}, bf16[2,64,256]{2,1,0:T(8,128)(2,1)S(1)}, u32[]{:S(2)}, u32[]{:S(2)}) collective-permute-start(bf16[2,64,256]{2,1,0:T(8,128)(2,1)S(1)} %slice.3), channel_id=1, source_target_pairs={{0,1},{1,2},{2,3},{3,4},{4,5},{5,6},{6,7},{7,8},{8,9},{9,10},{10,1... | collective-permute-start | bytes 196616 | tf_op jit(solution)/shard_map/ppermute | solution.py:242
  5.7 1.0 %copy-start = (bf16[2,64,1024]{2,1,0:T(8,128)(2,1)S(1)}, bf16[2,64,1024]{2,1,0:T(8,128)(2,1)}, u32[]{:S(2)}) copy-start(bf16[2,64,1024]{2,1,0:T(8,128)(2,1)} %volt_hbm.1) | copy-start | bytes 786436
  6.6 0.7 copy-start.1
  7.3 1.2 %copy-start.2 = (bf16[2,512,512]{2,1,0:T(8,128)(2,1)S(1)}, bf16[2,512,512]{2,1,0:T(8,128)(2,1)}, u32[]{:S(2)}) copy-start(bf16[2,512,512]{2,1,0:T(8,128)(2,1)} %constant.21.clone.table_hbm) | copy-start | bytes 3145732
  38.4 9.4 %collective-permute-start.1 = (bf16[1024,128]{1,0:T(8,128)(2,1)S(1)}, bf16[1024,128]{1,0:T(8,128)(2,1)S(1)}, u32[]{:S(2)}, u32[]{:S(2)}) collective-permute-start(bf16[1024,128]{1,0:T(8,128)(2,1)S(1)} %get-tuple-element.15.k0), channel_id=1, source_target_pairs={{0,1},{1,2},{2,3},{3,4},{4,5},{5,6},{6,7},{7,0},{8,15},{9,8},{10,9... | collective-permute-start | bytes 786440 | tf_op jit(solution)/shard_map/ppermute | solution.py:306
  44.1 8.3 %collective-permute-start.5 = (bf16[1024,128]{1,0:T(8,128)(2,1)S(1)}, bf16[1024,128]{1,0:T(8,128)(2,1)S(1)}, u32[]{:S(2)}, u32[]{:S(2)}) collective-permute-start(bf16[1024,128]{1,0:T(8,128)(2,1)S(1)} %get-tuple-element.16.g0), channel_id=1, source_target_pairs={{1,2},{2,3},{3,4},{4,5},{5,6},{6,7},{8,15},{9,8},{10,9},{11,10},{1... | collective-permute-start | bytes 786440 | tf_op jit(solution)/shard_map/ppermute | solution.py:310
  47.8 10.5 %collective-permute-start.2 = (bf16[1024,128]{1,0:T(8,128)(2,1)S(1)}, bf16[1024,128]{1,0:T(8,128)(2,1)S(1)}, u32[]{:S(2)}, u32[]{:S(2)}) collective-permute-start(bf16[1024,128]{1,0:T(8,128)(2,1)S(1)} %collective-permute-done.1.k1), channel_id=1, source_target_pairs={{1,2},{2,3},{3,4},{4,5},{5,6},{6,7},{7,0},{0,1},{15,14},{8,15},{9,... | collective-permute-start | bytes 786440 | tf_op jit(solution)/shard_map/ppermute | solution.py:306
  52.5 8.3 %collective-permute-start.6 = (bf16[1024,128]{1,0:T(8,128)(2,1)S(1)}, bf16[1024,128]{1,0:T(8,128)(2,1)S(1)}, u32[]{:S(2)}, u32[]{:S(2)}) collective-permute-start(bf16[1024,128]{1,0:T(8,128)(2,1)S(1)} %collective-permute-done.5.g1), channel_id=1, source_target_pairs={{2,3},{3,4},{4,5},{5,6},{6,7},{15,14},{8,15},{9,8},{10,9},{11,10},... | collective-permute-start | bytes 786440 | tf_op jit(solution)/shard_map/ppermute | solution.py:310
  58.3 8.3 %collective-permute-start.3 = (bf16[1024,128]{1,0:T(8,128)(2,1)S(1)}, bf16[1024,128]{1,0:T(8,128)(2,1)S(1)}, u32[]{:S(2)}, u32[]{:S(2)}) collective-permute-start(bf16[1024,128]{1,0:T(8,128)(2,1)S(1)} %collective-permute-done.2.k2), channel_id=1, source_target_pairs={{2,3},{3,4},{4,5},{5,6},{6,7},{7,0},{0,1},{1,2},{14,13},{15,14},{8... | collective-permute-start | bytes 786440 | tf_op jit(solution)/shard_map/ppermute | solution.py:306
  60.8 12.3 %collective-permute-start.7 = (bf16[1024,128]{1,0:T(8,128)(2,1)S(1)}, bf16[1024,128]{1,0:T(8,128)(2,1)S(1)}, u32[]{:S(2)}, u32[]{:S(2)}) collective-permute-start(bf16[1024,128]{1,0:T(8,128)(2,1)S(1)} %collective-permute-done.6.g2), channel_id=1, source_target_pairs={{3,4},{4,5},{5,6},{6,7},{14,13},{15,14},{8,15},{9,8},{10,9},{11,10... | collective-permute-start | bytes 786440 | tf_op jit(solution)/shard_map/ppermute | solution.py:310
  66.6 9.0 %collective-permute-start.8 = (bf16[1024,128]{1,0:T(8,128)(2,1)S(1)}, bf16[1024,128]{1,0:T(8,128)(2,1)S(1)}, u32[]{:S(2)}, u32[]{:S(2)}) collective-permute-start(bf16[1024,128]{1,0:T(8,128)(2,1)S(1)} %pad_maximum_fusion), channel_id=1, source_target_pairs={{13,4},{14,5},{15,6},{8,7},{29,20},{30,21},{31,22},{24,23},{45,36}... | collective-permute-start | bytes 786440 | tf_op jit(solution)/shard_map/ppermute | solution.py:320
  69.2 7.2 %collective-permute-start.4 = (bf16[1024,128]{1,0:T(8,128)(2,1)S(1)}, bf16[1024,128]{1,0:T(8,128)(2,1)S(1)}, u32[]{:S(2)}, u32[]{:S(2)}) collective-permute-start(bf16[1024,128]{1,0:T(8,128)(2,1)S(1)} %collective-permute-done.3.k3), channel_id=1, source_target_pairs={{3,4},{4,5},{5,6},{6,7},{7,0},{0,1},{1,2},{2,3},{13,12},{14,13},{1... | collective-permute-start | bytes 786440 | tf_op jit(solution)/shard_map/ppermute | solution.py:306

commit v7 on v6

--- a/solution.py
+++ b/solution.py
@@ -55,7 +55,13 @@
     return (spectra + product_nt(high, frames_high)).astype(jnp.bfloat16)
 
 
-def later_kernel(volt_hbm, taps_hbm, table_hbm, volt_out, taps_out, table_out, late_out, volt_ref, taps_ref, sems):
+def reach_of(half_rows, cols):
+    return (lax.axis_index("col") + 1) * cols - lax.axis_index("row") * half_rows
+
+
+def later_kernel(
+    tile_rows, volt_hbm, taps_hbm, table_hbm, volt_out, taps_out, table_out, late_out, vis_hbm, volt_ref, taps_ref, zero_ref, sems
+):
     copies = [
         pltpu.make_async_copy(source, target, sems.at[i])
         for i, (source, target) in enumerate(
@@ -64,6 +70,22 @@
     ]
     for copy in copies:
         copy.start()
+
+    half_rows, cols = vis_hbm.shape[2:]
+    reach = reach_of(half_rows, cols)
+    starts = range(0, half_rows, tile_rows)
+    zero_copies = [
+        pltpu.make_async_copy(zero_ref, vis_hbm.at[:, :, start : start + tile_rows, :], sems.at[3 + i])
+        for i, start in enumerate(starts)
+    ]
+
+    @pl.when(reach < half_rows)
+    def _():
+        zero_ref[...] = jnp.zeros(zero_ref.shape, zero_ref.dtype)
+
+    for start, copy in zip(starts, zero_copies):
+        pl.when(reach <= start)(copy.start)
+
     copies[0].wait()
     copies[1].wait()
     samples = volt_ref.shape[2]
@@ -77,6 +99,8 @@
     first = jnp.zeros((volt_ref.shape[1], frames.shape[1]), jnp.float32)
     copies[2].wait()
     late_out[...] = transformed(jnp.concatenate([first, frames], 0), table_out[0], table_out[1])
+    for start, copy in zip(starts, zero_copies):
+        pl.when(reach <= start)(copy.wait)
 
 
 def first_kernel(volt_ref, halo_ref, taps_ref, table_ref, late_ref, out_ref):
@@ -142,37 +166,62 @@
         right_ref[ch, lanes, cols : 2 * cols] = product_nt(turn, block).astype(jnp.bfloat16)
 
 
-def near_columns_kernel(k0, k1, k2, k3, g0, g1, g2, g3, right_ref):
-    _, _, at, elsewhere = place_of_columns(right_ref.shape[2] // 2, k0.shape[0])
-    near = [jnp.where(elsewhere, g[at, :], k[at, :]) for k, g in ((k0, g0), (k1, g1), (k2, g2), (k3, g3))]
-    put_columns(near[0], near[1], right_ref, 0)
-    put_columns(near[2], near[3], right_ref, LANES)
-
-
-def correlate_kernel(
-    scale, tile_rows, k0, k1, k2, k3, k4, near, s1, s2, s3, far, out_hbm, out_ref, right_ref, sems
-):
+def for_tiles(half_rows, tile_rows, cols, prepare, products, finish=None):
+    starts = range(0, half_rows, tile_rows)
+    reach = reach_of(half_rows, cols)
+
+    @pl.when(reach >= half_rows)
+    def _():
+        prepare()
+        for start in starts:
+            products(start)
+        for start in starts if finish else ():
+            finish(start)
+
+    @pl.when((reach > 0) & (reach < half_rows))
+    def _():
+        prepare()
+        for start in starts:
+            pl.when(reach > start)(functools.partial(products, start))
+        for start in starts if finish else ():
+            pl.when(reach > start)(functools.partial(finish, start))
+
+
+def near_kernel(tile_rows, k0, k1, k2, k3, g0, g1, g2, g3, sum_ref, right_ref):
+    half_rows = k0.shape[0]
+    cols = sum_ref.shape[2] // 2
+    _, _, at, elsewhere = place_of_columns(cols, half_rows)
+
+    def prepare():
+        near = [jnp.where(elsewhere, g[at, :], k[at, :]) for k, g in ((k0, g0), (k1, g1), (k2, g2), (k3, g3))]
+        put_columns(near[0], near[1], right_ref, 0)
+        put_columns(near[2], near[3], right_ref, LANES)
+
+    def products(start):
+        here = slice(start, start + tile_rows)
+        pairs = ((k0[here, :], k1[here, :]), (k2[here, :], k3[here, :]))
+        split = [by_channel(*pair) for pair in pairs]
+        for ch in range(2):
+            left = jnp.concatenate([blocks[ch] for blocks in split], 1)
+            sum_ref[ch, here, :] = jnp.dot(left, right_ref[ch], preferred_element_type=jnp.float32)
+
+    for_tiles(half_rows, tile_rows, cols, prepare, products)
+
+
+def correlate_kernel(scale, tile_rows, k4, s1, s2, s3, far, near, zeros_hbm, out_hbm, out_ref, right_ref, sems):
+    half_rows = k4.shape[0]
     cols = out_ref.shape[3]
-    half_rows = k0.shape[0]
     row, col, at, elsewhere = place_of_columns(cols, half_rows)
     away = 1 - row
     odd = col % 2 == 1
-    lefts = [
-        (lambda at: k0[at, :]),
-        (lambda at: k1[at, :]),
-        (lambda at: k2[at, :]),
-        (lambda at: k3[at, :]),
-        (lambda at: s2[away, at, :]),
-        (lambda at: s1[away, at, :]),
-        (lambda at: k4[at, :]),
-        (lambda at: s3[away, at, :]),
-    ]
 
     def prepare():
-        theirs = [far[cols * n : cols * (n + 1), :] for n in (1, 0, 3, 2)]
-        blocks = [jnp.where(elsewhere, other, own(at)) for own, other in zip(lefts[4:], theirs)]
-        put_columns(blocks[0], blocks[1], right_ref, 0)
-        put_columns(blocks[2], blocks[3], right_ref, LANES)
+        four = jnp.where(elsewhere, far[3 * cols : 4 * cols, :], k4[at, :])
+        three = jnp.where(elsewhere, far[2 * cols : 3 * cols, :], s3[away, at, :])
+        put_columns(four, three, right_ref, 0)
+        two = jnp.where(elsewhere, far[cols : 2 * cols, :], s2[away, at, :])
+        one = jnp.where(elsewhere, far[0:cols, :], s1[away, at, :])
+        put_columns(two, one, right_ref, LANES)
 
     def copy_of(start):
         here = slice(start, start + tile_rows)
@@ -182,51 +231,21 @@
 
     def products(start):
         here = slice(start, start + tile_rows)
-        channels = ([], [])
-        for pair in range(4):
-            for ch, block in enumerate(by_channel(lefts[2 * pair](here), lefts[2 * pair + 1](here))):
-                channels[ch].append(block)
+        pairs = ((k4[here, :], s3[away, here, :]), (s2[away, here, :], s1[away, here, :]))
+        split = [by_channel(*pair) for pair in pairs]
         row_ids = row * half_rows + start + lax.broadcasted_iota(jnp.int32, (tile_rows, cols), 0)
         col_ids = col * cols + lax.broadcasted_iota(jnp.int32, (tile_rows, cols), 1)
         upper = row_ids < col_ids
         for ch in range(2):
-            left = jnp.concatenate(channels[ch], 1)
-            total = jnp.dot(left[:, : 2 * LANES], near[ch], preferred_element_type=jnp.float32)
-            total = total + jnp.dot(left[:, 2 * LANES :], right_ref[ch], preferred_element_type=jnp.float32)
-            total = total * scale
+            left = jnp.concatenate([blocks[ch] for blocks in split], 1)
+            total = jnp.dot(left, right_ref[ch], preferred_element_type=jnp.float32)
+            total = (total + near[ch, here, :]) * scale
             goes_to = jnp.where(odd, 1 - ch, ch)
             out_ref[0, goes_to, here, :] = jnp.where(upper, total[:, :cols], 0.0).astype(jnp.bfloat16)
             out_ref[1, goes_to, here, :] = jnp.where(upper, total[:, cols:], 0.0).astype(jnp.bfloat16)
         copy_of(start).start()
 
-    starts = range(0, half_rows, tile_rows)
-    reach = (col + 1) * cols - row * half_rows
-
-    @pl.when(reach >= half_rows)
-    def _():
-        prepare()
-        for start in starts:
-            products(start)
-
-    @pl.when(reach < half_rows)
-    def _():
-        for start in starts:
-
-            @pl.when(reach <= start)
-            def _():
-                here = slice(start, start + tile_rows)
-                out_ref[:, :, here, :] = jnp.zeros((2, 2, tile_rows, cols), jnp.bfloat16)
-                copy_of(start).start()
-
-        @pl.when(reach > 0)
-        def _():
-            prepare()
-
-        for start in starts:
-            pl.when(reach > start)(functools.partial(products, start))
-
-    for start in starts:
-        copy_of(start).wait()
+    for_tiles(half_rows, tile_rows, cols, prepare, products, lambda start: copy_of(start).wait())
 
 
 def shards(voltages, fir_taps):
@@ -248,20 +267,26 @@
     frames_loc = samples // channels
     spectra_shape = (channels * 2 * group, frames_loc // group * inputs_loc)
     in_hbm = pl.BlockSpec(memory_space=pltpu.HBM)
-    volt_early, taps, table, late = pl.pallas_call(
-        later_kernel,
+    tile = 256
+    half = chan_size * inputs_loc // row_size
+    cols = chan_size * inputs_loc // col_size
+    vis_shape = jax.ShapeDtypeStruct((2, 2, half, cols), jnp.bfloat16)
+    volt_early, taps, table, late, visibilities = pl.pallas_call(
+        functools.partial(later_kernel, tile),
         out_shape=[
             jax.ShapeDtypeStruct((2, inputs_loc, group * channels), jnp.bfloat16),
             jax.ShapeDtypeStruct((fir_taps.shape[0], group * channels), jnp.float32),
             jax.ShapeDtypeStruct(table.shape, jnp.bfloat16),
             jax.ShapeDtypeStruct(spectra_shape, jnp.bfloat16),
+            vis_shape,
         ],
         in_specs=[in_hbm] * 3,
-        out_specs=[whole] * 4,
+        out_specs=[whole] * 4 + [pl.BlockSpec(memory_space=pl.ANY)],
         scratch_shapes=[
             pltpu.VMEM(voltages.shape, jnp.bfloat16),
             pltpu.VMEM(fir_taps.shape, jnp.float32),
-            pltpu.SemaphoreType.DMA((3,)),
+            pltpu.VMEM((2, 2, tile, cols), jnp.bfloat16),
+            pltpu.SemaphoreType.DMA((3 + half // tile,)),
         ],
         cost_estimate=pl.CostEstimate(flops=500_000_000, bytes_accessed=3_000_000, transcendentals=0),
         compiler_params=params,
@@ -279,7 +304,6 @@
     turned = lax.all_to_all(spectra, "chan", split_axis=0, concat_axis=0, tiled=True)
     both = lax.all_gather(turned, "row", axis=0)
 
-    half = chan_size * inputs_loc // row_size
     keep, give = pl.pallas_call(
         turn_kernel,
         out_shape=[jax.ShapeDtypeStruct((half, LANES), jnp.bfloat16)] * 2,
@@ -311,7 +335,6 @@
 
     on_chip = lambda array: lax.all_gather(array, "row", axis=0)
 
-    cols = chan_size * inputs_loc // col_size
     col_slice = lambda array, at: lax.dynamic_slice_in_dim(array, lax.rem(at, half // cols) * cols, cols, 0)
     keeps, gives = [keep], [give]
     for step in range(late - 1):
@@ -325,31 +348,30 @@
     keeps.append(keep_on(keeps[-1], late))
     shared = [on_chip(g) for g in gives[1:]]
 
-    tile = 256
     near = pl.pallas_call(
-        near_columns_kernel,
-        out_shape=jax.ShapeDtypeStruct((2, 2 * LANES, 2 * cols), jnp.bfloat16),
+        functools.partial(near_kernel, tile),
+        out_shape=jax.ShapeDtypeStruct((2, half, 2 * cols), jnp.float32),
         in_specs=[whole] * 8,
         out_specs=whole,
-        cost_estimate=pl.CostEstimate(flops=NEAR_FLOPS, bytes_accessed=1_500_000, transcendentals=0),
-        compiler_params=params,
-        name="near_columns",
+        scratch_shapes=[pltpu.VMEM((2, 2 * LANES, 2 * cols), jnp.bfloat16)],
+        cost_estimate=pl.CostEstimate(flops=NEAR_FLOPS, bytes_accessed=6_000_000, transcendentals=0),
+        compiler_params=params,
+        name="near_planes",
     )(*keeps[:-1], *gives)
-    operands = [*keeps, near, *shared, far]
-    out_shape = (2, 2, half, cols)
     return pl.pallas_call(
         functools.partial(correlate_kernel, 1.0 / math.sqrt(frames_loc * devices), tile),
-        out_shape=jax.ShapeDtypeStruct(out_shape, jnp.bfloat16),
-        in_specs=[whole] * len(operands),
+        out_shape=vis_shape,
+        in_specs=[whole] * 6 + [pl.BlockSpec(memory_space=pl.ANY)],
         out_specs=pl.BlockSpec(memory_space=pl.ANY),
+        input_output_aliases={6: 0},
         scratch_shapes=[
-            pltpu.VMEM(out_shape, jnp.bfloat16),
+            pltpu.VMEM(vis_shape.shape, jnp.bfloat16),
             pltpu.VMEM((2, 2 * LANES, 2 * cols), jnp.bfloat16),
             pltpu.SemaphoreType.DMA((half // tile,)),
         ],
         compiler_params=params,
         name="correlate",
-    )(*operands)
+    )(keeps[-1], *shared, far, near, visibilities)
 
 
 def solution(mesh):

time: 78.3 us -> 78.1 us (level)
  the two profiles are of different devices: /device:TPU:1 before, /device:TPU:8 now
where the time goes in v7:
time: 78.1 us; the launch traced here: 77.6 us
  blocking collectives  42.9 us (55%)
  starting transfers between devices  15.7 us (20%)
  waiting for transfers between devices  10.4 us (13%)
  Pallas kernels  4.63 us (6%)
  local copies, waits for them, and re-layouts  3.73 us (5%)
    all_to_all x1, blocking collectives, shards(): lax.all_to_all(spectra, 'chan', split_axis=0, concat_axis=0, tiled=True)  20.8 us
    all_gather x3, blocking collectives, shards(): on_chip = lambda array: lax.all_gather(array, 'row', axis=0)  17.3 us
    ppermute x4, waiting for transfers between devices, keep_on(): return lax.ppermute(array, ('row', 'col'), hops)  10.3 us
    ppermute x4, starting transfers between devices, keep_on(): return lax.ppermute(array, ('row', 'col'), hops)  8.74 us
    all_gather x1, blocking collectives, shards(): both = lax.all_gather(turned, 'row', axis=0)  4.86 us
    ppermute x1, starting transfers between devices, shards(): lax.ppermute(voltages[:, :, samples - group * channels:], ('row', 'col'),...  4.27 us
    unnamed x6, local copies, waits for them, and re-layouts  2.85 us
    ppermute x3, starting transfers between devices, give_on(): return lax.ppermute(array, ('row', 'col'), hops)  2.03 us
  transfers between devices with their start and end apart: 9, of which 3 were waited for; matrix products, arithmetic and copies ran while one was open for 0% of the time, Pallas kernels for 3%

profile of v7, /device:TPU:8, one launch (start us, length us, event | category | flops | bytes accessed | tf_op | source)
XLA Modules:
  0.0 77.6 jit_solution(16865777976374986581)
XLA Ops:
  0.0 0.8 %slice.3 = bf16[2,64,256]{2,1,0:T(8,128)(2,1)S(1)} slice(bf16[2,64,1024]{2,1,0:T(8,128)(2,1)} %volt_hbm.1), slice={[0:2], [0:64], [768:1024]} | slice | bytes 131072 | tf_op jit(solution)/shard_map/slice | solution.py:262
  0.8 4.3 %collective-permute-start = (bf16[2,64,256]{2,1,0:T(8,128)(2,1)S(1)}, bf16[2,64,256]{2,1,0:T(8,128)(2,1)S(1)}, u32[]{:S(2)}, u32[]{:S(2)}) collective-permute-start(bf16[2,64,256]{2,1,0:T(8,128)(2,1)S(1)} %slice.3), channel_id=1, source_target_pairs={{0,1},{1,2},{2,3},{3,4},{4,5},{5,6},{6,7},{7,8},{8,9},{9,10},{10,1... | collective-permute-start | bytes 196616 | tf_op jit(solution)/shard_map/ppermute | solution.py:261
  5.1 0.9 %copy-done = bf16[2,64,1024]{2,1,0:T(8,128)(2,1)S(1)} copy-done((bf16[2,64,1024]{2,1,0:T(8,128)(2,1)S(1)}, bf16[2,64,1024]{2,1,0:T(8,128)(2,1)}, u32[]{:S(2)}) %copy-start) | copy-done | bytes 262168
  6.1 0.7 copy-done.1
  6.8 1.2 %copy-done.2 = bf16[2,512,512]{2,1,0:T(8,128)(2,1)S(1)} copy-done((bf16[2,512,512]{2,1,0:T(8,128)(2,1)S(1)}, bf16[2,512,512]{2,1,0:T(8,128)(2,1)}, u32[]{:S(2)}) %copy-start.2) | copy-done | bytes 1048600
  8.0 1.3 %later_frames.1 = (bf16[2,64,256]{2,1,0:T(8,128)(2,1)S(1)}, f32[4,256]{1,0:T(4,128)S(1)}, bf16[2,512,512]{2,1,0:T(8,128)(2,1)S(1)}, bf16[512,256]{1,0:T(8,128)(2,1)S(1)}, bf16[2,2,1024,256]{3,2,1,0:T(8,128)(2,1)}) custom-call(bf16[2,64,1024]{2,1,0:T(8,128)(2,1)S(1)} %copy-done, f32[4,64]{1,0:T(4,128)S(1)} %copy-done.1, bf16[2,512,512]{2,1,0:T(8,128)(2,1)S(1)} %copy-done.2), custom_call_target="tpu_custom_call" | custom-call | flops 500000000 | bytes 3000000 | tf_op jit(solution)/shard_map/later_frames/pallas_call | solution.py:274
  9.3 0.7 first_frames.1
  10.0 20.8 %all_to_all.5 = bf16[32,16,256]{2,1,0:T(8,128)(2,1)S(1)} all-to-all(bf16[32,16,256]{2,1,0:T(8,128)(2,1)S(1)} %bitcast.9), channel_id=1, replica_groups=mesh['chan'=32,'row'=2,'col'=8] {'chan'}, dimensions={0} | all-to-all | bytes 524288 | tf_op jit(solution)/shard_map/all_to_all | solution.py:304
  30.8 4.9 %all-gather = bf16[64,16,256]{2,1,0:T(8,128)(2,1)S(1)} all-gather(bf16[32,16,256]{2,1,0:T(8,128)(2,1)S(1)} %all_to_all.5), channel_id=2, replica_groups=mesh['chan'=32,'row'=2,'col'=8] {'row'}, dimensions={0}, use_global_device_ids=true | all-gather | bytes 786432 | tf_op jit(solution)/shard_map/all_gather | solution.py:305
  36.2 2.8 %collective-permute-start.1 = (bf16[1024,128]{1,0:T(8,128)(2,1)S(1)}, bf16[1024,128]{1,0:T(8,128)(2,1)S(1)}, u32[]{:S(2)}, u32[]{:S(2)}) collective-permute-start(bf16[1024,128]{1,0:T(8,128)(2,1)S(1)} %get-tuple-element.16.k0), channel_id=1, source_target_pairs={{0,1},{1,2},{2,3},{3,4},{4,5},{5,6},{6,7},{7,0},{8,15},{9,8},{10,9... | collective-permute-start | bytes 786440 | tf_op jit(solution)/shard_map/ppermute | solution.py:330
  39.0 0.7 collective-permute-start.5
  39.7 7.0 %collective-permute-done.1.k1 = bf16[1024,128]{1,0:T(8,128)(2,1)S(1)} collective-permute-done((bf16[1024,128]{1,0:T(8,128)(2,1)S(1)}, bf16[1024,128]{1,0:T(8,128)(2,1)S(1)}, u32[]{:S(2)}, u32[]{:S(2)}) %collective-permute-start.1) | collective-permute-done | bytes 262176 | tf_op jit(solution)/shard_map/ppermute | solution.py:330
  46.8 2.1 %collective-permute-start.2 = (bf16[1024,128]{1,0:T(8,128)(2,1)S(1)}, bf16[1024,128]{1,0:T(8,128)(2,1)S(1)}, u32[]{:S(2)}, u32[]{:S(2)}) collective-permute-start(bf16[1024,128]{1,0:T(8,128)(2,1)S(1)} %collective-permute-done.1.k1), channel_id=1, source_target_pairs={{1,2},{2,3},{3,4},{4,5},{5,6},{6,7},{7,0},{0,1},{15,14},{8,15},{9,... | collective-permute-start | bytes 786440 | tf_op jit(solution)/shard_map/ppermute | solution.py:330
  48.9 0.7 collective-permute-start.6
  49.6 6.9 %all-gather.1 = bf16[2048,128]{1,0:T(8,128)(2,1)S(1)} all-gather(bf16[1024,128]{1,0:T(8,128)(2,1)S(1)} %collective-permute-done.5.g1), channel_id=3, replica_groups=mesh['chan'=32,'row'=2,'col'=8] {'row'}, dimensions={0}, use_global_device_ids=true | all-gather | bytes 786432 | tf_op jit(solution)/shard_map/all_gather | solution.py:336
  56.5 1.9 %collective-permute-start.3 = (bf16[1024,128]{1,0:T(8,128)(2,1)S(1)}, bf16[1024,128]{1,0:T(8,128)(2,1)S(1)}, u32[]{:S(2)}, u32[]{:S(2)}) collective-permute-start(bf16[1024,128]{1,0:T(8,128)(2,1)S(1)} %collective-permute-done.2.k2), channel_id=1, source_target_pairs={{2,3},{3,4},{4,5},{5,6},{6,7},{7,0},{0,1},{1,2},{14,13},{15,14},{8... | collective-permute-start | bytes 786440 | tf_op jit(solution)/shard_map/ppermute | solution.py:330
  58.4 0.7 collective-permute-start.7
  59.1 5.7 %all-gather.2 = bf16[2048,128]{1,0:T(8,128)(2,1)S(1)} all-gather(bf16[1024,128]{1,0:T(8,128)(2,1)S(1)} %collective-permute-done.6.g2), channel_id=4, replica_groups=mesh['chan'=32,'row'=2,'col'=8] {'row'}, dimensions={0}, use_global_device_ids=true | all-gather | bytes 786432 | tf_op jit(solution)/shard_map/all_gather | solution.py:336
  64.8 1.2 %collective-permute-done.3.k3 = bf16[1024,128]{1,0:T(8,128)(2,1)S(1)} collective-permute-done((bf16[1024,128]{1,0:T(8,128)(2,1)S(1)}, bf16[1024,128]{1,0:T(8,128)(2,1)S(1)}, u32[]{:S(2)}, u32[]{:S(2)}) %collective-permute-start.3) | collective-permute-done | bytes 262176 | tf_op jit(solution)/shard_map/ppermute | solution.py:330
  66.0 0.7 collective-permute-start.8
  66.6 1.9 %collective-permute-start.4 = (bf16[1024,128]{1,0:T(8,128)(2,1)S(1)}, bf16[1024,128]{1,0:T(8,128)(2,1)S(1)}, u32[]{:S(2)}, u32[]{:S(2)}) collective-permute-start(bf16[1024,128]{1,0:T(8,128)(2,1)S(1)} %collective-permute-done.3.k3), channel_id=1, source_target_pairs={{3,4},{4,5},{5,6},{6,7},{7,0},{0,1},{1,2},{2,3},{13,12},{14,13},{1... | collective-permute-start | bytes 786440 | tf_op jit(solution)/shard_map/ppermute | solution.py:330
  68.6 4.8 %all-gather.3 = bf16[2048,128]{1,0:T(8,128)(2,1)S(1)} all-gather(bf16[1024,128]{1,0:T(8,128)(2,1)S(1)} %collective-permute-done.7.g3), channel_id=5, replica_groups=mesh['chan'=32,'row'=2,'col'=8] {'row'}, dimensions={0}, use_global_device_ids=true | all-gather | bytes 786432 | tf_op jit(solution)/shard_map/all_gather | solution.py:336
  74.0 2.1 %collective-permute-done.4.k4 = bf16[1024,128]{1,0:T(8,128)(2,1)S(1)} collective-permute-done((bf16[1024,128]{1,0:T(8,128)(2,1)S(1)}, bf16[1024,128]{1,0:T(8,128)(2,1)S(1)}, u32[]{:S(2)}, u32[]{:S(2)}) %collective-permute-start.4) | collective-permute-done | bytes 262176 | tf_op jit(solution)/shard_map/ppermute | solution.py:330
  76.1 1.5 %correlate.1 = bf16[2,2,1024,256]{3,2,1,0:T(8,128)(2,1)} custom-call(bf16[1024,128]{1,0:T(8,128)(2,1)S(1)} %collective-permute-done.4.k4, bf16[2,1024,128]{2,1,0:T(8,128)(2,1)S(1)} %bitcast.5, bf16[2,1024,128]{2,1,0:T(8,128)(2,1)S(1)} %bitcast.6, bf16[2,1024,128]{2,1,0:T(8,128)(2,1)S(1)} %bitcast.7, ...), custom_call_target="tpu_custom_call", output_to_operand_aliasing={{}: (6, {})} | custom-call | tf_op jit(solution)/shard_map/correlate/pallas_call | solution.py:361
  (16 shorter events, 1.3 us)
Async XLA Ops:
  0.8 8.5 %collective-permute-start = (bf16[2,64,256]{2,1,0:T(8,128)(2,1)S(1)}, bf16[2,64,256]{2,1,0:T(8,128)(2,1)S(1)}, u32[]{:S(2)}, u32[]{:S(2)}) collective-permute-start(bf16[2,64,256]{2,1,0:T(8,128)(2,1)S(1)} %slice.3), channel_id=1, source_target_pairs={{0,1},{1,2},{2,3},{3,4},{4,5},{5,6},{6,7},{7,8},{8,9},{9,10},{10,1... | collective-permute-start | bytes 196616 | tf_op jit(solution)/shard_map/ppermute | solution.py:261
  5.1 1.0 %copy-start = (bf16[2,64,1024]{2,1,0:T(8,128)(2,1)S(1)}, bf16[2,64,1024]{2,1,0:T(8,128)(2,1)}, u32[]{:S(2)}) copy-start(bf16[2,64,1024]{2,1,0:T(8,128)(2,1)} %volt_hbm.1) | copy-start | bytes 786436
  6.1 0.7 copy-start.1
  6.8 1.2 %copy-start.2 = (bf16[2,512,512]{2,1,0:T(8,128)(2,1)S(1)}, bf16[2,512,512]{2,1,0:T(8,128)(2,1)}, u32[]{:S(2)}) copy-start(bf16[2,512,512]{2,1,0:T(8,128)(2,1)} %constant.21.clone.table_hbm) | copy-start | bytes 3145732
  36.2 10.6 %collective-permute-start.1 = (bf16[1024,128]{1,0:T(8,128)(2,1)S(1)}, bf16[1024,128]{1,0:T(8,128)(2,1)S(1)}, u32[]{:S(2)}, u32[]{:S(2)}) collective-permute-start(bf16[1024,128]{1,0:T(8,128)(2,1)S(1)} %get-tuple-element.16.k0), channel_id=1, source_target_pairs={{0,1},{1,2},{2,3},{3,4},{4,5},{5,6},{6,7},{7,0},{8,15},{9,8},{10,9... | collective-permute-start | bytes 786440 | tf_op jit(solution)/shard_map/ppermute | solution.py:330
  39.0 9.8 %collective-permute-start.5 = (bf16[1024,128]{1,0:T(8,128)(2,1)S(1)}, bf16[1024,128]{1,0:T(8,128)(2,1)S(1)}, u32[]{:S(2)}, u32[]{:S(2)}) collective-permute-start(bf16[1024,128]{1,0:T(8,128)(2,1)S(1)} %get-tuple-element.17.g0), channel_id=1, source_target_pairs={{1,2},{2,3},{3,4},{4,5},{5,6},{6,7},{8,15},{9,8},{10,9},{11,10},{1... | collective-permute-start | bytes 786440 | tf_op jit(solution)/shard_map/ppermute | solution.py:334
  46.8 9.7 %collective-permute-start.2 = (bf16[1024,128]{1,0:T(8,128)(2,1)S(1)}, bf16[1024,128]{1,0:T(8,128)(2,1)S(1)}, u32[]{:S(2)}, u32[]{:S(2)}) collective-permute-start(bf16[1024,128]{1,0:T(8,128)(2,1)S(1)} %collective-permute-done.1.k1), channel_id=1, source_target_pairs={{1,2},{2,3},{3,4},{4,5},{5,6},{6,7},{7,0},{0,1},{15,14},{8,15},{9,... | collective-permute-start | bytes 786440 | tf_op jit(solution)/shard_map/ppermute | solution.py:330
  48.9 9.5 %collective-permute-start.6 = (bf16[1024,128]{1,0:T(8,128)(2,1)S(1)}, bf16[1024,128]{1,0:T(8,128)(2,1)S(1)}, u32[]{:S(2)}, u32[]{:S(2)}) collective-permute-start(bf16[1024,128]{1,0:T(8,128)(2,1)S(1)} %collective-permute-done.5.g1), channel_id=1, source_target_pairs={{2,3},{3,4},{4,5},{5,6},{6,7},{15,14},{8,15},{9,8},{10,9},{11,10},... | collective-permute-start | bytes 786440 | tf_op jit(solution)/shard_map/ppermute | solution.py:334
  56.5 9.5 %collective-permute-start.3 = (bf16[1024,128]{1,0:T(8,128)(2,1)S(1)}, bf16[1024,128]{1,0:T(8,128)(2,1)S(1)}, u32[]{:S(2)}, u32[]{:S(2)}) collective-permute-start(bf16[1024,128]{1,0:T(8,128)(2,1)S(1)} %collective-permute-done.2.k2), channel_id=1, source_target_pairs={{2,3},{3,4},{4,5},{5,6},{6,7},{7,0},{0,1},{1,2},{14,13},{15,14},{8... | collective-permute-start | bytes 786440 | tf_op jit(solution)/shard_map/ppermute | solution.py:330
  58.4 10.2 %collective-permute-start.7 = (bf16[1024,128]{1,0:T(8,128)(2,1)S(1)}, bf16[1024,128]{1,0:T(8,128)(2,1)S(1)}, u32[]{:S(2)}, u32[]{:S(2)}) collective-permute-start(bf16[1024,128]{1,0:T(8,128)(2,1)S(1)} %collective-permute-done.6.g2), channel_id=1, source_target_pairs={{3,4},{4,5},{5,6},{6,7},{14,13},{15,14},{8,15},{9,8},{10,9},{11,10... | collective-permute-start | bytes 786440 | tf_op jit(solution)/shard_map/ppermute | solution.py:334
  66.0 8.0 %collective-permute-start.8 = (bf16[1024,128]{1,0:T(8,128)(2,1)S(1)}, bf16[1024,128]{1,0:T(8,128)(2,1)S(1)}, u32[]{:S(2)}, u32[]{:S(2)}) collective-permute-start(bf16[1024,128]{1,0:T(8,128)(2,1)S(1)} %pad_maximum_fusion), channel_id=1, source_target_pairs={{13,4},{14,5},{15,6},{8,7},{29,20},{30,21},{31,22},{24,23},{45,36}... | collective-permute-start | bytes 786440 | tf_op jit(solution)/shard_map/ppermute | solution.py:343
  66.6 9.5 %collective-permute-start.4 = (bf16[1024,128]{1,0:T(8,128)(2,1)S(1)}, bf16[1024,128]{1,0:T(8,128)(2,1)S(1)}, u32[]{:S(2)}, u32[]{:S(2)}) collective-permute-start(bf16[1024,128]{1,0:T(8,128)(2,1)S(1)} %collective-permute-done.3.k3), channel_id=1, source_target_pairs={{3,4},{4,5},{5,6},{6,7},{7,0},{0,1},{1,2},{2,3},{13,12},{14,13},{1... | collective-permute-start | bytes 786440 | tf_op jit(solution)/shard_map/ppermute | solution.py:330

commit v8 on v7

--- a/solution.py
+++ b/solution.py
@@ -223,11 +223,16 @@
         one = jnp.where(elsewhere, far[0:cols, :], s1[away, at, :])
         put_columns(two, one, right_ref, LANES)
 
-    def copy_of(start):
+    def copy_of(start, ch):
         here = slice(start, start + tile_rows)
+        goes_to = jnp.where(odd, 1 - ch, ch)
         return pltpu.make_async_copy(
-            out_ref.at[:, :, here, :], out_hbm.at[:, :, here, :], sems.at[start // tile_rows]
+            out_ref.at[:, goes_to, here, :], out_hbm.at[:, goes_to, here, :], sems.at[start // tile_rows, ch]
         )
+
+    def finish(start):
+        for ch in range(2):
+            copy_of(start, ch).wait()
 
     def products(start):
         here = slice(start, start + tile_rows)
@@ -243,9 +248,9 @@
             goes_to = jnp.where(odd, 1 - ch, ch)
             out_ref[0, goes_to, here, :] = jnp.where(upper, total[:, :cols], 0.0).astype(jnp.bfloat16)
             out_ref[1, goes_to, here, :] = jnp.where(upper, total[:, cols:], 0.0).astype(jnp.bfloat16)
-        copy_of(start).start()
-
-    for_tiles(half_rows, tile_rows, cols, prepare, products, lambda start: copy_of(start).wait())
+            copy_of(start, ch).start()
+
+    for_tiles(half_rows, tile_rows, cols, prepare, products, finish)
 
 
 def shards(voltages, fir_taps):
@@ -367,7 +372,7 @@
         scratch_shapes=[
             pltpu.VMEM(vis_shape.shape, jnp.bfloat16),
             pltpu.VMEM((2, 2 * LANES, 2 * cols), jnp.bfloat16),
-            pltpu.SemaphoreType.DMA((half // tile,)),
+            pltpu.SemaphoreType.DMA((half // tile, 2)),
         ],
         compiler_params=params,
         name="correlate",

time: 78.1 us -> 78.1 us (level)
  the two profiles are of different devices: /device:TPU:8 before, /device:TPU:1 now
where the time goes in v8:
time: 78.1 us; the launch traced here: 76.5 us
  starting transfers between devices  35.2 us (45%)
  blocking collectives  28.7 us (37%)
  waiting for transfers between devices  5.9 us (8%)
  local copies, waits for them, and re-layouts  3.74 us (5%)
  Pallas kernels  2.79 us (4%)
    all_to_all x1, blocking collectives, shards(): lax.all_to_all(spectra, 'chan', split_axis=0, concat_axis=0, tiled=True)  20 us
    ppermute x4, starting transfers between devices, keep_on(): return lax.ppermute(array, ('row', 'col'), hops)  17.3 us
    ppermute x3, starting transfers between devices, give_on(): return lax.ppermute(array, ('row', 'col'), hops)  10.4 us
    all_gather x3, blocking collectives, shards(): on_chip = lambda array: lax.all_gather(array, 'row', axis=0)  6.54 us
    ppermute x1, starting transfers between devices, shards(): lax.ppermute(voltages[:, :, samples - group * channels:], ('row', 'col'),...  4.82 us
    ppermute x1, waiting for transfers between devices, shards(): lax.ppermute(voltages[:, :, samples - group * channels:], ('row', 'col'),...  4.79 us
    unnamed x6, local copies, waits for them, and re-layouts  2.85 us
    ppermute x1, starting transfers between devices, shards(): lax.ppermute(jnp.concatenate([col_slice(k, col + col_size - 1) for k in k...  2.68 us
  transfers between devices with their start and end apart: 9, of which 2 were waited for; matrix products, arithmetic and copies ran while one was open for 0% of the time, Pallas kernels for 2%

profile of v8, /device:TPU:1, one launch (start us, length us, event | category | flops | bytes accessed | tf_op | source)
XLA Modules:
  0.0 76.5 jit_solution(6174200579904249593)
XLA Ops:
  0.0 0.8 %slice.3 = bf16[2,64,256]{2,1,0:T(8,128)(2,1)S(1)} slice(bf16[2,64,1024]{2,1,0:T(8,128)(2,1)} %volt_hbm.1), slice={[0:2], [0:64], [768:1024]} | slice | bytes 131072 | tf_op jit(solution)/shard_map/slice | solution.py:267
  0.8 4.8 %collective-permute-start = (bf16[2,64,256]{2,1,0:T(8,128)(2,1)S(1)}, bf16[2,64,256]{2,1,0:T(8,128)(2,1)S(1)}, u32[]{:S(2)}, u32[]{:S(2)}) collective-permute-start(bf16[2,64,256]{2,1,0:T(8,128)(2,1)S(1)} %slice.3), channel_id=1, source_target_pairs={{0,1},{1,2},{2,3},{3,4},{4,5},{5,6},{6,7},{7,8},{8,9},{9,10},{10,1... | collective-permute-start | bytes 196616 | tf_op jit(solution)/shard_map/ppermute | solution.py:266
  5.7 0.9 %copy-done = bf16[2,64,1024]{2,1,0:T(8,128)(2,1)S(1)} copy-done((bf16[2,64,1024]{2,1,0:T(8,128)(2,1)S(1)}, bf16[2,64,1024]{2,1,0:T(8,128)(2,1)}, u32[]{:S(2)}) %copy-start) | copy-done | bytes 262168
  6.6 0.7 copy-done.1
  7.3 1.2 %copy-done.2 = bf16[2,512,512]{2,1,0:T(8,128)(2,1)S(1)} copy-done((bf16[2,512,512]{2,1,0:T(8,128)(2,1)S(1)}, bf16[2,512,512]{2,1,0:T(8,128)(2,1)}, u32[]{:S(2)}) %copy-start.2) | copy-done | bytes 1048600
  8.5 1.5 %later_frames.1 = (bf16[2,64,256]{2,1,0:T(8,128)(2,1)S(1)}, f32[4,256]{1,0:T(4,128)S(1)}, bf16[2,512,512]{2,1,0:T(8,128)(2,1)S(1)}, bf16[512,256]{1,0:T(8,128)(2,1)S(1)}, bf16[2,2,1024,256]{3,2,1,0:T(8,128)(2,1)}) custom-call(bf16[2,64,1024]{2,1,0:T(8,128)(2,1)S(1)} %copy-done, f32[4,64]{1,0:T(4,128)S(1)} %copy-done.1, bf16[2,512,512]{2,1,0:T(8,128)(2,1)S(1)} %copy-done.2), custom_call_target="tpu_custom_call" | custom-call | flops 500000000 | bytes 3000000 | tf_op jit(solution)/shard_map/later_frames/pallas_call | solution.py:279
  10.0 4.8 %collective-permute-done.halo_ref = bf16[2,64,256]{2,1,0:T(8,128)(2,1)S(1)} collective-permute-done((bf16[2,64,256]{2,1,0:T(8,128)(2,1)S(1)}, bf16[2,64,256]{2,1,0:T(8,128)(2,1)S(1)}, u32[]{:S(2)}, u32[]{:S(2)}) %collective-permute-start) | collective-permute-done | bytes 65568 | tf_op jit(solution)/shard_map/ppermute | solution.py:266
  14.8 0.7 first_frames.1
  15.5 20.0 %all_to_all.5 = bf16[32,16,256]{2,1,0:T(8,128)(2,1)S(1)} all-to-all(bf16[32,16,256]{2,1,0:T(8,128)(2,1)S(1)} %bitcast.9), channel_id=1, replica_groups=mesh['chan'=32,'row'=2,'col'=8] {'chan'}, dimensions={0} | all-to-all | bytes 524288 | tf_op jit(solution)/shard_map/all_to_all | solution.py:309
  35.5 2.2 %all-gather = bf16[64,16,256]{2,1,0:T(8,128)(2,1)S(1)} all-gather(bf16[32,16,256]{2,1,0:T(8,128)(2,1)S(1)} %all_to_all.5), channel_id=2, replica_groups=mesh['chan'=32,'row'=2,'col'=8] {'row'}, dimensions={0}, use_global_device_ids=true | all-gather | bytes 786432 | tf_op jit(solution)/shard_map/all_gather | solution.py:310
  37.6 0.6 turn.1
  38.2 6.0 %collective-permute-start.1 = (bf16[1024,128]{1,0:T(8,128)(2,1)S(1)}, bf16[1024,128]{1,0:T(8,128)(2,1)S(1)}, u32[]{:S(2)}, u32[]{:S(2)}) collective-permute-start(bf16[1024,128]{1,0:T(8,128)(2,1)S(1)} %get-tuple-element.16.k0), channel_id=1, source_target_pairs={{0,1},{1,2},{2,3},{3,4},{4,5},{5,6},{6,7},{7,0},{8,15},{9,8},{10,9... | collective-permute-start | bytes 786440 | tf_op jit(solution)/shard_map/ppermute | solution.py:335
  44.2 3.5 %collective-permute-start.5 = (bf16[1024,128]{1,0:T(8,128)(2,1)S(1)}, bf16[1024,128]{1,0:T(8,128)(2,1)S(1)}, u32[]{:S(2)}, u32[]{:S(2)}) collective-permute-start(bf16[1024,128]{1,0:T(8,128)(2,1)S(1)} %get-tuple-element.17.g0), channel_id=1, source_target_pairs={{1,2},{2,3},{3,4},{4,5},{5,6},{6,7},{8,15},{9,8},{10,9},{11,10},{1... | collective-permute-start | bytes 786440 | tf_op jit(solution)/shard_map/ppermute | solution.py:339
  47.7 4.8 %collective-permute-start.2 = (bf16[1024,128]{1,0:T(8,128)(2,1)S(1)}, bf16[1024,128]{1,0:T(8,128)(2,1)S(1)}, u32[]{:S(2)}, u32[]{:S(2)}) collective-permute-start(bf16[1024,128]{1,0:T(8,128)(2,1)S(1)} %collective-permute-done.1.k1), channel_id=1, source_target_pairs={{1,2},{2,3},{3,4},{4,5},{5,6},{6,7},{7,0},{0,1},{15,14},{8,15},{9,... | collective-permute-start | bytes 786440 | tf_op jit(solution)/shard_map/ppermute | solution.py:335
  52.5 3.5 %collective-permute-start.6 = (bf16[1024,128]{1,0:T(8,128)(2,1)S(1)}, bf16[1024,128]{1,0:T(8,128)(2,1)S(1)}, u32[]{:S(2)}, u32[]{:S(2)}) collective-permute-start(bf16[1024,128]{1,0:T(8,128)(2,1)S(1)} %collective-permute-done.5.g1), channel_id=1, source_target_pairs={{2,3},{3,4},{4,5},{5,6},{6,7},{15,14},{8,15},{9,8},{10,9},{11,10},... | collective-permute-start | bytes 786440 | tf_op jit(solution)/shard_map/ppermute | solution.py:339
  56.0 2.2 %all-gather.1 = bf16[2048,128]{1,0:T(8,128)(2,1)S(1)} all-gather(bf16[1024,128]{1,0:T(8,128)(2,1)S(1)} %collective-permute-done.5.g1), channel_id=3, replica_groups=mesh['chan'=32,'row'=2,'col'=8] {'row'}, dimensions={0}, use_global_device_ids=true | all-gather | bytes 786432 | tf_op jit(solution)/shard_map/all_gather | solution.py:341
  58.2 2.6 %collective-permute-start.3 = (bf16[1024,128]{1,0:T(8,128)(2,1)S(1)}, bf16[1024,128]{1,0:T(8,128)(2,1)S(1)}, u32[]{:S(2)}, u32[]{:S(2)}) collective-permute-start(bf16[1024,128]{1,0:T(8,128)(2,1)S(1)} %collective-permute-done.2.k2), channel_id=1, source_target_pairs={{2,3},{3,4},{4,5},{5,6},{6,7},{7,0},{0,1},{1,2},{14,13},{15,14},{8... | collective-permute-start | bytes 786440 | tf_op jit(solution)/shard_map/ppermute | solution.py:335
  60.8 3.5 %collective-permute-start.7 = (bf16[1024,128]{1,0:T(8,128)(2,1)S(1)}, bf16[1024,128]{1,0:T(8,128)(2,1)S(1)}, u32[]{:S(2)}, u32[]{:S(2)}) collective-permute-start(bf16[1024,128]{1,0:T(8,128)(2,1)S(1)} %collective-permute-done.6.g2), channel_id=1, source_target_pairs={{3,4},{4,5},{5,6},{6,7},{14,13},{15,14},{8,15},{9,8},{10,9},{11,10... | collective-permute-start | bytes 786440 | tf_op jit(solution)/shard_map/ppermute | solution.py:339
  64.3 2.2 %all-gather.2 = bf16[2048,128]{1,0:T(8,128)(2,1)S(1)} all-gather(bf16[1024,128]{1,0:T(8,128)(2,1)S(1)} %collective-permute-done.6.g2), channel_id=4, replica_groups=mesh['chan'=32,'row'=2,'col'=8] {'row'}, dimensions={0}, use_global_device_ids=true | all-gather | bytes 786432 | tf_op jit(solution)/shard_map/all_gather | solution.py:341
  66.6 2.7 %collective-permute-start.8 = (bf16[1024,128]{1,0:T(8,128)(2,1)S(1)}, bf16[1024,128]{1,0:T(8,128)(2,1)S(1)}, u32[]{:S(2)}, u32[]{:S(2)}) collective-permute-start(bf16[1024,128]{1,0:T(8,128)(2,1)S(1)} %pad_maximum_fusion), channel_id=1, source_target_pairs={{13,4},{14,5},{15,6},{8,7},{29,20},{30,21},{31,22},{24,23},{45,36}... | collective-permute-start | bytes 786440 | tf_op jit(solution)/shard_map/ppermute | solution.py:348
  69.2 3.9 %collective-permute-start.4 = (bf16[1024,128]{1,0:T(8,128)(2,1)S(1)}, bf16[1024,128]{1,0:T(8,128)(2,1)S(1)}, u32[]{:S(2)}, u32[]{:S(2)}) collective-permute-start(bf16[1024,128]{1,0:T(8,128)(2,1)S(1)} %collective-permute-done.3.k3), channel_id=1, source_target_pairs={{3,4},{4,5},{5,6},{6,7},{7,0},{0,1},{1,2},{2,3},{13,12},{14,13},{1... | collective-permute-start | bytes 786440 | tf_op jit(solution)/shard_map/ppermute | solution.py:335
  73.2 2.2 %all-gather.3 = bf16[2048,128]{1,0:T(8,128)(2,1)S(1)} all-gather(bf16[1024,128]{1,0:T(8,128)(2,1)S(1)} %collective-permute-done.7.g3), channel_id=5, replica_groups=mesh['chan'=32,'row'=2,'col'=8] {'row'}, dimensions={0}, use_global_device_ids=true | all-gather | bytes 786432 | tf_op jit(solution)/shard_map/all_gather | solution.py:341
  75.4 1.1 %collective-permute-done.4.k4 = bf16[1024,128]{1,0:T(8,128)(2,1)S(1)} collective-permute-done((bf16[1024,128]{1,0:T(8,128)(2,1)S(1)}, bf16[1024,128]{1,0:T(8,128)(2,1)S(1)}, u32[]{:S(2)}, u32[]{:S(2)}) %collective-permute-start.4) | collective-permute-done | bytes 262176 | tf_op jit(solution)/shard_map/ppermute | solution.py:335
  76.4 0.1 correlate.1
  (16 shorter events, 0.1 us)
Async XLA Ops:
  0.8 14.0 %collective-permute-start = (bf16[2,64,256]{2,1,0:T(8,128)(2,1)S(1)}, bf16[2,64,256]{2,1,0:T(8,128)(2,1)S(1)}, u32[]{:S(2)}, u32[]{:S(2)}) collective-permute-start(bf16[2,64,256]{2,1,0:T(8,128)(2,1)S(1)} %slice.3), channel_id=1, source_target_pairs={{0,1},{1,2},{2,3},{3,4},{4,5},{5,6},{6,7},{7,8},{8,9},{9,10},{10,1... | collective-permute-start | bytes 196616 | tf_op jit(solution)/shard_map/ppermute | solution.py:266
  5.7 1.0 %copy-start = (bf16[2,64,1024]{2,1,0:T(8,128)(2,1)S(1)}, bf16[2,64,1024]{2,1,0:T(8,128)(2,1)}, u32[]{:S(2)}) copy-start(bf16[2,64,1024]{2,1,0:T(8,128)(2,1)} %volt_hbm.1) | copy-start | bytes 786436
  6.6 0.7 copy-start.1
  7.3 1.2 %copy-start.2 = (bf16[2,512,512]{2,1,0:T(8,128)(2,1)S(1)}, bf16[2,512,512]{2,1,0:T(8,128)(2,1)}, u32[]{:S(2)}) copy-start(bf16[2,512,512]{2,1,0:T(8,128)(2,1)} %constant.21.clone.table_hbm) | copy-start | bytes 3145732
  38.2 9.5 %collective-permute-start.1 = (bf16[1024,128]{1,0:T(8,128)(2,1)S(1)}, bf16[1024,128]{1,0:T(8,128)(2,1)S(1)}, u32[]{:S(2)}, u32[]{:S(2)}) collective-permute-start(bf16[1024,128]{1,0:T(8,128)(2,1)S(1)} %get-tuple-element.16.k0), channel_id=1, source_target_pairs={{0,1},{1,2},{2,3},{3,4},{4,5},{5,6},{6,7},{7,0},{8,15},{9,8},{10,9... | collective-permute-start | bytes 786440 | tf_op jit(solution)/shard_map/ppermute | solution.py:335
  44.2 8.3 %collective-permute-start.5 = (bf16[1024,128]{1,0:T(8,128)(2,1)S(1)}, bf16[1024,128]{1,0:T(8,128)(2,1)S(1)}, u32[]{:S(2)}, u32[]{:S(2)}) collective-permute-start(bf16[1024,128]{1,0:T(8,128)(2,1)S(1)} %get-tuple-element.17.g0), channel_id=1, source_target_pairs={{1,2},{2,3},{3,4},{4,5},{5,6},{6,7},{8,15},{9,8},{10,9},{11,10},{1... | collective-permute-start | bytes 786440 | tf_op jit(solution)/shard_map/ppermute | solution.py:339
  47.7 10.5 %collective-permute-start.2 = (bf16[1024,128]{1,0:T(8,128)(2,1)S(1)}, bf16[1024,128]{1,0:T(8,128)(2,1)S(1)}, u32[]{:S(2)}, u32[]{:S(2)}) collective-permute-start(bf16[1024,128]{1,0:T(8,128)(2,1)S(1)} %collective-permute-done.1.k1), channel_id=1, source_target_pairs={{1,2},{2,3},{3,4},{4,5},{5,6},{6,7},{7,0},{0,1},{15,14},{8,15},{9,... | collective-permute-start | bytes 786440 | tf_op jit(solution)/shard_map/ppermute | solution.py:335
  52.5 8.3 %collective-permute-start.6 = (bf16[1024,128]{1,0:T(8,128)(2,1)S(1)}, bf16[1024,128]{1,0:T(8,128)(2,1)S(1)}, u32[]{:S(2)}, u32[]{:S(2)}) collective-permute-start(bf16[1024,128]{1,0:T(8,128)(2,1)S(1)} %collective-permute-done.5.g1), channel_id=1, source_target_pairs={{2,3},{3,4},{4,5},{5,6},{6,7},{15,14},{8,15},{9,8},{10,9},{11,10},... | collective-permute-start | bytes 786440 | tf_op jit(solution)/shard_map/ppermute | solution.py:339
  58.2 8.3 %collective-permute-start.3 = (bf16[1024,128]{1,0:T(8,128)(2,1)S(1)}, bf16[1024,128]{1,0:T(8,128)(2,1)S(1)}, u32[]{:S(2)}, u32[]{:S(2)}) collective-permute-start(bf16[1024,128]{1,0:T(8,128)(2,1)S(1)} %collective-permute-done.2.k2), channel_id=1, source_target_pairs={{2,3},{3,4},{4,5},{5,6},{6,7},{7,0},{0,1},{1,2},{14,13},{15,14},{8... | collective-permute-start | bytes 786440 | tf_op jit(solution)/shard_map/ppermute | solution.py:335
  60.8 12.3 %collective-permute-start.7 = (bf16[1024,128]{1,0:T(8,128)(2,1)S(1)}, bf16[1024,128]{1,0:T(8,128)(2,1)S(1)}, u32[]{:S(2)}, u32[]{:S(2)}) collective-permute-start(bf16[1024,128]{1,0:T(8,128)(2,1)S(1)} %collective-permute-done.6.g2), channel_id=1, source_target_pairs={{3,4},{4,5},{5,6},{6,7},{14,13},{15,14},{8,15},{9,8},{10,9},{11,10... | collective-permute-start | bytes 786440 | tf_op jit(solution)/shard_map/ppermute | solution.py:339
  66.6 8.8 %collective-permute-start.8 = (bf16[1024,128]{1,0:T(8,128)(2,1)S(1)}, bf16[1024,128]{1,0:T(8,128)(2,1)S(1)}, u32[]{:S(2)}, u32[]{:S(2)}) collective-permute-start(bf16[1024,128]{1,0:T(8,128)(2,1)S(1)} %pad_maximum_fusion), channel_id=1, source_target_pairs={{13,4},{14,5},{15,6},{8,7},{29,20},{30,21},{31,22},{24,23},{45,36}... | collective-permute-start | bytes 786440 | tf_op jit(solution)/shard_map/ppermute | solution.py:348
  69.2 7.2 %collective-permute-start.4 = (bf16[1024,128]{1,0:T(8,128)(2,1)S(1)}, bf16[1024,128]{1,0:T(8,128)(2,1)S(1)}, u32[]{:S(2)}, u32[]{:S(2)}) collective-permute-start(bf16[1024,128]{1,0:T(8,128)(2,1)S(1)} %collective-permute-done.3.k3), channel_id=1, source_target_pairs={{3,4},{4,5},{5,6},{6,7},{7,0},{0,1},{1,2},{2,3},{13,12},{14,13},{1... | collective-permute-start | bytes 786440 | tf_op jit(solution)/shard_map/ppermute | solution.py:335
